TPU v7x, 128 devices: a whole 4x4x4 slice. The times are simulated.
128 devices in a mesh: enc: 32 (over y_lo, z, x), bb: 4 (over y_hi, core).
Axes of the slice: x: 4, y: 4 (y_hi: 2, y_lo: 2; y = y_hi * 2 + y_lo), z: 4, core: 2. Of those that a mesh axis runs over, the one named last changes fastest.
Arguments:
- image_tiles: bfloat16 [256, 16, 32, 384], P(('enc', 'bb')), may hold values from -6 to 6
- depth_kernel: float32 [7, 7, 384], replicated, may hold values from -0.875 to 0.875
- norm_gain: float32 [384], replicated, may hold values from 0.5 to 1.5
- weight_in: bfloat16 [384, 1536], replicated, may hold values from -0.3125 to 0.3125
- bias_in: float32 [1536], replicated, may hold values from -3 to 3
- weight_out: bfloat16 [1536, 384], replicated, may hold values from -0.15625 to 0.15625
- layer_scale: float32 [384], replicated, may hold values from 0.3 to 3
- weight_proj: bfloat16 [384, 4096], replicated, may hold values from -0.3125 to 0.3125
- image_counts: int32 [128], P(('enc', 'bb')), may hold values from 1 to 2, as said below
- destination: int32 [128, 32], P(('enc', 'bb')), may hold values from 0 to 31, as said below
- row_offset: int32 [128, 32], P(('enc', 'bb')), may hold values from 0 to 1, as said below
- connector: bfloat16 [4096, 3584], P(None, 'bb'), may hold values from -0.09375 to 0.09375
- cotangent: bfloat16 [16384, 3584], P('enc', 'bb'), may hold values from -6 to 6
Outputs:
- grad_kernel: float32 [7, 7, 384], replicated
- grad_gain: float32 [384], replicated
- grad_weight_in: bfloat16 [384, 1536], replicated
- grad_bias_in: float32 [1536], replicated
- grad_weight_out: bfloat16 [1536, 384], replicated
- grad_layer_scale: float32 [384], replicated
- grad_weight_proj: bfloat16 [384, 4096], replicated
- token_grads: bfloat16 [8192, 4096], P(('enc', 'bb'))
Inputs may be any that keep to these rules, and one draw needn't show every extreme that they name: `image_counts`: every source has at least one live image. `destination`: no group is named by more than 2 blocks of one source, and in every source some group is named by exactly 2 blocks of its first image. `row_offset`: the number of earlier blocks of the same source naming the same group, so a source's (destination, row_offset) pairs are distinct.
All inputs are finite; a program needn't handle non-finite values.
Results may differ from a plain program's by a relative error of at most 0.023.
Values may be sent and summed in bfloat16 or wider, within the bound.
No kernel may reach another device: no remote copies, remote signals or barrier semaphores. Data moves between devices by JAX's collectives and lax.ppermute only.
A program may use at most 128 MiB of HBM per device.

v0:
```python
import jax
import jax.numpy as jnp
from jax import lax
from jax.sharding import PartitionSpec as P

EPS = 1e-06


def contract_first(first_operand, second_operand):
    return lax.dot_general(
        first_operand, second_operand, (((0,), (0,)), ((), ())), preferred_element_type=jnp.float32
    )


def contract_last(first_operand, second_operand):
    return lax.dot_general(
        first_operand, second_operand, (((1,), (1,)), ((), ())), preferred_element_type=jnp.float32
    )


def front(image_tiles, depth_kernel, norm_gain):
    tile_height = image_tiles.shape[1]
    tile_width = image_tiles.shape[2]
    source = image_tiles.astype(jnp.float32)
    padded = jnp.pad(source, ((0, 0), (3, 3), (3, 3), (0, 0)))
    conv_sum = jnp.zeros_like(source)
    for row_shift in range(7):
        for col_shift in range(7):
            conv_sum = (
                conv_sum
                + padded[
                    :, row_shift : row_shift + tile_height, col_shift : col_shift + tile_width, :
                ]
                * depth_kernel[row_shift, col_shift]
            )
    centered = conv_sum - jnp.mean(conv_sum, axis=-1, keepdims=True)
    variance = jnp.mean(centered * centered, axis=-1, keepdims=True)
    return centered * lax.rsqrt(variance + EPS) * norm_gain


def encode(image_tiles, params):
    depth_kernel, norm_gain, weight_in, bias_in, weight_out, layer_scale, weight_proj = params
    tile_count, tile_height, tile_width, channels = image_tiles.shape
    normed = front(image_tiles, depth_kernel, norm_gain).astype(jnp.bfloat16).reshape(-1, channels)
    hidden_pre = jnp.dot(normed, weight_in, preferred_element_type=jnp.float32) + bias_in
    hidden = jax.nn.gelu(hidden_pre).astype(jnp.bfloat16)
    branch = jnp.dot(hidden, weight_out, preferred_element_type=jnp.float32)
    block_out = image_tiles.astype(jnp.float32).reshape(-1, channels) + layer_scale * branch
    pooled = block_out.reshape(tile_count, tile_height // 4, 4, tile_width // 4, 4, channels).mean(
        axis=(2, 4)
    )
    pooled = pooled.reshape(-1, channels).astype(jnp.bfloat16)
    visual = jnp.dot(pooled, weight_proj, preferred_element_type=jnp.float32).astype(jnp.bfloat16)
    return (visual, (normed, hidden_pre, hidden, branch, pooled))


def encode_grads(
    image_tiles, params, residuals, token_grads, settle_proj, settle_mlp, settle_front
):
    depth_kernel, norm_gain, weight_in, bias_in, weight_out, layer_scale, weight_proj = params
    normed, hidden_pre, hidden, branch, pooled = residuals
    tile_count, tile_height, tile_width, channels = image_tiles.shape
    grad_proj = settle_proj(contract_first(pooled, token_grads))
    grad_pooled = contract_last(token_grads, weight_proj) / 16.0
    spread_cells = jnp.broadcast_to(
        grad_pooled.reshape(tile_count, tile_height // 4, 1, tile_width // 4, 1, channels),
        (tile_count, tile_height // 4, 4, tile_width // 4, 4, channels),
    ).reshape(-1, channels)
    grad_scale = jnp.sum(spread_cells * branch, axis=0)
    grad_branch = (spread_cells * layer_scale).astype(jnp.bfloat16)
    grad_out = contract_first(hidden, grad_branch)
    grad_hidden = contract_last(grad_branch, weight_out)
    gelu_back = jax.vjp(jax.nn.gelu, hidden_pre)[1]
    grad_pre = gelu_back(grad_hidden)[0].astype(jnp.bfloat16)
    grad_in = contract_first(normed, grad_pre)
    grad_bias = jnp.sum(grad_pre.astype(jnp.float32), axis=0)
    grad_scale, grad_out, grad_in, grad_bias = settle_mlp(
        (grad_scale, grad_out, grad_in, grad_bias)
    )
    grad_normed = contract_last(grad_pre, weight_in).reshape(image_tiles.shape)

    def front_of(kernel_value, gain_value):
        return front(image_tiles, kernel_value, gain_value)

    front_back = jax.vjp(front_of, depth_kernel, norm_gain)[1]
    grad_kernel, grad_gain = settle_front(front_back(grad_normed))
    return (grad_kernel, grad_gain, grad_in, grad_bias, grad_out, grad_scale, grad_proj)


def unchanged(value_in):
    return value_in


def on_device(
    image_tiles,
    depth_kernel,
    norm_gain,
    weight_in,
    bias_in,
    weight_out,
    layer_scale,
    weight_proj,
    image_counts,
    destination,
    row_offset,
    connector,
    cotangent,
):
    params = (depth_kernel, norm_gain, weight_in, bias_in, weight_out, layer_scale, weight_proj)
    enc_size = lax.axis_size("enc")
    group_size = lax.axis_size("bb")
    tile_count = image_tiles.shape[0]
    visual, residuals = encode(image_tiles, params)
    feature = visual.shape[1]
    block_count = destination.shape[1]
    block_length = visual.shape[0] // block_count
    capacity = 2 * block_count // enc_size
    in_use = (
        jnp.arange(block_count, dtype=jnp.int32) // (block_count // tile_count) < image_counts[0]
    )
    blocks = jnp.where(
        in_use[:, None, None],
        visual.reshape(block_count, block_length, feature),
        jnp.zeros((), jnp.bfloat16),
    )
    outgoing = jnp.zeros((enc_size, capacity, block_length, feature), jnp.bfloat16)
    outgoing = (
        outgoing.at[destination[0], row_offset[0]]
        .set(blocks)
        .reshape(enc_size, capacity * block_length, feature)
    )
    arrived = lax.all_to_all(outgoing, "enc", split_axis=0, concat_axis=0, tiled=True).reshape(
        -1, feature
    )
    pre_act = jnp.dot(
        lax.all_gather(arrived, "bb", axis=0, tiled=True),
        connector,
        preferred_element_type=jnp.float32,
    )
    gelu_back = jax.vjp(jax.nn.gelu, pre_act)[1]
    grad_pre = gelu_back(cotangent.astype(jnp.float32))[0].astype(jnp.bfloat16)
    own_rows = lax.psum_scatter(
        contract_last(grad_pre, connector).astype(jnp.bfloat16),
        "bb",
        scatter_dimension=0,
        tiled=True,
    ).astype(jnp.float32)
    own_rows = own_rows.astype(jnp.bfloat16).reshape(enc_size, capacity * block_length, feature)
    returned = lax.all_to_all(own_rows, "enc", split_axis=0, concat_axis=0, tiled=True).reshape(
        enc_size, capacity, block_length, feature
    )
    picked = returned[destination[0], row_offset[0]]
    token_grads = jnp.where(in_use[:, None, None], picked, jnp.zeros((), jnp.bfloat16)).reshape(
        -1, feature
    )
    local_grads = encode_grads(
        image_tiles, params, residuals, token_grads, unchanged, unchanged, unchanged
    )
    summed = lax.psum(
        (
            local_grads[0],
            local_grads[1],
            local_grads[2],
            local_grads[3],
            local_grads[4],
            local_grads[5],
            local_grads[6],
        ),
        ("enc", "bb"),
    )
    factor = 1.0 / float(enc_size * group_size)
    return (
        summed[0] * factor,
        summed[1] * factor,
        (summed[2] * factor).astype(jnp.bfloat16),
        summed[3] * factor,
        (summed[4] * factor).astype(jnp.bfloat16),
        summed[5] * factor,
        (summed[6] * factor).astype(jnp.bfloat16),
        token_grads,
    )


def solution(mesh):
    in_specs = (
        P(("enc", "bb"), None, None, None),
        P(),
        P(),
        P(),
        P(),
        P(),
        P(),
        P(),
        P(("enc", "bb")),
        P(("enc", "bb"), None),
        P(("enc", "bb"), None),
        P(None, "bb"),
        P("enc", "bb"),
    )
    out_specs = (P(), P(), P(), P(), P(), P(), P(), P(("enc", "bb"), None))
    return jax.shard_map(
        on_device, mesh=mesh, in_specs=in_specs, out_specs=out_specs, check_vma=False
    )
```

profile of v0, /device:TPU:1, one launch (start us, length us, event | category | flops | bytes accessed | tf_op | source)
XLA Modules:
  0.0 487.9 jit_solution(14197670559163493092)
XLA Ops:
  11.4 2.5 convert_element_type.59
  13.9 43.3 %fusion.37 = (f32[2,16,32]{2,1,0:T(8,128)S(1)}, f32[2,16,32,384]{3,2,1,0:T(8,128)}) fusion(f32[384]{0:T(512)S(1)} %get-tuple-element.106, f32[384]{0:T(512)S(1)} %get-tuple-element.107, f32[384]{0:T(512)S(1)} %get-tuple-element.60, f32[384]{0:T(512)S(1)} %get-tuple-element.61, f32[384]{0:T(512)S(1)} %get-tuple-element.62, f32[384]{0:T(512)S(1)} %get-tuple-element.63, ...), kind=kLoop, calls=%fused_computation.229 | loop fusion | flops 38534144 | bytes 3225088 | tf_op jit(solution)/shard_map/reduce_sum | solution.py:36
  60.5 4.5 multiply_convert_fusion.1
  65.0 3.5 bitcast_add_fusion
  68.5 2.7 reshape.440
  74.6 2.2 reshape.441
  76.8 2.4 broadcast_select_fusion.1
  81.2 5.7 %scatter_fusion = bf16[32,2,2,4096]{3,2,1,0:T(2,128)(2,1)} fusion(bf16[32,2,2,4096]{3,2,1,0:T(2,128)(2,1)} %broadcast_in_dim.205, s32[32]{0:T(128)S(1)} %get-tuple-element.116, bf16[32,2,4096]{2,1,0:T(2,128)(2,1)} %broadcast_select_fusion.1), kind=kCustom, calls=%fused_computation.1 | custom fusion | bytes 1573120 | tf_op jit(solution)/shard_map/scatter | solution.py:129
  86.8 3.6 reshape.442
  90.4 25.5 %all_to_all.10 = bf16[32,4,4096]{2,1,0:T(4,128)(2,1)} all-to-all(bf16[32,4,4096]{2,1,0:T(4,128)(2,1)} %reshape.442), channel_id=1, replica_groups=mesh['enc'=32,'bb'=4] {'enc'}, dimensions={0} | all-to-all | bytes 2097152 | tf_op jit(solution)/shard_map/all_to_all | solution.py:132
  115.9 2.1 reshape.443
  118.1 38.9 %all-gather.2.cloned.1.call-done = bf16[512,4096]{1,0:T(8,128)(2,1)} async-done(((bf16[128,4096]{1,0:T(8,128)(2,1)}), bf16[512,4096]{1,0:T(8,128)(2,1)}) %all-gather.2.cloned.1.call-update) | async-done | bytes 4194320 | tf_op jit(solution)/shard_map/all_gather | solution.py:136
  157.0 17.8 %convolution_convert_fusion = bf16[512,4096]{1,0:T(8,128)(2,1)} fusion(bf16[4096,896]{1,0:T(8,128)(2,1)} %param.24, bf16[512,896]{1,0:T(8,128)(2,1)} %param.25, bf16[512,4096]{1,0:T(8,128)(2,1)} %all-gather.2.cloned.1.call-done), kind=kOutput, calls=%fused_computation.62 | convolution fusion | flops 7527923712 | bytes 16646144 | tf_op jit(solution)/shard_map/dot_general | solution.py:16
  174.8 50.6 %reduce-scatter.2.cloned.1.call-done = bf16[128,4096]{1,0:T(8,128)(2,1)} async-done(((bf16[512,4096]{1,0:T(8,128)(2,1)}), bf16[128,4096]{1,0:T(8,128)(2,1)}) %reduce-scatter.2.cloned.1.call-update) | async-done | bytes 1048592 | tf_op jit(solution)/shard_map/reduce_scatter | solution.py:142
  225.4 2.2 reshape.444
  227.6 7.1 %all-to-all-start.1 = ((bf16[32,4,4096]{2,1,0:T(4,128)(2,1)}), bf16[32,4,4096]{2,1,0:T(4,128)(2,1)}, u32[]{:S(2)}, u32[]{:S(2)}) async-start(bf16[32,4,4096]{2,1,0:T(4,128)(2,1)} %reshape.444), calls=%async_computation.2 | async-start | bytes 2097152 | tf_op jit(solution)/shard_map/all_to_all | solution.py:149
  235.0 15.4 %all-to-all-done.1 = bf16[32,4,4096]{2,1,0:T(4,128)(2,1)} async-done(((bf16[32,4,4096]{2,1,0:T(4,128)(2,1)}), bf16[32,4,4096]{2,1,0:T(4,128)(2,1)}, u32[]{:S(2)}, u32[]{:S(2)}) %all-to-all-start.1) | async-done | bytes 1048608 | tf_op jit(solution)/shard_map/all_to_all | solution.py:149
  250.3 3.5 reshape.445
  253.9 3.6 gather_fusion
  257.4 2.4 broadcast_select_fusion
  265.1 5.8 %fusion.24 = f32[1536,384]{1,0:T(8,128)} fusion(bf16[1024,1536]{1,0:T(8,128)(2,1)} %copy-done.24, f32[1024,384]{1,0:T(8,128)S(1)} %reshape.446, f32[384]{0:T(512)S(1)} %copy-done.23), kind=kOutput, calls=%fused_computation.149 | convolution fusion | flops 1208745984 | bytes 7079424 | tf_op jit(solution)/shard_map/dot_general | solution.py:10
  270.8 7.4 %convert_reduce_fusion = (f32[1536]{0:T(1024)S(1)}, bf16[1024,1536]{1,0:T(8,128)(2,1)S(1)}) fusion(f32[1024,1536]{1,0:T(8,128)} %get-tuple-element.121, f32[1536]{0:T(1024)S(1)} %copy-done.22, bf16[1536,384]{1,0:T(8,128)(2,1)S(1)} %copy-done.19, f32[1024,384]{1,0:T(8,128)S(1)} %reshape.446, f32[384]{0:T(512)S(1)} %copy-done.23), kind=kOutput, calls=%fused_computation.60 | convolution fusion | flops 1244920320 | bytes 12203520 | tf_op jit(solution)/shard_map/dot_general | solution.py:16
  280.1 2.8 fusion.41
  285.0 4.1 multiply_reduce_fusion.48
  289.1 5.0 %multiply_reduce_fusion.49 = (f32[384]{0:T(512)S(1)}, f32[384]{0:T(512)S(1)}, f32[384]{0:T(512)S(1)}, f32[384]{0:T(512)S(1)}, f32[384]{0:T(512)S(1)}, /*index=5*...) fusion(f32[2,16,32,384]{3,2,1,0:T(8,128)S(1)} %get-tuple-elemen, ...), kind=kLoop, calls=%fused_computation.131 | loop fusion | flops 14148864 | bytes 3173376 | tf_op jit(solution)/shard_map/transpose(jvp())/reduce_sum | solution.py:31
  294.1 5.2 %multiply_reduce_fusion.50 = (f32[384]{0:T(512)S(1)}, f32[384]{0:T(512)S(1)}, f32[384]{0:T(512)S(1)}, f32[384]{0:T(512)S(1)}, f32[384]{0:T(512)S(1)}, /*index=5*...) fusion(f32[2,16,32,384]{3,2,1,0:T(8,128)S(1)} %get-tuple-elemen, ...), kind=kLoop, calls=%fused_computation.132 | loop fusion | flops 14148864 | bytes 3173376 | tf_op jit(solution)/shard_map/transpose(jvp())/reduce_sum | solution.py:31
  300.2 3.7 fusion.42
  306.7 64.4 %all-reduce.50 = (f32[384]{0:T(512)S(1)}, f32[1536]{0:T(1024)S(1)}, f32[384]{0:T(512)S(1)}) all-reduce(f32[384]{0:T(512)S(1)} %get-tuple-element.56, f32[1536]{0:T(1024)S(1)} %get-tuple-element.124, f32[384]{0:T(512)S(1)} %multiply_reduce_fusion), channel_id=1, replica_groups=mesh['enc'=32,'bb'=4] {'enc','bb'}, use_global_device_ids=true, to_apply=%region_58.59 | all-reduce | flops 2304 | bytes 18432 | tf_op jit(solution)/shard_map/psum | solution.py:159
  372.3 98.5 %all-reduce.54.cloned.1.call-done = (f32[7,7,384]{2,1,0:T(8,128)}, f32[384,1536]{1,0:T(8,128)}, f32[1536,384]{1,0:T(8,128)}, f32[384,4096]{1,0:T(8,128)}) async-done(((f32[7,7,384]{2,1,0:T(8,128)}, f32[384,1536]{1,0:T(8,128)}, f32[1536,384]{1,0:T(8,128)}, f32[384,4096]{1,0:T(8,128)}), (f32[7,7,384]{2,1,0:T(8,128)}, f32[384,1536]{1,0:T(8,128)}, f32[1536,384]{1,0:T(8,128)}, ...) | async-done | bytes 11085328 | tf_op jit(solution)/shard_map/psum | solution.py:159
  472.3 3.0 multiply_convert_fusion.3
  475.3 2.9 multiply_convert_fusion.2
  478.2 2.1 multiply_convert_fusion
  (136 shorter events, 28.3 us)
Async XLA Ops:
  7.2 65.9 %copy-start = (bf16[384,4096]{1,0:T(8,128)(2,1)S(1)}, bf16[384,4096]{1,0:T(8,128)(2,1)}, u32[]{:S(2)}) copy-start(bf16[384,4096]{1,0:T(8,128)(2,1)} %param.20) | copy-start | bytes 9437188
  7.2 149.8 %all-gather.2.cloned.1.call-start = ((), (), s32[]{:S(2)}) async-start(), calls=%async_computation.3 | async-start | bytes 5242880 | tf_op jit(solution)/shard_map/all_gather | solution.py:136
  57.3 2.0 copy-start.2
  57.3 2.0 copy-start.15
  59.2 1.3 copy-start.20
  59.2 1.3 copy-start.22
  59.6 5.4 %copy-start.13 = (bf16[2,16,32,384]{3,2,1,0:T(8,128)(2,1)}, bf16[2,16,32,384]{3,2,1,0:T(8,128)(2,1)S(1)}, u32[]{:S(2)}) copy-start(bf16[2,16,32,384]{3,2,1,0:T(8,128)(2,1)S(1)} %multiply_convert_fusion.5) | copy-start | bytes 2359300
  60.5 4.6 copy-start.8
  60.5 4.6 copy-start.18
  60.5 4.6 copy-start.23
  65.0 3.5 copy-start.24
  73.1 3.7 copy-start.16
  73.1 3.7 copy-start.17
  118.0 107.3 %reduce-scatter.2.cloned.1.call-start = ((), (), s32[]{:S(2)}) async-start(), calls=%async_computation.4 | async-start | bytes 5242880 | tf_op jit(solution)/shard_map/reduce_scatter | solution.py:142
  227.6 22.7 %all-to-all-start.1 = ((bf16[32,4,4096]{2,1,0:T(4,128)(2,1)}), bf16[32,4,4096]{2,1,0:T(4,128)(2,1)}, u32[]{:S(2)}, u32[]{:S(2)}) async-start(bf16[32,4,4096]{2,1,0:T(4,128)(2,1)} %reshape.444), calls=%async_computation.2 | async-start | bytes 2097152 | tf_op jit(solution)/shard_map/all_to_all | solution.py:149
  234.7 236.1 %all-reduce.54.cloned.1.call-start = ((), (), s32[]{:S(2)}) async-start(), calls=%async_computation.5 | async-start | bytes 22192128 | tf_op jit(solution)/shard_map/psum | solution.py:159
  263.0 1.1 copy-start.10
  265.0 5.8 %copy-start.6 = (f32[1024,384]{1,0:T(8,128)}, f32[1024,384]{1,0:T(8,128)S(1)}, u32[]{:S(2)}) copy-start(f32[1024,384]{1,0:T(8,128)S(1)} %reshape.446) | copy-start | bytes 4718596
  265.0 5.8 %copy-start.19 = (bf16[1536,384]{1,0:T(8,128)(2,1)S(1)}, bf16[1536,384]{1,0:T(8,128)(2,1)}, u32[]{:S(2)}) copy-start(bf16[1536,384]{1,0:T(8,128)(2,1)} %param.18) | copy-start | bytes 3538948
  270.8 7.4 %copy-start.21 = (bf16[384,1536]{1,0:T(8,128)(2,1)S(1)}, bf16[384,1536]{1,0:T(8,128)(2,1)}, u32[]{:S(2)}) copy-start(bf16[384,1536]{1,0:T(8,128)(2,1)} %param.16) | copy-start | bytes 3538948
  278.3 1.8 copy-start.14
  280.1 2.8 copy-start.3
  283.4 1.4 copy-start.4
  283.4 1.6 copy-start.9
  294.1 5.3 %copy-start.11 = (bf16[32,2,4096]{2,1,0:T(2,128)(2,1)S(1)}, bf16[32,2,4096]{2,1,0:T(2,128)(2,1)}, u32[]{:S(2)}) copy-start(bf16[32,2,4096]{2,1,0:T(2,128)(2,1)} %broadcast_select_fusion) | copy-start | bytes 1572868
  304.5 1.4 copy-start.7
  304.5 1.9 copy-start.12
  472.3 5.8 %copy-start.5 = (f32[384,4096]{1,0:T(8,128)S(1)}, f32[384,4096]{1,0:T(8,128)}, u32[]{:S(2)}) copy-start(f32[384,4096]{1,0:T(8,128)} %get-tuple-element.114) | copy-start | bytes 18874372
  478.2 3.0 copy-start.1
Sparse Core Ops, SparseCore 0:
  118.2 38.7 all-gather.1
  174.9 50.4 reduce-scatter.1
  304.7 166.0 all-reduce.53
where the time goes:
time: 498 us; the launch traced here: 488 us
  waiting for transfers between devices  203 us (41%)
  blocking collectives  89.8 us (18%)
  other arithmetic  83.2 us (17%)
  matrix products  49.8 us (10%)
  local copies, waits for them, and re-layouts  39.1 us (8%)
  between operations  15.4 us (3%)
  starting transfers between devices  7.23 us (1%)
    psum x1, waiting for transfers between devices, on_device(): lax.psum((local_grads[0], local_grads[1], local_grads[2], local_grads[3],...  98.5 us
    psum x1, blocking collectives, on_device(): lax.psum((local_grads[0], local_grads[1], local_grads[2], local_grads[3],...  64.4 us
    reduce_scatter x1, waiting for transfers between devices, on_device(): lax.psum_scatter(contract_last(grad_pre, connector).astype(jnp.bfloat16),...  50.6 us
    reduce_sum x1, other arithmetic, front(): centered = conv_sum - jnp.mean(conv_sum, axis=-1, keepdims=True)  43.3 us
    all_gather x1, waiting for transfers between devices, on_device(): lax.all_gather(arrived, 'bb', axis=0, tiled=True)  38.9 us
    dot_general x4, matrix products, contract_last(): lax.dot_general(first_operand, second_operand, (((1,), (1,)), ((), ())),...  28.1 us
    all_to_all x1, blocking collectives, on_device(): lax.all_to_all(outgoing, 'enc', split_axis=0, concat_axis=0, tiled=True)  25.5 us
    all_to_all x1, waiting for transfers between devices, on_device(): lax.all_to_all(own_rows, 'enc', split_axis=0, concat_axis=0, tiled=True)  15.4 us
  transfers between devices with their start and end apart: 4, of which 4 were waited for; matrix products, arithmetic and copies ran while one was open for 0% of the time, Pallas kernels for 0%

commit v1 on v0

v1 whole, which is shorter than its diff:
```python
import functools

import jax
import jax.numpy as jnp
import numpy as np
from jax import lax
from jax.experimental import pallas as pl
from jax.experimental.pallas import tpu as pltpu
from jax.sharding import Mesh, PartitionSpec as P

EPS = 1e-06
GELU_A = float(np.sqrt(2.0 / np.pi))
GELU_B = 0.044715
BF = jnp.bfloat16
F32 = jnp.float32
ALL = ("yl", "z", "x", "yh", "co")
ENC = ("yl", "z", "x")
BB = ("yh", "co")
SAME_CORE = ("yl", "z", "x", "yh")
PLANE = ("z", "x")
COLS = ("yl", "yh", "co")
VMEM_LIMIT = 56 * 1024 * 1024


def nn(a, b):
    return lax.dot_general(a, b, (((1,), (0,)), ((), ())), preferred_element_type=F32)


def nt(a, b):
    return lax.dot_general(a, b, (((1,), (1,)), ((), ())), preferred_element_type=F32)


def gelu_parts(u):
    u2 = u * u
    t = jnp.tanh(u * (GELU_A + (GELU_A * GELU_B) * u2))
    half = 0.5 * (1.0 + t)
    value = u * half
    slope = half + 0.5 * u * (1.0 - t * t) * (GELU_A + (3.0 * GELU_A * GELU_B) * u2)
    return value, slope


def vmem():
    return pl.BlockSpec(memory_space=pltpu.VMEM)


def smem():
    return pl.BlockSpec(memory_space=pltpu.SMEM)


def call(kernel, out_shape, scratch, in_specs, flops=0, nbytes=0):
    multi = isinstance(out_shape, (list, tuple))
    return pl.pallas_call(
        kernel,
        out_shape=out_shape,
        in_specs=in_specs,
        out_specs=[vmem()] * len(out_shape) if multi else vmem(),
        scratch_shapes=scratch,
        compiler_params=pltpu.CompilerParams(vmem_limit_bytes=VMEM_LIMIT),
        cost_estimate=pl.CostEstimate(flops=flops, bytes_accessed=nbytes, transcendentals=0),
    )


def arrange_kernel(cot_ref, out_ref):
    r = lax.broadcasted_iota(jnp.int32, (512, 512), 0)
    s = lax.broadcasted_iota(jnp.int32, (512, 512), 1)
    want = ((r // 4) % 4) * 128 + (r // 16) * 4 + r % 4
    pick = jnp.where(s == want, 1.0, 0.0).astype(BF)
    out_ref[...] = nn(pick, cot_ref[...]).astype(BF)


def forward_kernel(
    x_ref, k_ref, gain_ref, win_ref, bias_ref, wout_ref, scale_ref, code_ref,
    pay_ref, normt_ref, xhat_ref, rstd_ref, slope_ref, hsum_ref, gsum_ref, bsum_ref, xs_ref,
    xf_ref, kb_ref, conv_ref, norm_ref, hs_ref,
):
    for lt in range(3):
        lanes = slice(lt * 128, lt * 128 + 128)
        kb_ref[lt] = k_ref[:, lanes]
        for t in range(2):
            xf_ref[lt, t] = x_ref[t, :, :, lanes].astype(F32)

    row = lax.broadcasted_iota(jnp.int32, (8, 128), 0)
    first = row == 0
    last = row == 7

    def split(n, carry):
        lt = n // 2
        t = n % 2
        for jj in range(4):
            for i in range(16):
                v = xf_ref[lt, t, i, pl.ds(jj, 8, stride=4), :]
                xs_ref[1, lt, t, jj, i] = v
                xs_ref[0, lt, t, jj, i] = jnp.where(first, 0.0, pltpu.roll(v, 1, 0))
                xs_ref[2, lt, t, jj, i] = jnp.where(last, 0.0, pltpu.roll(v, 7, 0))
        return carry

    lax.fori_loop(0, 6, split, 0)

    def conv(n, carry):
        lt = n // 8
        t = (n // 4) % 2
        jj = n % 4
        acc = [None] * 16
        for b in range(7):
            q = jj + (b + 1)
            s = q // 4
            jin = q % 4
            w = [
                jnp.broadcast_to(kb_ref[lt, pl.ds(a * 7 + b, 1), :], (8, 128)) for a in range(7)
            ]
            for r in range(16):
                v = xs_ref[s, lt, t, jin, r]
                for a in range(7):
                    i = r - a + 3
                    if 0 <= i < 16:
                        term = v * w[a]
                        acc[i] = term if acc[i] is None else acc[i] + term
        for i in range(16):
            conv_ref[lt, t, i // 4, jj, i % 4] = acc[i]
        return carry

    lax.fori_loop(0, 24, conv, 0)

    def block(n, carry):
        t = n // 4
        q = n % 4
        rows = pl.ds(pl.multiple_of(n * 128, 128), 128)
        c = [conv_ref[lt, t, q].reshape(128, 128) for lt in range(3)]
        mean = jnp.sum(c[0] + c[1] + c[2], axis=1, keepdims=True) * (1.0 / 384.0)
        c = [v - mean for v in c]
        var = jnp.sum(c[0] * c[0] + c[1] * c[1] + c[2] * c[2], axis=1, keepdims=True) * (
            1.0 / 384.0
        )
        rstd = lax.rsqrt(var + EPS)
        rstd_ref[rows, :] = jnp.broadcast_to(rstd, (128, 128))
        for lt in range(3):
            lanes = slice(lt * 128, lt * 128 + 128)
            xhat = c[lt] * rstd
            xhat_ref[lt, rows, :] = xhat
            normed = xhat * gain_ref[:, lanes]
            norm_ref[:, lanes] = normed.astype(BF)
            normt_ref[n, lanes, :] = normed.T.astype(BF)
        toks = pl.ds(pl.multiple_of(n * 8, 8), 8)
        for h in range(6):
            hid = slice(h * 256, h * 256 + 256)
            u = nn(norm_ref[...], win_ref[:, hid]) + bias_ref[:, hid]
            value, slope = gelu_parts(u)
            value = value.astype(BF).astype(F32)
            hs_ref[toks, hid] = jnp.sum(value.reshape(16, 8, 256), axis=0)
            gsum_ref[toks, hid] = jnp.sum(slope.reshape(16, 8, 256), axis=0)
            slope_ref[rows, hid] = slope.astype(BF)
        return carry

    lax.fori_loop(0, 8, block, 0)

    hs = hs_ref[...]
    hi = hs.astype(BF)
    hsum_ref[...] = hi
    lo = (hs - hi.astype(F32)).astype(BF)
    bsum = nn(hi, wout_ref[...]) + nn(lo, wout_ref[...])
    bsum_ref[...] = bsum
    for lt in range(3):
        lanes = slice(lt * 128, lt * 128 + 128)
        for t in range(2):
            for q in range(4):
                total = xs_ref[1, lt, t, 0, 4 * q]
                for jj in range(4):
                    for im in range(4):
                        if jj + im > 0:
                            total = total + xs_ref[1, lt, t, jj, 4 * q + im]
                tok = slice(t * 32 + q * 8, t * 32 + q * 8 + 8)
                hs_ref[tok, lanes] = total
    pooled = (hs_ref[:, 0:384] + scale_ref[...] * bsum) * (1.0 / 16.0)
    pay_ref[:, 0:384] = pooled.astype(BF)
    pay_ref[:, 384:512] = code_ref[...]


def forward(x, k, gain, win, bias, wout, scale, code):
    shape = jax.ShapeDtypeStruct
    return call(
        forward_kernel,
        [
            shape((64, 512), BF),
            shape((8, 384, 128), BF),
            shape((3, 1024, 128), F32),
            shape((1024, 128), F32),
            shape((1024, 1536), BF),
            shape((64, 1536), BF),
            shape((64, 1536), F32),
            shape((64, 384), F32),
            shape((3, 3, 2, 4, 16, 8, 128), F32),
        ],
        [
            pltpu.VMEM((3, 2, 16, 32, 128), F32),
            pltpu.VMEM((3, 49, 128), F32),
            pltpu.VMEM((3, 2, 4, 4, 4, 8, 128), F32),
            pltpu.VMEM((128, 384), BF),
            pltpu.VMEM((64, 1536), F32),
        ],
        [vmem()] * 8,
        flops=20_000_000_000,
        nbytes=10_000_000,
    )(x, k, gain, win, bias, wout, scale, code)


def connector_kernel(
    bb_ref, p0_ref, p1_ref, p2_ref, p3_ref, cot_ref, wc_ref, gp_ref, t_ref, s_ref,
    pick_ref, pool_ref,
):
    row = lax.broadcasted_iota(jnp.int32, (64, 128), 0)
    lane = lax.broadcasted_iota(jnp.int32, (64, 128), 1)
    for d, p_ref in enumerate((p0_ref, p1_ref, p2_ref, p3_ref)):
        tok = slice(d * 64, d * 64 + 64)
        pool_ref[tok, :] = p_ref[:, 0:384]
        code = p_ref[:, 384:512].astype(F32).astype(jnp.int32)
        src = bb_ref[0] ^ d
        want = (code >> 1) * 16 + src * 4 + (code & 1) * 2 + (row & 1)
        want = jnp.where(code < 0, -1, want)
        for q in range(4):
            pick_ref[tok, q * 128 : q * 128 + 128] = jnp.where(
                lane + q * 128 == want, 1.0, 0.0
            ).astype(BF)
    for h in range(7):
        cols = slice(h * 128, h * 128 + 128)
        cot = nn(pick_ref[...], cot_ref[:, cols])
        pre = nn(pool_ref[...], wc_ref[:, cols])
        gp_ref[:, cols] = (cot * gelu_parts(pre)[1]).astype(BF)
    t_ref[...] = nt(gp_ref[...], wc_ref[...])
    pool_t = pool_ref[...].astype(F32).T.astype(BF)
    s_ref[...] = nn(pool_t, gp_ref[...]).astype(BF)


def connector_part(bb, pays, cot, wc):
    shape = jax.ShapeDtypeStruct
    return call(
        connector_kernel,
        [shape((256, 896), BF), shape((256, 384), F32), shape((384, 896), BF)],
        [pltpu.VMEM((256, 512), BF), pltpu.VMEM((256, 384), BF)],
        [smem()] + [vmem()] * 6,
        flops=1_000_000_000,
        nbytes=2_000_000,
    )(bb, *pays, cot, wc)


def mlp_back_kernel(
    co_ref, dtok_ref, normt_ref, slope_ref, hsum_ref, gsum_ref, bsum_ref, wout_ref, scale_ref,
    keep_ref, send_ref, dpre_ref, small_ref, dh_ref,
):
    dtok = dtok_ref[...] * (1.0 / 16.0)
    small_ref[0:1, :] = jnp.sum(dtok * bsum_ref[...], axis=0, keepdims=True)
    dbr = (dtok * scale_ref[...]).astype(BF)
    dh_ref[...] = nt(dbr, wout_ref[...])
    db = jnp.sum(dh_ref[...] * gsum_ref[...], axis=0, keepdims=True)
    for q in range(4):
        small_ref[1 + q : 2 + q, :] = db[:, q * 384 : q * 384 + 384]
    small_ref[5:8, :] = jnp.zeros((3, 384), F32)

    def block(n, carry):
        rows = pl.ds(pl.multiple_of(n * 128, 128), 128)
        toks = pl.ds(pl.multiple_of(n * 8, 8), 8)
        for h in range(4):
            hid = slice(h * 384, h * 384 + 384)
            g = slope_ref[rows, hid].astype(F32).reshape(16, 8, 384)
            d = g * dh_ref[toks, hid][None]
            dpre_ref[h, rows, :] = d.reshape(128, 384).astype(BF)
        return carry

    lax.fori_loop(0, 8, block, 0)
    hsum_t = hsum_ref[...].astype(F32).T.astype(BF)
    normt = jnp.concatenate([normt_ref[n] for n in range(8)], axis=1)
    mine = co_ref[0] == 0
    for h in range(2):
        def put(out_ref):
            for q in range(2):
                rows = slice(q * 384, q * 384 + 384)
                out_ref[rows, :] = nn(normt, dpre_ref[2 * h + q]).astype(out_ref.dtype)
            out_ref[768:1536, :] = nn(hsum_t[h * 768 : h * 768 + 768], dbr).astype(out_ref.dtype)

        here = mine if h == 0 else jnp.logical_not(mine)

        @pl.when(here)
        def _():
            put(keep_ref)

        @pl.when(jnp.logical_not(here))
        def _():
            put(send_ref)


def mlp_back(co, dtok, normt, slope, hsum, gsum, bsum, wout, scale):
    shape = jax.ShapeDtypeStruct
    return call(
        mlp_back_kernel,
        [
            shape((1536, 384), BF),
            shape((1536, 384), BF),
            shape((4, 1024, 384), BF),
            shape((8, 384), F32),
        ],
        [pltpu.VMEM((64, 1536), F32)],
        [smem()] + [vmem()] * 8,
        flops=4_000_000_000,
        nbytes=10_000_000,
    )(co, dtok, normt, slope, hsum, gsum, bsum, wout, scale)


def front_back_kernel(
    dpre_ref, win_ref, xhat_ref, rstd_ref, gain_ref, xs_ref, out_ref, dc_ref, dk_ref
):
    def block(n, carry):
        t = n // 4
        q = n % 4
        rows = pl.ds(pl.multiple_of(n * 128, 128), 128)
        dn = nt(dpre_ref[0, rows, :], win_ref[:, 0:384])
        for h in range(1, 4):
            dn = dn + nt(dpre_ref[h, rows, :], win_ref[:, h * 384 : h * 384 + 384])
        rstd = rstd_ref[rows, :]
        dx = []
        xh = []
        gains = []
        for lt in range(3):
            lanes = slice(lt * 128, lt * 128 + 128)
            xhat = xhat_ref[lt, rows, :]
            part = dn[:, lanes]
            gains.append(jnp.sum((part * xhat).reshape(16, 8, 128), axis=0))
            dx.append(part * gain_ref[:, lanes])
            xh.append(xhat)
        m1 = jnp.sum(dx[0] + dx[1] + dx[2], axis=1, keepdims=True) * (1.0 / 384.0)
        m2 = jnp.sum(dx[0] * xh[0] + dx[1] * xh[1] + dx[2] * xh[2], axis=1, keepdims=True) * (
            1.0 / 384.0
        )
        for lt in range(3):
            dc = rstd * (dx[lt] - m1 - xh[lt] * m2)
            dc_ref[lt, t, q] = dc.reshape(4, 4, 8, 128)
        return tuple(c + g for c, g in zip(carry, gains))

    zero = jnp.zeros((8, 128), F32)
    gains = lax.fori_loop(0, 8, block, (zero, zero, zero))
    for lt in range(3):
        lanes = slice(lt * 128, lt * 128 + 128)
        out_ref[49:50, lanes] = jnp.sum(gains[lt], axis=0, keepdims=True)

    dk_ref[...] = jnp.zeros_like(dk_ref)

    def conv(n, carry):
        lt = n // 8
        t = (n // 4) % 2
        jj = n % 4
        d = [dc_ref[lt, t, i // 4, jj, i % 4] for i in range(16)]
        for b in range(7):
            q = jj + (b + 1)
            s = q // 4
            jin = q % 4
            acc = [None] * 7
            for r in range(16):
                v = xs_ref[s, lt, t, jin, r]
                for a in range(7):
                    i = r - a + 3
                    if 0 <= i < 16:
                        term = v * d[i]
                        acc[a] = term if acc[a] is None else acc[a] + term
            for a in range(7):
                dk_ref[lt, a * 7 + b] += acc[a]
        return carry

    lax.fori_loop(0, 24, conv, 0)
    for lt in range(3):
        lanes = slice(lt * 128, lt * 128 + 128)
        out_ref[0:49, lanes] = jnp.sum(dk_ref[lt], axis=1)
    out_ref[50:56, :] = jnp.zeros((6, 384), F32)


def front_back(dpre, win, xhat, rstd, gain, xs):
    return call(
        front_back_kernel,
        jax.ShapeDtypeStruct((56, 384), F32),
        [pltpu.VMEM((3, 2, 4, 4, 4, 8, 128), F32), pltpu.VMEM((3, 49, 8, 128), F32)],
        [vmem()] * 6,
        flops=10_000_000_000,
        nbytes=10_000_000,
    )(dpre, win, xhat, rstd, gain, xs)


def swap(v, axes, size, d):
    return lax.ppermute(v, axes, [(i, i ^ d) for i in range(size)])


def ring_sum(v, axes, size):
    others = [lax.ppermute(v, axes, [(i, (i + d) % size) for i in range(size)]) for d in range(1, size)]
    for other in others:
        v = v + other
    return v


def exchange(v, axes):
    return lax.all_to_all(v, axes, split_axis=0, concat_axis=0, tiled=True)


def spread(v, axes, size):
    return exchange(jnp.broadcast_to(v[None], (size,) + v.shape), axes)


def on_device(
    image_tiles,
    depth_kernel,
    norm_gain,
    weight_in,
    bias_in,
    weight_out,
    layer_scale,
    weight_proj,
    image_counts,
    destination,
    row_offset,
    connector,
    cotangent,
):
    bb = lax.axis_index(BB).astype(jnp.int32)
    co = lax.axis_index("co").astype(jnp.int32)
    factor = 1.0 / 128.0

    sent = call(
        arrange_kernel, jax.ShapeDtypeStruct((512, 896), BF), [], [vmem()], 500_000_000, 2_000_000
    )(cotangent)
    cot = exchange(sent.reshape(32, 16, 896), ENC).reshape(512, 896)

    live = jnp.arange(32, dtype=jnp.int32) // 16 < image_counts[0]
    code = jnp.where(live, destination[0] * 2 + row_offset[0], -1).astype(BF)
    code = jnp.broadcast_to(jnp.repeat(code, 2)[:, None], (64, 128))
    gain = norm_gain.reshape(1, 384)
    scale = layer_scale.reshape(1, 384)
    pay, normt, xhat, rstd, slope, hsum, gsum, bsum, xs = forward(
        image_tiles,
        depth_kernel.reshape(49, 384),
        gain,
        weight_in,
        bias_in.reshape(1, 1536),
        weight_out,
        scale,
        code,
    )
    wc = nn(weight_proj, connector).astype(BF)
    pays = [pay] + [swap(pay, BB, 4, d) for d in (1, 2, 3)]
    grad_pre, tok, outer = connector_part(bb.reshape(1), pays, cot, wc)

    tok = tok.reshape(4, 64, 384)
    near = swap(jnp.concatenate([tok[1], tok[3]], axis=0), "co", 2, 1)
    far = swap(tok[2] + near[64:], "yh", 2, 1)
    dtok = tok[0] + near[:64] + far

    keep, send, dpre, small_a = mlp_back(
        co.reshape(1), dtok, normt, slope, hsum, gsum, bsum, weight_out, scale
    )
    pair = keep.astype(F32) + swap(send, "co", 2, 1).astype(F32)
    parts = exchange(pair.astype(BF).reshape(64, 24, 384), SAME_CORE)
    mine = (jnp.sum(parts.astype(F32), axis=0) * factor).astype(BF)

    small_b = front_back(dpre, weight_in, xhat, rstd, gain, xs)
    small = jnp.concatenate([small_a, small_b], axis=0)
    small = small + swap(small, "co", 2, 1)
    small = ring_sum(small, "x", 4)
    small = ring_sum(small, "z", 4)
    small = ring_sum(small, ("yl", "yh"), 4) * factor

    rows = nt(grad_pre, connector).astype(BF).reshape(4, 64, 4096)
    near = swap(jnp.concatenate([rows[1], rows[3]], axis=0), "co", 2, 1).astype(F32)
    far = swap((rows[2].astype(F32) + near[64:]).astype(BF), "yh", 2, 1)
    token_grads = (rows[0].astype(F32) + near[:64] + far.astype(F32)).astype(BF)

    outer = jnp.sum(exchange(outer.reshape(16, 24, 896), PLANE).astype(F32), axis=0).astype(BF)
    proj = lax.dot_general(
        connector.reshape(8, 512, 896), outer, (((2,), (1,)), ((), ())), preferred_element_type=F32
    )
    proj = proj.transpose(0, 2, 1).astype(BF)
    proj = jnp.sum(exchange(proj, COLS).astype(F32), axis=0) * factor
    proj = spread(proj.astype(BF), SAME_CORE, 64)
    other = swap(proj, "co", 2, 1)
    both = jnp.stack([jnp.where(co == 0, proj, other), jnp.where(co == 0, other, proj)])
    both = both.reshape(2, 2, 16, 2, 24, 512).transpose(2, 4, 1, 3, 0, 5)
    grad_proj = both.reshape(384, 4096)

    full = spread(mine, SAME_CORE, 64).reshape(1536, 384)
    other = swap(full, "co", 2, 1)
    low = jnp.where(co == 0, full, other)
    high = jnp.where(co == 0, other, full)
    grad_in = jnp.concatenate([low[:384], low[384:768], high[:384], high[384:768]], axis=1)
    grad_out = jnp.concatenate([low[768:], high[768:]], axis=0)

    return (
        small[8:57].reshape(7, 7, 384),
        small[57],
        grad_in,
        small[1:5].reshape(1536),
        grad_out,
        small[0],
        grad_proj,
        token_grads,
    )


def solution(mesh):
    fine = Mesh(mesh.devices.reshape(2, 4, 4, 2, 2), ALL)
    in_specs = (
        P(ALL, None, None, None),
        P(),
        P(),
        P(),
        P(),
        P(),
        P(),
        P(),
        P(ALL),
        P(ALL, None),
        P(ALL, None),
        P(None, BB),
        P(ENC, BB),
    )
    out_specs = (P(), P(), P(), P(), P(), P(), P(), P(ALL, None))
    return jax.shard_map(
        on_device, mesh=fine, in_specs=in_specs, out_specs=out_specs, check_vma=False
    )
```

time: 498 us -> 245 us (0.49); the launches traced: 488 us -> 244 us
  waiting for transfers between devices: 203 us -> 64.7 us
  blocking collectives: 89.8 us -> 0 us
  other arithmetic: 83.2 us -> 21 us
  starting transfers between devices: 7.23 us -> 68.1 us
  Pallas kernels: 0 us -> 49.9 us
  matrix products: 49.8 us -> 19.4 us
  local copies, waits for them, and re-layouts: 39.1 us -> 19.3 us
  between operations: 15.4 us -> 1.74 us
    psum x1 -> x0, waiting for transfers between devices: 98.5 us -> none  [on_device(): lax.psum((local_grads[0], local_grads[1], local_grads[2], local_grads[3],...]
    psum x1 -> x0, blocking collectives: 64.4 us -> none  [on_device(): lax.psum((local_grads[0], local_grads[1], local_grads[2], local_grads[3],...]
    reduce_sum x9 -> x3, other arithmetic: 63 us -> 0.32 us  [the longest x1 0.19 us: on_device(): mine = (jnp.sum(parts.astype(F32), axis=0) * factor).astype(BF)]
    reduce_scatter x1 -> x0, waiting for transfers between devices: 50.6 us -> none  [on_device(): lax.psum_scatter(contract_last(grad_pre, connector).astype(jnp.bfloat16),...]
    pallas_call x0 -> x5, Pallas kernels: none -> 49.9 us  [the longest x1 19.5 us: forward(): call(forward_kernel, [shape((64, 512), BF), shape((8, 384, 128), BF), sha...]
    all_gather x1 -> x0, waiting for transfers between devices: 38.9 us -> none  [on_device(): lax.all_gather(arrived, 'bb', axis=0, tiled=True)]
    ppermute x0 -> x20, starting transfers between devices: none -> 32.2 us  [the longest x11 20.8 us: swap(): return lax.ppermute(v, axes, [(i, i ^ d) for i in range(size)])]
    ppermute x0 -> x20, waiting for transfers between devices: none -> 31.4 us  [the longest x9 26.5 us: ring_sum(): lax.ppermute(v, axes, [(i, (i + d) % size) for i in range(size)])]
  transfers between devices with their start and end apart: 4 -> 26, of which waited for: 4 -> 12; matrix products, arithmetic and copies ran while one was open for 0% -> 18% of each run, Pallas kernels for 0% -> 7%
where the time goes in v1:
time: 245 us; the launch traced here: 244 us
  starting transfers between devices  68.1 us (28%)
  waiting for transfers between devices  64.7 us (26%)
  Pallas kernels  49.9 us (20%)
  other arithmetic  21 us (9%)
  matrix products  19.4 us (8%)
  local copies, waits for them, and re-layouts  19.3 us (8%)
    all_to_all x6, starting transfers between devices, exchange(): return lax.all_to_all(v, axes, split_axis=0, concat_axis=0, tiled=True)  35.9 us
    all_to_all x6, waiting for transfers between devices, exchange(): return lax.all_to_all(v, axes, split_axis=0, concat_axis=0, tiled=True)  33.3 us
    ppermute x9, waiting for transfers between devices, ring_sum(): lax.ppermute(v, axes, [(i, (i + d) % size) for i in range(size)])  26.5 us
    ppermute x11, starting transfers between devices, swap(): return lax.ppermute(v, axes, [(i, i ^ d) for i in range(size)])  20.8 us
    pallas_call x1, Pallas kernels, forward(): call(forward_kernel, [shape((64, 512), BF), shape((8, 384, 128), BF), sha...  19.5 us
    pallas_call x1, Pallas kernels, front_back(): call(front_back_kernel, jax.ShapeDtypeStruct((56, 384), F32), [pltpu.VMEM...  15.1 us
    ppermute x9, starting transfers between devices, ring_sum(): lax.ppermute(v, axes, [(i, (i + d) % size) for i in range(size)])  11.3 us
    pallas_call x1, Pallas kernels, mlp_back(): call(mlp_back_kernel, [shape((1536, 384), BF), shape((1536, 384), BF), sh...  8.55 us
  transfers between devices with their start and end apart: 26, of which 12 were waited for; matrix products, arithmetic and copies ran while one was open for 18% of the time, Pallas kernels for 7%

profile of v1, /device:TPU:1, one launch (start us, length us, event | category | flops | bytes accessed | tf_op | source)
XLA Modules:
  0.0 244.1 jit_solution(5217419533915500749)
XLA Ops:
  8.5 19.5 %shard_map.188 = (bf16[64,512]{1,0:T(8,128)(2,1)}, bf16[8,384,128]{2,1,0:T(8,128)(2,1)}, f32[3,1024,128]{2,1,0:T(8,128)}, f32[1024,128]{1,0:T(8,128)}, bf16[1024...) custom-call(bf16[2,16,32,384]{3,2,1,0:T(8,128)(2,1)} %x_ref.1, ...), custom_call_target="tpu_custom_call" | custom-call | flops 20000000000 | bytes 10000000 | tf_op jit(solution)/shard_map/pallas_call | solution.py:180
  28.0 4.3 %collective-permute-start.2 = (bf16[64,512]{1,0:T(8,128)(2,1)}, bf16[64,512]{1,0:T(8,128)(2,1)S(1)}, u32[]{:S(2)}, u32[]{:S(2)}) collective-permute-start(bf16[64,512]{1,0:T(8,128)(2,1)} %get-tuple-element.24.p0_ref), channel_id=1, source_target_pairs={{0,3},{1,2},{2,1},{3,0},{4,7},{5,6},{6,5},{7,4},{8,11},{9,10},{10,... | collective-permute-start | bytes 196616 | tf_op jit(solution)/shard_map/ppermute | solution.py:385
  32.8 2.8 %shard_map.189 = bf16[512,896]{1,0:T(8,128)(2,1)} custom-call(bf16[512,896]{1,0:T(8,128)(2,1)} %cot_ref.1), custom_call_target="tpu_custom_call" | custom-call | flops 500000000 | bytes 2000000 | tf_op jit(solution)/shard_map/pallas_call | solution.py:422
  35.6 8.7 %all-to-all-start = ((bf16[32,16,896]{2,1,0:T(8,128)(2,1)}), bf16[32,16,896]{2,1,0:T(8,128)(2,1)}, u32[]{:S(2)}, u32[]{:S(2)}) async-start(bf16[32,16,896]{2,1,0:T(8,128)(2,1)} %bitcast.31), calls=%async_computation | async-start | bytes 1835008 | tf_op jit(solution)/shard_map/all_to_all | solution.py:396
  44.3 6.5 %convolution_convert_fusion.1.wc_ref = bf16[384,896]{1,0:T(8,128)(2,1)} fusion(bf16[384,4096]{1,0:T(8,128)(2,1)S(1)} %copy-done, bf16[4096,896]{1,0:T(8,128)(2,1)} %param.24), kind=kOutput, calls=%fused_computation.6 | convolution fusion | flops 2818916352 | bytes 11173888 | tf_op jit(solution)/shard_map/dot_general | solution.py:26
  50.9 7.9 %all-to-all-done = bf16[32,16,896]{2,1,0:T(8,128)(2,1)} async-done(((bf16[32,16,896]{2,1,0:T(8,128)(2,1)}), bf16[32,16,896]{2,1,0:T(8,128)(2,1)}, u32[]{:S(2)}, u32[]{:S(2)}) %all-to-all-start) | async-done | bytes 917536 | tf_op jit(solution)/shard_map/all_to_all | solution.py:396
  58.8 3.9 %shard_map.190 = (bf16[256,896]{1,0:T(8,128)(2,1)}, f32[256,384]{1,0:T(8,128)}, bf16[384,896]{1,0:T(8,128)(2,1)}) custom-call(s32[1]{0:T(128)} %bitcast.1.bb_ref, bf16[64,512]{1,0:T(8,128)(2,1)} %get-tuple-element.24.p0_ref, bf16[64,512]{1,0:T(8,128)(2,1)} %copy-done.7, bf16[64,512]{1,0:T(8,128)(2,1)} %copy-done.6, bf16[64,512]{1,0:T(8,128)(2,1)} %copy-done.5, ...), custom_call_target="tpu_custom_call" | custom-call | flops 1000000000 | bytes 2000000 | tf_op jit(solution)/shard_map/pallas_call | solution.py:235
  67.8 2.7 %collective-permute-start.4 = (f32[64,384]{1,0:T(8,128)S(1)}, f32[64,384]{1,0:T(8,128)S(1)}, u32[]{:S(2)}, u32[]{:S(2)}) collective-permute-start(f32[64,384]{1,0:T(8,128)S(1)} %slice_add_fusion.2), channel_id=1, source_target_pairs={{0,2},{2,0},{1,3},{3,1},{4,6},{6,4},{5,7},{7,5},{8,10},{10,8},{9,1... | collective-permute-start | bytes 294920 | tf_op jit(solution)/shard_map/ppermute | solution.py:385
  70.5 2.9 %collective-permute-done.4 = f32[64,384]{1,0:T(8,128)S(1)} collective-permute-done((f32[64,384]{1,0:T(8,128)S(1)}, f32[64,384]{1,0:T(8,128)S(1)}, u32[]{:S(2)}, u32[]{:S(2)}) %collective-permute-start.4) | collective-permute-done | bytes 98336 | tf_op jit(solution)/shard_map/ppermute | solution.py:385
  74.9 8.5 %shard_map.191 = (bf16[1536,384]{1,0:T(8,128)(2,1)}, bf16[1536,384]{1,0:T(8,128)(2,1)}, bf16[4,1024,384]{2,1,0:T(8,128)(2,1)}, f32[8,384]{1,0:T(8,128)}) custom-call(s32[1]{0:T(128)} %bitcast.co_ref, f32[64,384]{1,0:T(8,128)} %fusion.4.dtok_ref, bf16[8,384,128]{2,1,0:T(8,128)(2,1)} %get-tuple-element.26.normt_ref, ...), custom_call_target="tpu_custom_call" | custom-call | flops 4000000000 | bytes 10000000 | tf_op jit(solution)/shard_map/pallas_call | solution.py:292
  84.9 3.8 %all-to-all-start.3 = ((bf16[16,24,896]{2,1,0:T(8,128)(2,1)}), bf16[16,24,896]{2,1,0:T(8,128)(2,1)S(1)}, u32[]{:S(2)}, u32[]{:S(2)}) async-start(bf16[16,24,896]{2,1,0:T(8,128)(2,1)} %bitcast.8), calls=%async_computation.3 | async-start | bytes 1376256 | tf_op jit(solution)/shard_map/all_to_all | solution.py:396
  88.7 6.8 %convolution_convert_fusion = bf16[256,4096]{1,0:T(8,128)(2,1)} fusion(bf16[256,896]{1,0:T(8,128)(2,1)S(1)} %copy-done.8, bf16[4096,896]{1,0:T(8,128)(2,1)} %param.24), kind=kOutput, calls=%fused_computation | convolution fusion | flops 1880096768 | bytes 9895936 | tf_op jit(solution)/shard_map/dot_general | solution.py:30
  95.5 5.9 %all-to-all-done.3 = bf16[16,24,896]{2,1,0:T(8,128)(2,1)S(1)} async-done(((bf16[16,24,896]{2,1,0:T(8,128)(2,1)}), bf16[16,24,896]{2,1,0:T(8,128)(2,1)S(1)}, u32[]{:S(2)}, u32[]{:S(2)}) %all-to-all-start.3) | async-done | bytes 688160 | tf_op jit(solution)/shard_map/all_to_all | solution.py:396
  101.5 6.1 %fusion = bf16[8,24,512]{2,1,0:T(8,128)(2,1)} fusion(bf16[8,512,896]{2,1,0:T(8,128)(2,1)} %bitcast.28, bf16[24,896]{1,0:T(8,128)(2,1)S(1)} %reduce_sum.31), kind=kOutput, calls=%fused_computation.12 | convolution fusion | flops 176259072 | bytes 7579648 | tf_op jit(solution)/shard_map/dot_general | solution.py:471
  107.6 5.6 %all-to-all-start.4 = ((bf16[8,24,512]{2,1,0:T(8,128)(2,1)}), bf16[8,24,512]{2,1,0:T(8,128)(2,1)S(1)}, u32[]{:S(2)}, u32[]{:S(2)}) async-start(bf16[8,24,512]{2,1,0:T(8,128)(2,1)} %fusion), calls=%async_computation.4 | async-start | bytes 393216 | tf_op jit(solution)/shard_map/all_to_all | solution.py:396
  113.3 2.7 %add_convert_fusion = bf16[1536,384]{1,0:T(8,128)(2,1)} fusion(bf16[1536,384]{1,0:T(8,128)(2,1)} %collective-permute-done.15, bf16[1536,384]{1,0:T(8,128)(2,1)S(1)} %copy-done.3), kind=kLoop, calls=%fused_computation.3 | loop fusion | flops 2359296 | bytes 3538944 | tf_op jit(solution)/shard_map/convert_element_type | solution.py:455
  116.0 3.1 %all-to-all-done.4 = bf16[8,24,512]{2,1,0:T(8,128)(2,1)S(1)} async-done(((bf16[8,24,512]{2,1,0:T(8,128)(2,1)}), bf16[8,24,512]{2,1,0:T(8,128)(2,1)S(1)}, u32[]{:S(2)}, u32[]{:S(2)}) %all-to-all-start.4) | async-done | bytes 196640 | tf_op jit(solution)/shard_map/all_to_all | solution.py:396
  119.1 4.7 %all-to-all-start.1 = ((bf16[64,24,384]{2,1,0:T(8,128)(2,1)}), bf16[64,24,384]{2,1,0:T(8,128)(2,1)S(1)}, u32[]{:S(2)}, u32[]{:S(2)}) async-start(bf16[64,24,384]{2,1,0:T(8,128)(2,1)} %bitcast.6), calls=%async_computation.1 | async-start | bytes 2359296 | tf_op jit(solution)/shard_map/all_to_all | solution.py:396
  125.1 16.4 %all-to-all-done.1 = bf16[64,24,384]{2,1,0:T(8,128)(2,1)S(1)} async-done(((bf16[64,24,384]{2,1,0:T(8,128)(2,1)}), bf16[64,24,384]{2,1,0:T(8,128)(2,1)S(1)}, u32[]{:S(2)}, u32[]{:S(2)}) %all-to-all-start.1) | async-done | bytes 1179680 | tf_op jit(solution)/shard_map/all_to_all | solution.py:396
  142.8 6.1 %all-to-all-start.5 = ((bf16[64,24,512]{2,1,0:T(8,128)(2,1)}), bf16[64,24,512]{2,1,0:T(8,128)(2,1)}, u32[]{:S(2)}, u32[]{:S(2)}) async-start(bf16[64,24,512]{2,1,0:T(8,128)(2,1)} %broadcast_in_dim.28), calls=%async_computation.5 | async-start | bytes 3145728 | tf_op jit(solution)/shard_map/all_to_all | solution.py:396
  148.9 15.1 %shard_map.192 = f32[56,384]{1,0:T(8,128)} custom-call(bf16[4,1024,384]{2,1,0:T(8,128)(2,1)} %get-tuple-element.32.dpre_ref, bf16[384,1536]{1,0:T(8,128)(2,1)} %win_ref.3, f32[3,1024,128]{2,1,0:T(8,128)} %get-tuple-element.33.xhat_ref, f32[1024,128]{1,0:T(8,128)} %get-tuple-element.34.rstd_ref, f32[1,384]{1,0:T(1,128)} %reshape.99.gain_ref, ...), custom_call_target="tpu_custom_call" | custom-call | flops 10000000000 | bytes 10000000 | tf_op jit(solution)/shard_map/pallas_call | solution.py:374
  173.3 3.4 %collective-permute-done.7 = f32[64,384]{1,0:T(8,128)S(1)} collective-permute-done((f32[64,384]{1,0:T(8,128)S(1)}, f32[64,384]{1,0:T(8,128)S(1)}, u32[]{:S(2)}, u32[]{:S(2)}) %collective-permute-start.7) | collective-permute-done | bytes 98336 | tf_op jit(solution)/shard_map/ppermute | solution.py:389
  176.6 3.0 %collective-permute-done.6 = f32[64,384]{1,0:T(8,128)S(1)} collective-permute-done((f32[64,384]{1,0:T(8,128)S(1)}, f32[64,384]{1,0:T(8,128)S(1)}, u32[]{:S(2)}, u32[]{:S(2)}) %collective-permute-start.6) | collective-permute-done | bytes 98336 | tf_op jit(solution)/shard_map/ppermute | solution.py:389
  179.7 2.6 %collective-permute-start.11 = (f32[64,384]{1,0:T(8,128)S(1)}, f32[64,384]{1,0:T(8,128)S(1)}, u32[]{:S(2)}, u32[]{:S(2)}) collective-permute-start(f32[64,384]{1,0:T(8,128)S(1)} %add_add_fusion.1), channel_id=1, source_target_pairs={{0,48},{16,0},{32,16},{48,32},{1,49},{17,1},{33,17},{49,33},{2,50}... | collective-permute-start | bytes 294920 | tf_op jit(solution)/shard_map/ppermute | solution.py:389
  186.2 7.0 %all-to-all-start.2 = ((bf16[64,24,384]{2,1,0:T(8,128)(2,1)}), bf16[64,24,384]{2,1,0:T(8,128)(2,1)}, u32[]{:S(2)}, u32[]{:S(2)}) async-start(bf16[64,24,384]{2,1,0:T(8,128)(2,1)} %broadcast_in_dim.27), calls=%async_computation.2 | async-start | bytes 2359296 | tf_op jit(solution)/shard_map/all_to_all | solution.py:396
  194.3 2.5 %collective-permute-start.19 = (bf16[64,4096]{1,0:T(8,128)(2,1)S(1)}, bf16[64,4096]{1,0:T(8,128)(2,1)S(1)}, u32[]{:S(2)}, u32[]{:S(2)}) collective-permute-start(bf16[64,4096]{1,0:T(8,128)(2,1)S(1)} %fusion.1), channel_id=1, source_target_pairs={{0,2},{2,0},{1,3},{3,1},{4,6},{6,4},{5,7},{7,5},{8,10},{10,8},{9,1... | collective-permute-start | bytes 1572872 | tf_op jit(solution)/shard_map/ppermute | solution.py:385
  196.8 2.7 %collective-permute-start.17 = (bf16[64,24,512]{2,1,0:T(8,128)(2,1)}, bf16[64,24,512]{2,1,0:T(8,128)(2,1)}, u32[]{:S(2)}, u32[]{:S(2)}) collective-permute-start(bf16[64,24,512]{2,1,0:T(8,128)(2,1)} %all-to-all-done.5), channel_id=1, source_target_pairs={{0,1},{1,0},{2,3},{3,2},{4,5},{5,4},{6,7},{7,6},{8,9},{9,8},{10,11... | collective-permute-start | bytes 4718600 | tf_op jit(solution)/shard_map/ppermute | solution.py:385
  201.5 3.0 %collective-permute-start.12 = (f32[64,384]{1,0:T(8,128)S(1)}, f32[64,384]{1,0:T(8,128)}, u32[]{:S(2)}, u32[]{:S(2)}) collective-permute-start(f32[64,384]{1,0:T(8,128)S(1)} %add_add_fusion), channel_id=1, source_target_pairs={{0,2},{2,64},{64,66},{66,0},{1,3},{3,65},{65,67},{67,1},{4,6},{6,6... | collective-permute-start | bytes 294920 | tf_op jit(solution)/shard_map/ppermute | solution.py:389
  204.5 16.1 %collective-permute-done.14 = f32[64,384]{1,0:T(8,128)S(1)} collective-permute-done((f32[64,384]{1,0:T(8,128)S(1)}, f32[64,384]{1,0:T(8,128)S(1)}, u32[]{:S(2)}, u32[]{:S(2)}) %collective-permute-start.14) | collective-permute-done | bytes 98336 | tf_op jit(solution)/shard_map/ppermute | solution.py:389
  220.6 3.4 %collective-permute-done.12 = f32[64,384]{1,0:T(8,128)} collective-permute-done((f32[64,384]{1,0:T(8,128)S(1)}, f32[64,384]{1,0:T(8,128)}, u32[]{:S(2)}, u32[]{:S(2)}) %collective-permute-start.12) | collective-permute-done | bytes 98336 | tf_op jit(solution)/shard_map/ppermute | solution.py:389
  232.4 3.2 %copy.21 = bf16[16,24,2,2,2,512]{5,4,3,2,1,0:T(2,128)(2,1)S(1)} copy(bf16[16,24,2,2,2,512]{5,1,3,0,2,4:T(8,128)(2,1)S(1)} %maximum_bitcast_fusion) | data formatting | bytes 6291456 | tf_op jit(solution)/shard_map/transpose | solution.py:479
  235.6 4.0 %reshape.110 = bf16[384,4096]{1,0:T(8,128)(2,1)} reshape(bf16[16,24,2,2,2,512]{5,4,3,2,1,0:T(2,128)(2,1)S(1)} %copy.21) | data formatting | bytes 6291456 | tf_op jit(solution)/shard_map/reshape | solution.py:480
  (91 shorter events, 47.3 us)
Async XLA Ops:
  0.6 43.7 %copy-start = (bf16[384,4096]{1,0:T(8,128)(2,1)S(1)}, bf16[384,4096]{1,0:T(8,128)(2,1)}, u32[]{:S(2)}) copy-start(bf16[384,4096]{1,0:T(8,128)(2,1)} %param.20) | copy-start | bytes 9437188
  28.0 22.9 %collective-permute-start.2 = (bf16[64,512]{1,0:T(8,128)(2,1)}, bf16[64,512]{1,0:T(8,128)(2,1)S(1)}, u32[]{:S(2)}, u32[]{:S(2)}) collective-permute-start(bf16[64,512]{1,0:T(8,128)(2,1)} %get-tuple-element.24.p0_ref), channel_id=1, source_target_pairs={{0,3},{1,2},{2,1},{3,0},{4,7},{5,6},{6,5},{7,4},{8,11},{9,10},{10,... | collective-permute-start | bytes 196616 | tf_op jit(solution)/shard_map/ppermute | solution.py:385
  32.3 18.6 %collective-permute-start.1 = (bf16[64,512]{1,0:T(8,128)(2,1)}, bf16[64,512]{1,0:T(8,128)(2,1)S(1)}, u32[]{:S(2)}, u32[]{:S(2)}) collective-permute-start(bf16[64,512]{1,0:T(8,128)(2,1)} %get-tuple-element.24.p0_ref), channel_id=1, source_target_pairs={{0,2},{1,3},{2,0},{3,1},{4,6},{5,7},{6,4},{7,5},{8,10},{9,11},{10,... | collective-permute-start | bytes 196616 | tf_op jit(solution)/shard_map/ppermute | solution.py:385
  32.3 18.6 %collective-permute-start = (bf16[64,512]{1,0:T(8,128)(2,1)}, bf16[64,512]{1,0:T(8,128)(2,1)S(1)}, u32[]{:S(2)}, u32[]{:S(2)}) collective-permute-start(bf16[64,512]{1,0:T(8,128)(2,1)} %get-tuple-element.24.p0_ref), channel_id=1, source_target_pairs={{0,1},{1,0},{2,3},{3,2},{4,5},{5,4},{6,7},{7,6},{8,9},{9,8},{10,11... | collective-permute-start | bytes 196616 | tf_op jit(solution)/shard_map/ppermute | solution.py:385
  35.6 23.2 %all-to-all-start = ((bf16[32,16,896]{2,1,0:T(8,128)(2,1)}), bf16[32,16,896]{2,1,0:T(8,128)(2,1)}, u32[]{:S(2)}, u32[]{:S(2)}) async-start(bf16[32,16,896]{2,1,0:T(8,128)(2,1)} %bitcast.31), calls=%async_computation | async-start | bytes 1835008 | tf_op jit(solution)/shard_map/all_to_all | solution.py:396
  50.9 7.9 %copy-start.5 = (bf16[64,512]{1,0:T(8,128)(2,1)}, bf16[64,512]{1,0:T(8,128)(2,1)S(1)}, u32[]{:S(2)}) copy-start(bf16[64,512]{1,0:T(8,128)(2,1)S(1)} %collective-permute-done.2.p3_ref) | copy-start | bytes 196612
  63.7 3.2 %collective-permute-start.3 = (f32[128,384]{1,0:T(8,128)S(1)}, f32[128,384]{1,0:T(8,128)S(1)}, u32[]{:S(2)}, u32[]{:S(2)}) collective-permute-start(f32[128,384]{1,0:T(8,128)S(1)} %pad_maximum_fusion.3), channel_id=1, source_target_pairs={{0,1},{1,0},{2,3},{3,2},{4,5},{5,4},{6,7},{7,6},{8,9},{9,8},{10,11... | collective-permute-start | bytes 589832 | tf_op jit(solution)/shard_map/ppermute | solution.py:385
  67.8 5.6 %collective-permute-start.4 = (f32[64,384]{1,0:T(8,128)S(1)}, f32[64,384]{1,0:T(8,128)S(1)}, u32[]{:S(2)}, u32[]{:S(2)}) collective-permute-start(f32[64,384]{1,0:T(8,128)S(1)} %slice_add_fusion.2), channel_id=1, source_target_pairs={{0,2},{2,0},{1,3},{3,1},{4,6},{6,4},{5,7},{7,5},{8,10},{10,8},{9,1... | collective-permute-start | bytes 294920 | tf_op jit(solution)/shard_map/ppermute | solution.py:385
  74.9 13.7 %copy-start.8 = (bf16[256,896]{1,0:T(8,128)(2,1)S(1)}, bf16[256,896]{1,0:T(8,128)(2,1)}, u32[]{:S(2)}) copy-start(bf16[256,896]{1,0:T(8,128)(2,1)} %get-tuple-element.39) | copy-start | bytes 1376260
  83.5 29.8 %collective-permute-start.15 = (bf16[1536,384]{1,0:T(8,128)(2,1)}, bf16[1536,384]{1,0:T(8,128)(2,1)}, u32[]{:S(2)}, u32[]{:S(2)}) collective-permute-start(bf16[1536,384]{1,0:T(8,128)(2,1)} %get-tuple-element.37), channel_id=1, source_target_pairs={{0,1},{1,0},{2,3},{3,2},{4,5},{5,4},{6,7},{7,6},{8,9},{9,8},{10,11... | collective-permute-start | bytes 3538952 | tf_op jit(solution)/shard_map/ppermute | solution.py:385
  84.9 16.5 %all-to-all-start.3 = ((bf16[16,24,896]{2,1,0:T(8,128)(2,1)}), bf16[16,24,896]{2,1,0:T(8,128)(2,1)S(1)}, u32[]{:S(2)}, u32[]{:S(2)}) async-start(bf16[16,24,896]{2,1,0:T(8,128)(2,1)} %bitcast.8), calls=%async_computation.3 | async-start | bytes 1376256 | tf_op jit(solution)/shard_map/all_to_all | solution.py:396
  101.5 11.8 %copy-start.3 = (bf16[1536,384]{1,0:T(8,128)(2,1)S(1)}, bf16[1536,384]{1,0:T(8,128)(2,1)}, u32[]{:S(2)}) copy-start(bf16[1536,384]{1,0:T(8,128)(2,1)} %get-tuple-element.36) | copy-start | bytes 3538948
  107.6 11.5 %all-to-all-start.4 = ((bf16[8,24,512]{2,1,0:T(8,128)(2,1)}), bf16[8,24,512]{2,1,0:T(8,128)(2,1)S(1)}, u32[]{:S(2)}, u32[]{:S(2)}) async-start(bf16[8,24,512]{2,1,0:T(8,128)(2,1)} %fusion), calls=%async_computation.4 | async-start | bytes 393216 | tf_op jit(solution)/shard_map/all_to_all | solution.py:396
  113.3 10.5 %copy-start.2 = (bf16[256,4096]{1,0:T(8,128)(2,1)S(1)}, bf16[256,4096]{1,0:T(8,128)(2,1)}, u32[]{:S(2)}) copy-start(bf16[256,4096]{1,0:T(8,128)(2,1)} %convolution_convert_fusion) | copy-start | bytes 6291460
  119.1 22.4 %all-to-all-start.1 = ((bf16[64,24,384]{2,1,0:T(8,128)(2,1)}), bf16[64,24,384]{2,1,0:T(8,128)(2,1)S(1)}, u32[]{:S(2)}, u32[]{:S(2)}) async-start(bf16[64,24,384]{2,1,0:T(8,128)(2,1)} %bitcast.6), calls=%async_computation.1 | async-start | bytes 2359296 | tf_op jit(solution)/shard_map/all_to_all | solution.py:396
  123.9 59.5 %collective-permute-start.18 = (bf16[128,4096]{1,0:T(8,128)(2,1)S(1)}, bf16[128,4096]{1,0:T(8,128)(2,1)}, u32[]{:S(2)}, u32[]{:S(2)}) collective-permute-start(bf16[128,4096]{1,0:T(8,128)(2,1)S(1)} %pad_maximum_fusion.2), channel_id=1, source_target_pairs={{0,1},{1,0},{2,3},{3,2},{4,5},{5,4},{6,7},{7,6},{8,9},{9,8},{10,11... | collective-permute-start | bytes 3145736 | tf_op jit(solution)/shard_map/ppermute | solution.py:385
  142.8 42.2 %all-to-all-start.5 = ((bf16[64,24,512]{2,1,0:T(8,128)(2,1)}), bf16[64,24,512]{2,1,0:T(8,128)(2,1)}, u32[]{:S(2)}, u32[]{:S(2)}) async-start(bf16[64,24,512]{2,1,0:T(8,128)(2,1)} %broadcast_in_dim.28), calls=%async_computation.5 | async-start | bytes 3145728 | tf_op jit(solution)/shard_map/all_to_all | solution.py:396
  148.9 15.1 %copy-start.4 = (f32[8,384]{1,0:T(8,128)S(1)}, f32[8,384]{1,0:T(8,128)}, u32[]{:S(2)}) copy-start(f32[8,384]{1,0:T(8,128)} %get-tuple-element.31) | copy-start | bytes 36868
  164.9 3.3 %collective-permute-start.5 = (f32[64,384]{1,0:T(8,128)S(1)}, f32[64,384]{1,0:T(8,128)S(1)}, u32[]{:S(2)}, u32[]{:S(2)}) collective-permute-start(f32[64,384]{1,0:T(8,128)S(1)} %pad_maximum_fusion.4), channel_id=1, source_target_pairs={{0,1},{1,0},{2,3},{3,2},{4,5},{5,4},{6,7},{7,6},{8,9},{9,8},{10,11... | collective-permute-start | bytes 294920 | tf_op jit(solution)/shard_map/ppermute | solution.py:385
  169.1 4.2 %collective-permute-start.8 = (f32[64,384]{1,0:T(8,128)S(1)}, f32[64,384]{1,0:T(8,128)S(1)}, u32[]{:S(2)}, u32[]{:S(2)}) collective-permute-start(f32[64,384]{1,0:T(8,128)S(1)} %fusion.7), channel_id=1, source_target_pairs={{0,12},{4,0},{8,4},{12,8},{1,13},{5,1},{9,5},{13,9},{2,14},{6,2},{... | collective-permute-start | bytes 294920 | tf_op jit(solution)/shard_map/ppermute | solution.py:389
  171.6 5.1 %collective-permute-start.7 = (f32[64,384]{1,0:T(8,128)S(1)}, f32[64,384]{1,0:T(8,128)S(1)}, u32[]{:S(2)}, u32[]{:S(2)}) collective-permute-start(f32[64,384]{1,0:T(8,128)S(1)} %fusion.7), channel_id=1, source_target_pairs={{0,8},{4,12},{8,0},{12,4},{1,9},{5,13},{9,1},{13,5},{2,10},{6,14},... | collective-permute-start | bytes 294920 | tf_op jit(solution)/shard_map/ppermute | solution.py:389
  172.2 7.5 %collective-permute-start.6 = (f32[64,384]{1,0:T(8,128)S(1)}, f32[64,384]{1,0:T(8,128)S(1)}, u32[]{:S(2)}, u32[]{:S(2)}) collective-permute-start(f32[64,384]{1,0:T(8,128)S(1)} %fusion.7), channel_id=1, source_target_pairs={{0,4},{4,8},{8,12},{12,0},{1,5},{5,9},{9,13},{13,1},{2,6},{6,10},{... | collective-permute-start | bytes 294920 | tf_op jit(solution)/shard_map/ppermute | solution.py:389
  179.7 19.8 %collective-permute-start.11 = (f32[64,384]{1,0:T(8,128)S(1)}, f32[64,384]{1,0:T(8,128)S(1)}, u32[]{:S(2)}, u32[]{:S(2)}) collective-permute-start(f32[64,384]{1,0:T(8,128)S(1)} %add_add_fusion.1), channel_id=1, source_target_pairs={{0,48},{16,0},{32,16},{48,32},{1,49},{17,1},{33,17},{49,33},{2,50}... | collective-permute-start | bytes 294920 | tf_op jit(solution)/shard_map/ppermute | solution.py:389
  182.3 17.2 %collective-permute-start.10 = (f32[64,384]{1,0:T(8,128)S(1)}, f32[64,384]{1,0:T(8,128)}, u32[]{:S(2)}, u32[]{:S(2)}) collective-permute-start(f32[64,384]{1,0:T(8,128)S(1)} %add_add_fusion.1), channel_id=1, source_target_pairs={{0,32},{16,48},{32,0},{48,16},{1,33},{17,49},{33,1},{49,17},{2,34}... | collective-permute-start | bytes 294920 | tf_op jit(solution)/shard_map/ppermute | solution.py:389
  182.8 16.7 %collective-permute-start.9 = (f32[64,384]{1,0:T(8,128)S(1)}, f32[64,384]{1,0:T(8,128)}, u32[]{:S(2)}, u32[]{:S(2)}) collective-permute-start(f32[64,384]{1,0:T(8,128)S(1)} %add_add_fusion.1), channel_id=1, source_target_pairs={{0,16},{16,32},{32,48},{48,0},{1,17},{17,33},{33,49},{49,1},{2,18}... | collective-permute-start | bytes 294920 | tf_op jit(solution)/shard_map/ppermute | solution.py:389
  186.2 40.6 %all-to-all-start.2 = ((bf16[64,24,384]{2,1,0:T(8,128)(2,1)}), bf16[64,24,384]{2,1,0:T(8,128)(2,1)}, u32[]{:S(2)}, u32[]{:S(2)}) async-start(bf16[64,24,384]{2,1,0:T(8,128)(2,1)} %broadcast_in_dim.27), calls=%async_computation.2 | async-start | bytes 2359296 | tf_op jit(solution)/shard_map/all_to_all | solution.py:396
  194.3 33.7 %collective-permute-start.19 = (bf16[64,4096]{1,0:T(8,128)(2,1)S(1)}, bf16[64,4096]{1,0:T(8,128)(2,1)S(1)}, u32[]{:S(2)}, u32[]{:S(2)}) collective-permute-start(bf16[64,4096]{1,0:T(8,128)(2,1)S(1)} %fusion.1), channel_id=1, source_target_pairs={{0,2},{2,0},{1,3},{3,1},{4,6},{6,4},{5,7},{7,5},{8,10},{10,8},{9,1... | collective-permute-start | bytes 1572872 | tf_op jit(solution)/shard_map/ppermute | solution.py:385
  196.8 33.2 %collective-permute-start.17 = (bf16[64,24,512]{2,1,0:T(8,128)(2,1)}, bf16[64,24,512]{2,1,0:T(8,128)(2,1)}, u32[]{:S(2)}, u32[]{:S(2)}) collective-permute-start(bf16[64,24,512]{2,1,0:T(8,128)(2,1)} %all-to-all-done.5), channel_id=1, source_target_pairs={{0,1},{1,0},{2,3},{3,2},{4,5},{5,4},{6,7},{7,6},{8,9},{9,8},{10,11... | collective-permute-start | bytes 4718600 | tf_op jit(solution)/shard_map/ppermute | solution.py:385
  200.5 20.1 %collective-permute-start.14 = (f32[64,384]{1,0:T(8,128)S(1)}, f32[64,384]{1,0:T(8,128)S(1)}, u32[]{:S(2)}, u32[]{:S(2)}) collective-permute-start(f32[64,384]{1,0:T(8,128)S(1)} %add_add_fusion), channel_id=1, source_target_pairs={{0,66},{2,0},{64,2},{66,64},{1,67},{3,1},{65,3},{67,65},{4,70},{6,... | collective-permute-start | bytes 294920 | tf_op jit(solution)/shard_map/ppermute | solution.py:389
  201.5 19.1 %collective-permute-start.13 = (f32[64,384]{1,0:T(8,128)S(1)}, f32[64,384]{1,0:T(8,128)S(1)}, u32[]{:S(2)}, u32[]{:S(2)}) collective-permute-start(f32[64,384]{1,0:T(8,128)S(1)} %add_add_fusion), channel_id=1, source_target_pairs={{0,64},{2,66},{64,0},{66,2},{1,65},{3,67},{65,1},{67,3},{4,68},{6,... | collective-permute-start | bytes 294920 | tf_op jit(solution)/shard_map/ppermute | solution.py:389
  201.5 22.5 %collective-permute-start.12 = (f32[64,384]{1,0:T(8,128)S(1)}, f32[64,384]{1,0:T(8,128)}, u32[]{:S(2)}, u32[]{:S(2)}) collective-permute-start(f32[64,384]{1,0:T(8,128)S(1)} %add_add_fusion), channel_id=1, source_target_pairs={{0,2},{2,64},{64,66},{66,0},{1,3},{3,65},{65,67},{67,1},{4,6},{6,6... | collective-permute-start | bytes 294920 | tf_op jit(solution)/shard_map/ppermute | solution.py:389
  226.8 12.8 %collective-permute-start.16 = (bf16[1536,384]{1,0:T(8,128)(2,1)}, bf16[1536,384]{1,0:T(8,128)(2,1)}, u32[]{:S(2)}, u32[]{:S(2)}) collective-permute-start(bf16[1536,384]{1,0:T(8,128)(2,1)} %bitcast.7), channel_id=1, source_target_pairs={{0,1},{1,0},{2,3},{3,2},{4,5},{5,4},{6,7},{7,6},{8,9},{9,8},{10,11... | collective-permute-start | bytes 3538952 | tf_op jit(solution)/shard_map/ppermute | solution.py:385
  (3 other events, 18.2 us)

commit v2 on v1

v2 whole, which is shorter than its diff:
```python
import jax
import jax.numpy as jnp
import numpy as np
from jax import lax
from jax.experimental import pallas as pl
from jax.experimental.pallas import tpu as pltpu
from jax.sharding import Mesh, PartitionSpec as P

EPS = 1e-06
GELU_A = float(np.sqrt(2.0 / np.pi))
GELU_B = 0.044715
BF = jnp.bfloat16
F32 = jnp.float32
ALL = ("yl", "z", "x", "yh", "co")
ENC = ("yl", "z", "x")
BB = ("yh", "co")
SAME_CORE = ("yl", "z", "x", "yh")
PLANE = ("z", "x")
MIB = 1024 * 1024


def cost(us):
    return pl.CostEstimate(flops=int(us * 1.1e9) + 1, bytes_accessed=1, transcendentals=0)


def nn(a, b):
    return lax.dot_general(a, b, (((1,), (0,)), ((), ())), preferred_element_type=F32)


def nt(a, b):
    return lax.dot_general(a, b, (((1,), (1,)), ((), ())), preferred_element_type=F32)


def gelu_parts(u):
    u2 = u * u
    t = jnp.tanh(u * (GELU_A + (GELU_A * GELU_B) * u2))
    half = 0.5 * (1.0 + t)
    value = u * half
    slope = half + 0.5 * u * (1.0 - t * t) * (GELU_A + (3.0 * GELU_A * GELU_B) * u2)
    return value, slope


def vmem():
    return pl.BlockSpec(memory_space=pltpu.VMEM)


def smem():
    return pl.BlockSpec(memory_space=pltpu.SMEM)


def call(kernel, out_shape, scratch, in_specs, limit, us):
    multi = isinstance(out_shape, (list, tuple))
    return pl.pallas_call(
        kernel,
        out_shape=out_shape,
        in_specs=in_specs,
        out_specs=[vmem()] * len(out_shape) if multi else vmem(),
        scratch_shapes=scratch,
        compiler_params=pltpu.CompilerParams(vmem_limit_bytes=limit * MIB),
        cost_estimate=cost(us),
    )


def arrange_kernel(cot_ref, out_ref):
    r = lax.broadcasted_iota(jnp.int32, (512, 512), 0)
    s = lax.broadcasted_iota(jnp.int32, (512, 512), 1)
    want = ((r // 4) % 4) * 128 + (r // 16) * 4 + r % 4
    pick = jnp.where(s == want, 1.0, 0.0).astype(BF)
    out_ref[...] = nn(pick, cot_ref[...]).astype(BF)


def shifted(v):
    row = lax.broadcasted_iota(jnp.int32, (8, 128), 0)
    down = jnp.where(row == 0, 0.0, pltpu.roll(v, 1, 0))
    up = jnp.where(row == 7, 0.0, pltpu.roll(v, 7, 0))
    return down, v, up


def forward_kernel(
    x_ref, k_ref, gain_ref, win_ref, bias_ref, wout_ref, scale_ref, code_ref,
    pay_ref, normt_ref, xhat_ref, rstd_ref, slope_ref, hsum_ref, gsum_ref, bsum_ref, xp_ref,
    xf_ref, xs_ref, kb_ref, conv_ref, norm_ref, hs_ref,
):
    for lt in range(3):
        lanes = slice(lt * 128, lt * 128 + 128)
        for a in range(7):
            kb_ref[lt, a] = k_ref[a, :, lanes]
        for t in range(2):
            xf_ref[lt, t] = x_ref[t, :, :, lanes].astype(F32)

    def split(n, carry):
        lt = n // 2
        t = n % 2
        for jj in range(4):
            plain = []
            for i in range(16):
                v = xf_ref[lt, t, i, pl.ds(jj, 8, stride=4), :]
                plain.append(v)
                for s, w in enumerate(shifted(v)):
                    xs_ref[s, lt, t, jj, i] = w
            xp_ref[lt, t, jj] = jnp.concatenate(plain, axis=0).astype(BF)
        return carry

    lax.fori_loop(0, 6, split, 0)

    def conv(n, carry):
        lt = n // 8
        t = (n // 4) % 2
        jj = n % 4
        acc = [None] * 16
        for b in range(7):
            q = jj + (b + 1)
            s = q // 4
            jin = q % 4
            w = [
                jnp.broadcast_to(kb_ref[lt, a, pl.ds(b, 1), :], (8, 128)) for a in range(7)
            ]
            for r in range(16):
                v = xs_ref[s, lt, t, jin, r]
                for a in range(7):
                    i = r - a + 3
                    if 0 <= i < 16:
                        term = v * w[a]
                        acc[i] = term if acc[i] is None else acc[i] + term
        for i in range(16):
            conv_ref[lt, t, i // 4, jj, i % 4] = acc[i]
        return carry

    lax.fori_loop(0, 24, conv, 0)

    def block(n, carry):
        t = n // 4
        q = n % 4
        rows = pl.ds(pl.multiple_of(n * 128, 128), 128)
        c = [conv_ref[lt, t, q].reshape(128, 128) for lt in range(3)]
        mean = jnp.sum(c[0] + c[1] + c[2], axis=1, keepdims=True) * (1.0 / 384.0)
        c = [v - mean for v in c]
        var = jnp.sum(c[0] * c[0] + c[1] * c[1] + c[2] * c[2], axis=1, keepdims=True) * (
            1.0 / 384.0
        )
        rstd = lax.rsqrt(var + EPS)
        rstd_ref[rows, :] = jnp.broadcast_to(rstd, (128, 128))
        for lt in range(3):
            lanes = slice(lt * 128, lt * 128 + 128)
            xhat = c[lt] * rstd
            xhat_ref[lt, rows, :] = xhat
            normed = xhat * gain_ref[lanes].reshape(1, 128)
            norm_ref[:, lanes] = normed.astype(BF)
            normt_ref[n, lanes, :] = normed.T.astype(BF)
        toks = pl.ds(pl.multiple_of(n * 8, 8), 8)
        for h in range(6):
            hid = slice(h * 256, h * 256 + 256)
            u = nn(norm_ref[...], win_ref[:, hid]) + bias_ref[hid].reshape(1, 256)
            value, slope = gelu_parts(u)
            value = value.astype(BF).astype(F32)
            hs_ref[toks, hid] = jnp.sum(value.reshape(16, 8, 256), axis=0)
            gsum_ref[toks, hid] = jnp.sum(slope.reshape(16, 8, 256), axis=0)
            slope_ref[rows, hid] = slope.astype(BF)
        return carry

    lax.fori_loop(0, 8, block, 0)

    hs = hs_ref[...]
    hi = hs.astype(BF)
    hsum_ref[...] = hi
    lo = (hs - hi.astype(F32)).astype(BF)
    bsum = nn(hi, wout_ref[...]) + nn(lo, wout_ref[...])
    bsum_ref[...] = bsum
    for lt in range(3):
        lanes = slice(lt * 128, lt * 128 + 128)
        for t in range(2):
            for q in range(4):
                total = xs_ref[1, lt, t, 0, 4 * q]
                for jj in range(4):
                    for im in range(4):
                        if jj + im > 0:
                            total = total + xs_ref[1, lt, t, jj, 4 * q + im]
                tok = slice(t * 32 + q * 8, t * 32 + q * 8 + 8)
                hs_ref[tok, lanes] = total
        pooled = hs_ref[:, lanes] + scale_ref[lanes].reshape(1, 128) * bsum[:, lanes]
        pay_ref[:, lanes] = (pooled * (1.0 / 16.0)).astype(BF)
    pay_ref[:, 384:512] = code_ref[...]


def forward(x, k, gain, win, bias, wout, scale, code):
    shape = jax.ShapeDtypeStruct
    return call(
        forward_kernel,
        [
            shape((64, 512), BF),
            shape((8, 384, 128), BF),
            shape((3, 1024, 128), F32),
            shape((1024, 128), F32),
            shape((1024, 1536), BF),
            shape((64, 1536), BF),
            shape((64, 1536), F32),
            shape((64, 384), F32),
            shape((3, 2, 4, 128, 128), BF),
        ],
        [
            pltpu.VMEM((3, 2, 16, 32, 128), F32),
            pltpu.VMEM((3, 3, 2, 4, 16, 8, 128), F32),
            pltpu.VMEM((3, 7, 7, 128), F32),
            pltpu.VMEM((3, 2, 4, 4, 4, 8, 128), F32),
            pltpu.VMEM((128, 384), BF),
            pltpu.VMEM((64, 1536), F32),
        ],
        [vmem()] * 8,
        26,
        14,
    )(x, k, gain, win, bias, wout, scale, code)


def fold_kernel(proj_ref, conn_ref, out_ref, acc_ref):
    n = pl.program_id(0)

    @pl.when(n == 0)
    def _():
        acc_ref[...] = jnp.zeros_like(acc_ref)

    acc_ref[...] += nn(proj_ref[...], conn_ref[...])

    @pl.when(n == pl.num_programs(0) - 1)
    def _():
        out_ref[...] = acc_ref[...].astype(BF)


def fold(weight_proj, connector):
    return pl.pallas_call(
        fold_kernel,
        out_shape=jax.ShapeDtypeStruct((384, 896), BF),
        grid=(8,),
        in_specs=[
            pl.BlockSpec((384, 512), lambda n: (0, n)),
            pl.BlockSpec((512, 896), lambda n: (n, 0)),
        ],
        out_specs=pl.BlockSpec((384, 896), lambda n: (0, 0)),
        scratch_shapes=[pltpu.VMEM((384, 896), F32)],
        compiler_params=pltpu.CompilerParams(vmem_limit_bytes=12 * MIB),
        cost_estimate=cost(0),
    )(weight_proj, connector)


def rows_kernel(gp_ref, conn_ref, keep_ref, send_ref):
    out = nt(gp_ref[...], conn_ref[...]).astype(BF)
    keep_ref[...] = out[:128]
    send_ref[...] = out[128:]


def token_rows(grad_pre, connector):
    shape = jax.ShapeDtypeStruct((128, 4096), BF)
    return pl.pallas_call(
        rows_kernel,
        out_shape=[shape, shape],
        grid=(8,),
        in_specs=[
            pl.BlockSpec((256, 896), lambda n: (0, 0)),
            pl.BlockSpec((512, 896), lambda n: (n, 0)),
        ],
        out_specs=[pl.BlockSpec((128, 512), lambda n: (0, n))] * 2,
        compiler_params=pltpu.CompilerParams(vmem_limit_bytes=12 * MIB),
        cost_estimate=cost(5),
    )(grad_pre, connector)


def proj_kernel(at_ref, parts_ref, conn_ref, send_ref, keep_ref, sum_ref):
    n = pl.program_id(0)

    @pl.when(n == 0)
    def _():
        total = parts_ref[0].astype(F32)
        for m in range(1, 16):
            total = total + parts_ref[m].astype(F32)
        sum_ref[...] = total.astype(BF)

    out = nt(sum_ref[...], conn_ref[...])

    @pl.when(n < 4)
    def _():
        send_ref[0] = out.astype(BF)

    @pl.when(n >= 4)
    def _():
        keep_ref[0] = out


def proj_rows(at, parts, connector):
    def chunk(n, at):
        return (
            (at[0] ^ (1 - n // 4)) * 4 + (at[1] ^ (1 - (n % 4) // 2)) * 2 + (at[2] ^ (1 - n % 2)),
            0,
        )

    return pl.pallas_call(
        proj_kernel,
        out_shape=[
            jax.ShapeDtypeStruct((4, 24, 512), BF),
            jax.ShapeDtypeStruct((4, 24, 512), F32),
        ],
        grid_spec=pltpu.PrefetchScalarGridSpec(
            num_scalar_prefetch=1,
            grid=(8,),
            in_specs=[
                pl.BlockSpec((16, 24, 896), lambda n, at: (0, 0, 0)),
                pl.BlockSpec((512, 896), chunk),
            ],
            out_specs=[
                pl.BlockSpec((1, 24, 512), lambda n, at: (jnp.minimum(n, 3), 0, 0)),
                pl.BlockSpec((1, 24, 512), lambda n, at: (jnp.maximum(n - 4, 0), 0, 0)),
            ],
            scratch_shapes=[pltpu.VMEM((24, 896), BF)],
        ),
        compiler_params=pltpu.CompilerParams(vmem_limit_bytes=12 * MIB),
        cost_estimate=cost(4),
    )(at, parts, connector)


def connector_kernel(
    bb_ref, p0_ref, p1_ref, p2_ref, p3_ref, cot_ref, wc_ref,
    gp_ref, keep_ref, send_ref, s_ref, pick_ref, pool_ref,
):
    row = lax.broadcasted_iota(jnp.int32, (64, 128), 0)
    lane = lax.broadcasted_iota(jnp.int32, (64, 128), 1)
    for n, (d, p_ref) in enumerate(((0, p0_ref), (2, p1_ref), (1, p2_ref), (3, p3_ref))):
        tok = slice(n * 64, n * 64 + 64)
        pool_ref[tok, :] = p_ref[:, 0:384]
        code = p_ref[:, 384:512].astype(F32).astype(jnp.int32)
        src = bb_ref[0] ^ d
        want = (code >> 1) * 16 + src * 4 + (code & 1) * 2 + (row & 1)
        want = jnp.where(code < 0, -1, want)
        for q in range(4):
            pick_ref[tok, q * 128 : q * 128 + 128] = jnp.where(
                lane + q * 128 == want, 1.0, 0.0
            ).astype(BF)
    for h in range(7):
        cols = slice(h * 128, h * 128 + 128)
        cot = nn(pick_ref[...], cot_ref[:, cols])
        pre = nn(pool_ref[...], wc_ref[:, cols])
        gp_ref[:, cols] = (cot * gelu_parts(pre)[1]).astype(BF)
    tok = nt(gp_ref[...], wc_ref[...])
    keep_ref[...] = tok[:128]
    send_ref[...] = tok[128:]
    pool_t = pool_ref[...].astype(F32).T.astype(BF)
    s_ref[...] = nn(pool_t, gp_ref[...]).astype(BF)


def connector_part(bb, pays, cot, wc):
    shape = jax.ShapeDtypeStruct
    return call(
        connector_kernel,
        [
            shape((256, 896), BF),
            shape((128, 384), F32),
            shape((128, 384), F32),
            shape((384, 896), BF),
        ],
        [pltpu.VMEM((256, 512), BF), pltpu.VMEM((256, 384), BF)],
        [smem()] + [vmem()] * 6,
        12,
        3,
    )(bb, *pays, cot, wc)


def mlp_back_kernel(
    co_ref, near_ref, part_ref, far_ref, normt_ref, slope_ref, hsum_ref, gsum_ref, bsum_ref, wout_ref, scale_ref,
    keep_ref, send_ref, dpre_ref, small_ref, dh_ref,
):
    dtok = (part_ref[0:64, :] + near_ref[0:64, :] + far_ref[...]) * (1.0 / 16.0)
    small_ref[0:1, :] = jnp.sum(dtok * bsum_ref[...], axis=0, keepdims=True)
    dbr = (dtok * scale_ref[...].reshape(1, 384)).astype(BF)
    dh_ref[...] = nt(dbr, wout_ref[...])
    db = jnp.sum(dh_ref[...] * gsum_ref[...], axis=0, keepdims=True)
    for q in range(4):
        small_ref[1 + q : 2 + q, :] = db[:, q * 384 : q * 384 + 384]
    small_ref[5:8, :] = jnp.zeros((3, 384), F32)

    def block(n, carry):
        rows = pl.ds(pl.multiple_of(n * 128, 128), 128)
        toks = pl.ds(pl.multiple_of(n * 8, 8), 8)
        for h in range(4):
            hid = slice(h * 384, h * 384 + 384)
            g = slope_ref[rows, hid].astype(F32).reshape(16, 8, 384)
            d = g * dh_ref[toks, hid][None]
            dpre_ref[h, rows, :] = d.reshape(128, 384).astype(BF)
        return carry

    lax.fori_loop(0, 8, block, 0)
    hsum_t = hsum_ref[...].astype(F32).T.astype(BF)
    normt = jnp.concatenate([normt_ref[n] for n in range(8)], axis=1)
    mine = co_ref[0] == 0
    for h in range(2):
        def put(out_ref):
            for q in range(2):
                rows = slice(q * 384, q * 384 + 384)
                out_ref[rows, :] = nn(normt, dpre_ref[2 * h + q]).astype(out_ref.dtype)
            out_ref[768:1536, :] = nn(hsum_t[h * 768 : h * 768 + 768], dbr).astype(out_ref.dtype)

        here = mine if h == 0 else jnp.logical_not(mine)

        @pl.when(here)
        def _():
            put(keep_ref)

        @pl.when(jnp.logical_not(here))
        def _():
            put(send_ref)


def mlp_back(co, near, part, far, normt, slope, hsum, gsum, bsum, wout, scale):
    shape = jax.ShapeDtypeStruct
    return call(
        mlp_back_kernel,
        [
            shape((1536, 384), BF),
            shape((1536, 384), BF),
            shape((4, 1024, 384), BF),
            shape((8, 384), F32),
        ],
        [pltpu.VMEM((64, 1536), F32)],
        [smem()] + [vmem()] * 10,
        20,
        5,
    )(co, near, part, far, normt, slope, hsum, gsum, bsum, wout, scale)


def front_back_kernel(
    dpre_ref, win_ref, xhat_ref, rstd_ref, gain_ref, xp_ref, out_ref, dc_ref, dk_ref
):
    def block(n, carry):
        t = n // 4
        q = n % 4
        rows = pl.ds(pl.multiple_of(n * 128, 128), 128)
        dn = nt(dpre_ref[0, rows, :], win_ref[:, 0:384])
        for h in range(1, 4):
            dn = dn + nt(dpre_ref[h, rows, :], win_ref[:, h * 384 : h * 384 + 384])
        rstd = rstd_ref[rows, :]
        dx = []
        xh = []
        gains = []
        for lt in range(3):
            lanes = slice(lt * 128, lt * 128 + 128)
            xhat = xhat_ref[lt, rows, :]
            part = dn[:, lanes]
            gains.append(jnp.sum((part * xhat).reshape(16, 8, 128), axis=0))
            dx.append(part * gain_ref[lanes].reshape(1, 128))
            xh.append(xhat)
        m1 = jnp.sum(dx[0] + dx[1] + dx[2], axis=1, keepdims=True) * (1.0 / 384.0)
        m2 = jnp.sum(dx[0] * xh[0] + dx[1] * xh[1] + dx[2] * xh[2], axis=1, keepdims=True) * (
            1.0 / 384.0
        )
        for lt in range(3):
            dc = rstd * (dx[lt] - m1 - xh[lt] * m2)
            for jj in range(4):
                for im in range(4):
                    at = (jj * 4 + im) * 8
                    for s, w in enumerate(shifted(dc[at : at + 8])):
                        dc_ref[s, lt, t, jj, q * 4 + im] = w
        return tuple(c + g for c, g in zip(carry, gains))

    zero = jnp.zeros((8, 128), F32)
    gains = lax.fori_loop(0, 8, block, (zero, zero, zero))
    for lt in range(3):
        lanes = slice(lt * 128, lt * 128 + 128)
        out_ref[49:50, lanes] = jnp.sum(gains[lt], axis=0, keepdims=True)

    dk_ref[...] = jnp.zeros_like(dk_ref)

    def conv(n, carry):
        lt = n // 8
        t = (n // 4) % 2
        jj = n % 4
        x = xp_ref[lt, t, jj].astype(F32)
        x = [x[i * 8 : i * 8 + 8] for i in range(16)]
        for b in range(7):
            q = jj + (7 - b)
            s = q // 4
            jin = q % 4
            acc = [None] * 7
            for i in range(16):
                v = dc_ref[s, lt, t, jin, i]
                for a in range(7):
                    r = i + a - 3
                    if 0 <= r < 16:
                        term = v * x[r]
                        acc[a] = term if acc[a] is None else acc[a] + term
            for a in range(7):
                dk_ref[lt, a * 7 + b] += acc[a]
        return carry

    lax.fori_loop(0, 24, conv, 0)
    for lt in range(3):
        lanes = slice(lt * 128, lt * 128 + 128)
        out_ref[0:49, lanes] = jnp.sum(dk_ref[lt], axis=1)
    out_ref[50:56, :] = jnp.zeros((6, 384), F32)


def front_back(dpre, win, xhat, rstd, gain, xp):
    return call(
        front_back_kernel,
        jax.ShapeDtypeStruct((56, 384), F32),
        [pltpu.VMEM((3, 3, 2, 4, 16, 8, 128), F32), pltpu.VMEM((3, 49, 8, 128), F32)],
        [vmem()] * 6,
        20,
        10,
    )(dpre, win, xhat, rstd, gain, xp)


def three(v):
    return [v[:, q * 128 : q * 128 + 128] for q in range(3)]


def two_parts(v):
    high = v.astype(BF).astype(F32)
    return three(high) + three(v - high)


def pack_kernel(keep_ref, recv_ref, a_ref, b_ref, out_ref):
    pad = jnp.zeros((2, 128), F32)

    def one(n, small):
        rows = slice(n * 24, n * 24 + 24)
        pair = keep_ref[rows, :].astype(F32) + recv_ref[rows, :].astype(F32)
        out_ref[n] = jnp.concatenate(three(pair) + two_parts(small) + [pad], axis=0).astype(BF)

    for n in range(64):
        one(n, a_ref[n : n + 1, :] if n < 8 else b_ref[n - 8 : n - 7, :])


def pack(keep, recv, small_a, small_b):
    return call(
        pack_kernel, jax.ShapeDtypeStruct((64, 80, 128), BF), [], [vmem()] * 4, 12, 2
    )(keep, recv, small_a, small_b)


def settle_kernel(parts_ref, proj_ref, more_ref, out_ref):
    total = parts_ref[0].astype(F32)
    for n in range(1, 64):
        total = total + parts_ref[n].astype(F32)
    total = total * (1.0 / 128.0)
    small = total[72:75] + total[75:78]
    high = small.astype(BF).astype(F32)
    proj = (proj_ref[...] + more_ref[...].astype(F32)) * (1.0 / 128.0)
    shard = jnp.concatenate(
        [total[:72], high, small - high, total[78:80]]
        + [proj[:, q * 128 : q * 128 + 128] for q in range(4)],
        axis=0,
    ).astype(BF)
    for n in range(64):
        out_ref[n] = shard


def settle(parts, proj, more):
    return call(
        settle_kernel, jax.ShapeDtypeStruct((64, 176, 128), BF), [], [vmem()] * 3, 12, 2
    )(parts, proj, more)


def place_kernel(co_ref, mine_ref, other_ref, in_ref, out_ref, proj_ref, small_ref):
    def put(src_ref, half):
        def pair(low, high, at):
            return jnp.concatenate(
                [
                    src_ref[low, at : at + 24, :].astype(F32),
                    src_ref[high, at : at + 24, :].astype(F32),
                ],
                axis=0,
            ).astype(BF)

        for p in range(3):
            for m in range(8):
                rows = slice(m * 48, m * 48 + 48)
                for q in range(2):
                    n = q * 16 + 2 * m
                    col = half * 768 + q * 384 + p * 128
                    in_ref[rows, col : col + 128] = pair(n, n + 1, p * 24)
            for m in range(16):
                at = half * 768 + m * 48
                out_ref[at : at + 48, p * 128 : p * 128 + 128] = pair(
                    32 + 2 * m, 33 + 2 * m, p * 24
                )
        for yl in range(2):
            for yh in range(2):
                for p in range(4):
                    col = (half * 4 + yh * 2 + yl) * 512 + p * 128
                    for m in range(8):
                        n = yl * 32 + 4 * m + yh
                        proj_ref[m * 48 : m * 48 + 48, col : col + 128] = pair(
                            n, n + 2, 80 + p * 24
                        )

    low = co_ref[0] == 0

    @pl.when(low)
    def _():
        put(mine_ref, 0)
        put(other_ref, 1)

    @pl.when(jnp.logical_not(low))
    def _():
        put(other_ref, 0)
        put(mine_ref, 1)

    for n in range(64):
        small = mine_ref[n, 64:80, :].astype(F32) + other_ref[n, 64:80, :].astype(F32)
        small = small[8:11] + small[11:14]
        for p in range(3):
            small_ref[n : n + 1, p * 128 : p * 128 + 128] = small[p : p + 1]


def place(co, mine, other):
    shape = jax.ShapeDtypeStruct
    return call(
        place_kernel,
        [
            shape((384, 1536), BF),
            shape((1536, 384), BF),
            shape((384, 4096), BF),
            shape((64, 384), F32),
        ],
        [],
        [smem()] + [vmem()] * 2,
        26,
        5,
    )(co, mine, other)


def swap(v, axes, size, d):
    return lax.ppermute(v, axes, [(i, i ^ d) for i in range(size)])


def exchange(v, axes):
    return lax.all_to_all(v, axes, split_axis=0, concat_axis=0, tiled=True)


def on_device(
    image_tiles,
    depth_kernel,
    norm_gain,
    weight_in,
    bias_in,
    weight_out,
    layer_scale,
    weight_proj,
    image_counts,
    destination,
    row_offset,
    connector,
    cotangent,
):
    bb = lax.axis_index(BB).astype(jnp.int32)
    co = lax.axis_index("co").astype(jnp.int32)

    sent = call(arrange_kernel, jax.ShapeDtypeStruct((512, 896), BF), [], [vmem()], 8, 2)(cotangent)
    cot = exchange(sent.reshape(32, 16, 896), ENC).reshape(512, 896)
    image_tiles, sent = lax.optimization_barrier((image_tiles, sent))

    live = jnp.arange(32, dtype=jnp.int32) // 16 < image_counts[0]
    code = jnp.where(live, destination[0] * 2 + row_offset[0], -1).astype(BF)
    code = jnp.broadcast_to(jnp.repeat(code, 2)[:, None], (64, 128))
    pay, normt, xhat, rstd, slope, hsum, gsum, bsum, xp = forward(
        image_tiles,
        depth_kernel,
        norm_gain,
        weight_in,
        bias_in,
        weight_out,
        layer_scale,
        code,
    )
    pays = [pay] + [swap(pay, BB, 4, d) for d in (2, 1, 3)]
    wc = fold(lax.optimization_barrier((weight_proj, pay))[0], connector)
    grad_pre, part, give, outer = connector_part(bb.reshape(1), pays, cot, wc)

    near = swap(give, "co", 2, 1)
    tail, outer = lax.optimization_barrier((part[64:] + near[64:], outer))
    far = swap(tail, "yh", 2, 1)
    outer = exchange(outer.reshape(16, 24, 896), PLANE)

    keep, send, dpre, small_a = mlp_back(
        co.reshape(1), near, part, far, normt, slope, hsum, gsum, bsum, weight_out, layer_scale
    )
    keep, send, outer = lax.optimization_barrier((keep, send, outer))
    recv = swap(send, "co", 2, 1)
    at = jnp.stack([lax.axis_index(axis) for axis in ("co", "yh", "yl")]).astype(jnp.int32)
    give, own = proj_rows(at, outer, connector)
    own = own + swap(give, "co", 2, 1).astype(F32)
    own = own[2:] + swap(own[:2].astype(BF), "yh", 2, 1).astype(F32)
    own, more = own[1], swap(own[0].astype(BF), "yl", 2, 1)

    small_b = front_back(dpre, weight_in, xhat, rstd, norm_gain, xp)
    packed = pack(keep, recv, small_a, small_b)
    packed, own, more, grad_pre = lax.optimization_barrier((packed, own, more, grad_pre))
    shards = settle(exchange(packed, SAME_CORE), own, more)
    whole = exchange(shards, SAME_CORE)

    part, give = token_rows(grad_pre, connector)
    near = swap(give, "co", 2, 1).astype(F32)
    far = swap((part[64:].astype(F32) + near[64:]).astype(BF), "yh", 2, 1)
    token_grads = (part[:64].astype(F32) + near[:64] + far.astype(F32)).astype(BF)

    whole, token_grads = lax.optimization_barrier((whole, token_grads))
    grad_in, grad_out, grad_proj, small = place(co.reshape(1), whole, swap(whole, "co", 2, 1))

    return (
        small[8:57].reshape(7, 7, 384),
        small[57],
        grad_in,
        small[1:5].reshape(1536),
        grad_out,
        small[0],
        grad_proj,
        token_grads,
    )


def solution(mesh):
    fine = Mesh(mesh.devices.reshape(2, 4, 4, 2, 2), ALL)
    in_specs = (
        P(ALL, None, None, None),
        P(),
        P(),
        P(),
        P(),
        P(),
        P(),
        P(),
        P(ALL),
        P(ALL, None),
        P(ALL, None),
        P(None, BB),
        P(ENC, BB),
    )
    out_specs = (P(), P(), P(), P(), P(), P(), P(), P(ALL, None))
    return jax.shard_map(
        on_device, mesh=fine, in_specs=in_specs, out_specs=out_specs, check_vma=False
    )
```

time: 245 us -> 187 us (0.76)
  matrix products: 19.4 us -> 0 us
  other arithmetic: 21 us -> 2.68 us
  starting transfers between devices: 68.1 us -> 51.6 us
  waiting for transfers between devices: 64.7 us -> 56.5 us
  local copies, waits for them, and re-layouts: 19.3 us -> 22.1 us
    ppermute x11 -> x12, waiting for transfers between devices: 4.93 us -> 49 us  [swap(): return lax.ppermute(v, axes, [(i, i ^ d) for i in range(size)])]
    ppermute x9 -> x0, waiting for transfers between devices: 26.5 us -> none  [ring_sum(): lax.ppermute(v, axes, [(i, (i + d) % size) for i in range(size)])]
    all_to_all x6 -> x4, waiting for transfers between devices: 33.3 us -> 7.48 us  [exchange(): return lax.all_to_all(v, axes, split_axis=0, concat_axis=0, tiled=True)]
    unnamed x18 -> x78, local copies, waits for them, and re-layouts: 0.16 us -> 20 us
    dot_general x3 -> x0, matrix products: 19.4 us -> none  [the longest x1 6.77 us: nt(): lax.dot_general(a, b, (((1,), (1,)), ((), ())), preferred_element_type=F32)]
    pallas_call x1 -> x7, Pallas kernels: 3.9 us -> 21.9 us  [the longest x1 5.11 us: fold(): pl.pallas_call(fold_kernel, out_shape=jax.ShapeDtypeStruct((384, 896), BF...]
    ppermute x9 -> x0, starting transfers between devices: 11.3 us -> none  [ring_sum(): lax.ppermute(v, axes, [(i, (i + d) % size) for i in range(size)])]
    reshape x5 -> x0, local copies, waits for them, and re-layouts: 9.47 us -> none  [the longest x1 3.99 us: on_device(): grad_proj = both.reshape(384, 4096)]
  transfers between devices with their start and end apart: 26 -> 16, of which waited for: 12 -> 7; matrix products, arithmetic and copies ran while one was open for 18% -> 2% of each run, Pallas kernels for 7% -> 21%
where the time goes in v2:
time: 187 us; the launch traced here: 186 us
  waiting for transfers between devices  56.5 us (30%)
  starting transfers between devices  51.6 us (28%)
  Pallas kernels  51.1 us (27%)
  local copies, waits for them, and re-layouts  22.1 us (12%)
  other arithmetic  2.68 us (1%)
    ppermute x12, waiting for transfers between devices, swap(): return lax.ppermute(v, axes, [(i, i ^ d) for i in range(size)])  49 us
    all_to_all x4, starting transfers between devices, exchange(): return lax.all_to_all(v, axes, split_axis=0, concat_axis=0, tiled=True)  31.6 us
    ppermute x12, starting transfers between devices, swap(): return lax.ppermute(v, axes, [(i, i ^ d) for i in range(size)])  20 us
    unnamed x78, local copies, waits for them, and re-layouts  20 us
    pallas_call x1, Pallas kernels, forward(): call(forward_kernel, [shape((64, 512), BF), shape((8, 384, 128), BF), sha...  14 us
    pallas_call x1, Pallas kernels, front_back(): call(front_back_kernel, jax.ShapeDtypeStruct((56, 384), F32), [pltpu.VMEM...  10.2 us
    all_to_all x4, waiting for transfers between devices, exchange(): return lax.all_to_all(v, axes, split_axis=0, concat_axis=0, tiled=True)  7.48 us
    pallas_call x1, Pallas kernels, fold(): pl.pallas_call(fold_kernel, out_shape=jax.ShapeDtypeStruct((384, 896), BF...  5.11 us
  transfers between devices with their start and end apart: 16, of which 7 were waited for; matrix products, arithmetic and copies ran while one was open for 2% of the time, Pallas kernels for 21%

profile of v2, /device:TPU:1, one launch (start us, length us, event | category | flops | bytes accessed | tf_op | source)
XLA Modules:
  0.0 185.8 jit_solution(2471042770154319804)
XLA Ops:
  2.0 1.6 shard_map.188
  3.6 9.7 %all-to-all-start = ((bf16[32,16,896]{2,1,0:T(8,128)(2,1)}), bf16[32,16,896]{2,1,0:T(8,128)(2,1)S(1)}, u32[]{:S(2)}, u32[]{:S(2)}) async-start(bf16[32,16,896]{2,1,0:T(8,128)(2,1)} %bitcast.4), calls=%async_computation | async-start | bytes 1835008 | tf_op jit(solution)/shard_map/all_to_all | solution.py:632
  14.4 1.4 copy-done.7
  15.8 14.0 %shard_map.189 = (bf16[64,512]{1,0:T(8,128)(2,1)S(1)}, bf16[8,384,128]{2,1,0:T(8,128)(2,1)S(1)}, f32[3,1024,128]{2,1,0:T(8,128)S(1)}, f32[1024,128]{1,0:T(8,128)...) custom-call(bf16[2,16,32,384]{3,2,1,0:T(8,128)(2,1)S(1)} %copy-done., ...), custom_call_target="tpu_custom_call" | custom-call | flops 15400000512 | bytes 1 | tf_op jit(solution)/shard_map/pallas_call | solution.py:187
  29.8 3.5 %collective-permute-start.2 = (bf16[64,512]{1,0:T(8,128)(2,1)S(1)}, bf16[64,512]{1,0:T(8,128)(2,1)S(1)}, u32[]{:S(2)}, u32[]{:S(2)}) collective-permute-start(bf16[64,512]{1,0:T(8,128)(2,1)S(1)} %get-tuple-element.47.p0_ref), channel_id=1, source_target_pairs={{0,3},{1,2},{2,1},{3,0},{4,7},{5,6},{6,5},{7,4},{8,11},{9,10},{10,... | collective-permute-start | bytes 196616 | tf_op jit(solution)/shard_map/ppermute | solution.py:628
  33.8 5.1 %shard_map.190.wc_ref = bf16[384,896]{1,0:T(8,128)(2,1)S(1)} custom-call(bf16[384,4096]{1,0:T(8,128)(2,1)S(1)} %copy-done.2, bf16[4096,896]{1,0:T(8,128)(2,1)S(1)} %bitcast.16), custom_call_target="tpu_custom_call" | custom-call | flops 1 | bytes 1 | tf_op jit(solution)/shard_map/pallas_call | solution.py:229
  39.0 2.4 %shard_map.191 = (bf16[256,896]{1,0:T(8,128)(2,1)S(1)}, f32[128,384]{1,0:T(8,128)S(1)}, f32[128,384]{1,0:T(8,128)S(1)}, bf16[384,896]{1,0:T(8,128)(2,1)}) custom-call(s32[1]{0:T(128)} %bitcast.1.bb_ref, bf16[64,512]{1,0:T(8,128)(2,1)S(1)} %get-tuple-element.47.p0_ref, bf16[64,512]{1,0:T(8,128)(2,1)S(1)} %collective-permute-done.p1_ref, ...), custom_call_target="tpu_custom_call" | custom-call | flops 3300000000 | bytes 1 | tf_op jit(solution)/shard_map/pallas_call | solution.py:349
  44.0 6.8 %all-to-all-start.1 = ((bf16[16,24,896]{2,1,0:T(8,128)(2,1)}), bf16[16,24,896]{2,1,0:T(8,128)(2,1)S(1)}, u32[]{:S(2)}, u32[]{:S(2)}) async-start(bf16[16,24,896]{2,1,0:T(8,128)(2,1)} %bitcast.6), calls=%async_computation.1 | async-start | bytes 1376256 | tf_op jit(solution)/shard_map/all_to_all | solution.py:632
  50.9 2.7 %collective-permute-start.4 = (f32[64,384]{1,0:T(8,128)S(1)}, f32[64,384]{1,0:T(8,128)S(1)}, u32[]{:S(2)}, u32[]{:S(2)}) collective-permute-start(f32[64,384]{1,0:T(8,128)S(1)} %slice_add_fusion.3), channel_id=1, source_target_pairs={{0,2},{2,0},{1,3},{3,1},{4,6},{6,4},{5,7},{7,5},{8,10},{10,8},{9,1... | collective-permute-start | bytes 294920 | tf_op jit(solution)/shard_map/ppermute | solution.py:628
  53.6 2.3 %collective-permute-done.4.far_ref = f32[64,384]{1,0:T(8,128)S(1)} collective-permute-done((f32[64,384]{1,0:T(8,128)S(1)}, f32[64,384]{1,0:T(8,128)S(1)}, u32[]{:S(2)}, u32[]{:S(2)}) %collective-permute-start.4) | collective-permute-done | bytes 98336 | tf_op jit(solution)/shard_map/ppermute | solution.py:628
  55.9 1.9 %copy-done.20 = bf16[1024,1536]{1,0:T(8,128)(2,1)S(1)} copy-done((bf16[1024,1536]{1,0:T(8,128)(2,1)S(1)}, bf16[1024,1536]{1,0:T(8,128)(2,1)}, u32[]{:S(2)}) %copy-start.20) | copy-done | bytes 3145752
  59.9 3.4 %shard_map.192 = (bf16[1536,384]{1,0:T(8,128)(2,1)S(1)}, bf16[1536,384]{1,0:T(8,128)(2,1)S(1)}, bf16[4,1024,384]{2,1,0:T(8,128)(2,1)S(1)}, f32[8,384]{1,0:T(8,128)S(1)}) custom-call(s32[1]{0:T(128)} %bitcast.co_ref, f32[128,384]{1,0:T(8,128)S(1)} %collective-permute-done.3.near_ref, f32[128,384]{1,0:T(8,128)S(1)} %get-tuple-element.50.part_ref, ...), custom_call_target="tpu_custom_call" | custom-call | flops 5500000256 | bytes 1 | tf_op jit(solution)/shard_map/pallas_call | solution.py:411
  65.3 1.7 copy-done.21
  67.0 3.1 %copy-done = bf16[4096,896]{1,0:T(8,128)(2,1)S(1)} copy-done((bf16[4096,896]{1,0:T(8,128)(2,1)S(1)}, bf16[4096,896]{1,0:T(8,128)(2,1)}, u32[]{:S(2)}) %copy-start) | copy-done | bytes 7340056
  70.1 3.7 %shard_map.195 = (bf16[4,24,512]{2,1,0:T(8,128)(2,1)S(1)}, f32[4,24,512]{2,1,0:T(8,128)S(1)}) custom-call(s32[3]{0:T(128)S(1)} %pad_add_fusion.at_ref, bf16[16,24,896]{2,1,0:T(8,128)(2,1)S(1)} %all-to-all-done.1.parts_ref, bf16[4096,896]{1,0:T(8,128)(2,1)S(1)} %copy-done), custom_call_target="tpu_custom_call" | custom-call | flops 4400000000 | bytes 1 | tf_op jit(solution)/shard_map/pallas_call | solution.py:294
  73.8 2.0 %collective-permute-start.6 = (bf16[4,24,512]{2,1,0:T(8,128)(2,1)S(1)}, bf16[4,24,512]{2,1,0:T(8,128)(2,1)S(1)}, u32[]{:S(2)}, u32[]{:S(2)}) collective-permute-start(bf16[4,24,512]{2,1,0:T(8,128)(2,1)S(1)} %get-tuple-element.70), channel_id=1, source_target_pairs={{0,1},{1,0},{2,3},{3,2},{4,5},{5,4},{6,7},{7,6},{8,9},{9,8},{10,11... | collective-permute-start | bytes 294920 | tf_op jit(solution)/shard_map/ppermute | solution.py:628
  76.9 2.9 %collective-permute-start.7 = (bf16[2,24,512]{2,1,0:T(8,128)(2,1)S(1)}, bf16[2,24,512]{2,1,0:T(8,128)(2,1)S(1)}, u32[]{:S(2)}, u32[]{:S(2)}) collective-permute-start(bf16[2,24,512]{2,1,0:T(8,128)(2,1)S(1)} %slice.85), channel_id=1, source_target_pairs={{0,2},{2,0},{1,3},{3,1},{4,6},{6,4},{5,7},{7,5},{8,10},{10,8},{9,1... | collective-permute-start | bytes 147464 | tf_op jit(solution)/shard_map/ppermute | solution.py:628
  79.8 10.2 %shard_map.193.b_ref = f32[56,384]{1,0:T(8,128)S(1)} custom-call(bf16[4,1024,384]{2,1,0:T(8,128)(2,1)S(1)} %copy-done.22, bf16[384,1536]{1,0:T(8,128)(2,1)S(1)} %copy-done.8, f32[3,1024,128]{2,1,0:T(8,128)S(1)} %copy-done.30, f32[1024,128]{1,0:T(8,128)S(1)} %copy-done.34, f32[384]{0:T(512)S(1)} %copy-done.16, bf16[3,2,4,128,128]{4,3,2,1,0:T(8,128)(2,1)S(1)} %copy-done.32), custom_call_target="tpu_custom_call" | custom-call | flops 11000000512 | bytes 1 | tf_op jit(solution)/shard_map/pallas_call | solution.py:498
  90.8 1.6 shard_map.194
  92.8 8.7 %all-to-all-start.2 = ((bf16[64,80,128]{2,1,0:T(8,128)(2,1)}), bf16[64,80,128]{2,1,0:T(8,128)(2,1)S(1)}, u32[]{:S(2)}, u32[]{:S(2)}) async-start(bf16[64,80,128]{2,1,0:T(8,128)(2,1)} %shard_map.194), calls=%async_computation.2 | async-start | bytes 2621440 | tf_op jit(solution)/shard_map/all_to_all | solution.py:632
  101.5 3.1 %copy-done.1 = bf16[4096,896]{1,0:T(8,128)(2,1)S(1)} copy-done((bf16[4096,896]{1,0:T(8,128)(2,1)S(1)}, bf16[4096,896]{1,0:T(8,128)(2,1)}, u32[]{:S(2)}) %copy-start.1) | copy-done | bytes 7340056
  104.6 5.0 %shard_map.197 = (bf16[128,4096]{1,0:T(8,128)(2,1)S(1)}, bf16[128,4096]{1,0:T(8,128)(2,1)}) custom-call(bf16[256,896]{1,0:T(8,128)(2,1)S(1)} %copy-done.24, bf16[4096,896]{1,0:T(8,128)(2,1)S(1)} %copy-done.1), custom_call_target="tpu_custom_call" | custom-call | flops 5500000256 | bytes 1 | tf_op jit(solution)/shard_map/pallas_call | solution.py:252
  110.6 1.9 %collective-permute-start.9 = (bf16[128,4096]{1,0:T(8,128)(2,1)}, bf16[128,4096]{1,0:T(8,128)(2,1)}, u32[]{:S(2)}, u32[]{:S(2)}) collective-permute-start(bf16[128,4096]{1,0:T(8,128)(2,1)} %get-tuple-element.77), channel_id=1, source_target_pairs={{0,1},{1,0},{2,3},{3,2},{4,5},{5,4},{6,7},{7,6},{8,9},{9,8},{10,11... | collective-permute-start | bytes 3145736 | tf_op jit(solution)/shard_map/ppermute | solution.py:628
  112.4 7.5 %all-to-all-done.2.parts_ref = bf16[64,80,128]{2,1,0:T(8,128)(2,1)S(1)} async-done(((bf16[64,80,128]{2,1,0:T(8,128)(2,1)}), bf16[64,80,128]{2,1,0:T(8,128)(2,1)S(1)}, u32[]{:S(2)}, u32[]{:S(2)}) %all-to-all-start.2) | async-done | bytes 1310752 | tf_op jit(solution)/shard_map/all_to_all | solution.py:632
  120.3 1.6 copy-done.3
  121.8 6.3 %all-to-all-start.3 = ((bf16[64,176,128]{2,1,0:T(8,128)(2,1)}), bf16[64,176,128]{2,1,0:T(8,128)(2,1)S(1)}, u32[]{:S(2)}, u32[]{:S(2)}) async-start(bf16[64,176,128]{2,1,0:T(8,128)(2,1)} %copy-done.3), calls=%async_computation.3 | async-start | bytes 5767168 | tf_op jit(solution)/shard_map/all_to_all | solution.py:632
  128.2 1.5 convert_element_type.37
  129.8 2.6 %collective-permute-start.10 = (bf16[64,4096]{1,0:T(8,128)(2,1)S(1)}, bf16[64,4096]{1,0:T(8,128)(2,1)S(1)}, u32[]{:S(2)}, u32[]{:S(2)}) collective-permute-start(bf16[64,4096]{1,0:T(8,128)(2,1)S(1)} %fusion), channel_id=1, source_target_pairs={{0,2},{2,0},{1,3},{3,1},{4,6},{6,4},{5,7},{7,5},{8,10},{10,8},{9,1... | collective-permute-start | bytes 1572872 | tf_op jit(solution)/shard_map/ppermute | solution.py:628
  132.4 39.4 %collective-permute-done.10 = bf16[64,4096]{1,0:T(8,128)(2,1)S(1)} collective-permute-done((bf16[64,4096]{1,0:T(8,128)(2,1)S(1)}, bf16[64,4096]{1,0:T(8,128)(2,1)S(1)}, u32[]{:S(2)}, u32[]{:S(2)}) %collective-permute-start.10) | collective-permute-done | bytes 524320 | tf_op jit(solution)/shard_map/ppermute | solution.py:628
  172.7 2.5 %collective-permute-start.11 = (bf16[64,176,128]{2,1,0:T(8,128)(2,1)S(1)}, bf16[64,176,128]{2,1,0:T(8,128)(2,1)S(1)}, u32[]{:S(2)}, u32[]{:S(2)}) collective-permute-start(bf16[64,176,128]{2,1,0:T(8,128)(2,1)S(1)} %all-to-all-done.3.mine_ref), channel_id=1, source_target_pairs={{0,1},{1,0},{2,3},{3,2},{4,5},{5,4},{6,7},{7,6},{8,9},{9,8},{10,11... | collective-permute-start | bytes 8650760 | tf_op jit(solution)/shard_map/ppermute | solution.py:628
  175.2 4.9 %collective-permute-done.11.other_ref = bf16[64,176,128]{2,1,0:T(8,128)(2,1)S(1)} collective-permute-done((bf16[64,176,128]{2,1,0:T(8,128)(2,1)S(1)}, bf16[64,176,128]{2,1,0:T(8,128)(2,1)S(1)}, u32[]{:S(2)}, u32[]{:S(2)}) %collective-permute-start.11) | collective-permute-done | bytes 2883616 | tf_op jit(solution)/shard_map/ppermute | solution.py:628
  180.2 3.8 %shard_map.198 = (bf16[384,1536]{1,0:T(8,128)(2,1)}, bf16[1536,384]{1,0:T(8,128)(2,1)}, bf16[384,4096]{1,0:T(8,128)(2,1)}, f32[64,384]{1,0:T(8,128)S(1)}) custom-call(s32[1]{0:T(128)} %bitcast.co_ref, bf16[64,176,128]{2,1,0:T(8,128)(2,1)S(1)} %all-to-all-done.3.mine_ref, bf16[64,176,128]{2,1,0:T(8,128)(2,1)S(1)} %collective-permute-done.11.other_ref), custom_call_target="tpu_custom_call" | custom-call | flops 5500000256 | bytes 1 | tf_op jit(solution)/shard_map/pallas_call | solution.py:612
  (109 shorter events, 15.3 us)
Async XLA Ops:
  0.6 13.7 %copy-start.6 = (bf16[1536,384]{1,0:T(8,128)(2,1)S(1)}, bf16[1536,384]{1,0:T(8,128)(2,1)}, u32[]{:S(2)}) copy-start(bf16[1536,384]{1,0:T(8,128)(2,1)} %wout_ref.3) | copy-start | bytes 3538948
  1.9 12.1 %copy-start.35 = (s32[1,32]{1,0:T(1,128)S(1)}, s32[1,32]{1,0:T(1,128)}, u32[]{:S(2)}) copy-start(s32[1,32]{1,0:T(1,128)} %param.23) | copy-start | bytes 388
  1.9 12.1 %copy-start.36 = (s32[1,32]{1,0:T(1,128)S(1)}, s32[1,32]{1,0:T(1,128)}, u32[]{:S(2)}) copy-start(s32[1,32]{1,0:T(1,128)} %param.22) | copy-start | bytes 388
  1.9 12.4 %copy-start.12 = (bf16[2,16,32,384]{3,2,1,0:T(8,128)(2,1)S(1)}, bf16[2,16,32,384]{3,2,1,0:T(8,128)(2,1)}, u32[]{:S(2)}) copy-start(bf16[2,16,32,384]{3,2,1,0:T(8,128)(2,1)} %x_ref) | copy-start | bytes 2359300
  1.9 12.4 %copy-start.13 = (f32[7,7,384]{2,1,0:T(8,128)S(1)}, f32[7,7,384]{2,1,0:T(8,128)}, u32[]{:S(2)}) copy-start(f32[7,7,384]{2,1,0:T(8,128)} %k_ref.1) | copy-start | bytes 225796
  1.9 12.4 %copy-start.14 = (f32[1536]{0:T(1024)S(1)}, f32[1536]{0:T(1024)}, u32[]{:S(2)}) copy-start(f32[1536]{0:T(1024)} %bias_ref.1) | copy-start | bytes 18436
  1.9 12.4 %copy-start.15 = (f32[384]{0:T(512)S(1)}, f32[384]{0:T(512)}, u32[]{:S(2)}) copy-start(f32[384]{0:T(512)} %scale_ref.3) | copy-start | bytes 4612
  2.0 12.4 %copy-start.16 = (f32[384]{0:T(512)S(1)}, f32[384]{0:T(512)}, u32[]{:S(2)}) copy-start(f32[384]{0:T(512)} %gain_ref.3) | copy-start | bytes 4612
  3.6 35.4 %all-to-all-start = ((bf16[32,16,896]{2,1,0:T(8,128)(2,1)}), bf16[32,16,896]{2,1,0:T(8,128)(2,1)S(1)}, u32[]{:S(2)}, u32[]{:S(2)}) async-start(bf16[32,16,896]{2,1,0:T(8,128)(2,1)} %bitcast.4), calls=%async_computation | async-start | bytes 1835008 | tf_op jit(solution)/shard_map/all_to_all | solution.py:632
  14.2 19.5 %slice-start = ((s8[7340032]{0:T(1024)(128)(4,1)}), s8[4194304]{0:T(1024)(128)(4,1)S(1)}, s32[]{:S(2)}) async-start(s8[7340032]{0:T(1024)(128)(4,1)} %bitcast.15), calls=%async_computation.4 | async-start | bytes 8388608
  15.8 18.0 %slice-start.1 = ((s8[7340032]{0:T(1024)(128)(4,1)}), s8[3145728]{0:T(1024)(128)(4,1)S(1)}, s32[]{:S(2)}) async-start(s8[7340032]{0:T(1024)(128)(4,1)} %bitcast.15), calls=%async_computation.5 | async-start | bytes 6291456
  15.8 18.0 %copy-start.2 = (bf16[384,4096]{1,0:T(8,128)(2,1)S(1)}, bf16[384,4096]{1,0:T(8,128)(2,1)}, u32[]{:S(2)}) copy-start(bf16[384,4096]{1,0:T(8,128)(2,1)} %proj_ref) | copy-start | bytes 9437188
  29.8 9.1 %collective-permute-start.2 = (bf16[64,512]{1,0:T(8,128)(2,1)S(1)}, bf16[64,512]{1,0:T(8,128)(2,1)S(1)}, u32[]{:S(2)}, u32[]{:S(2)}) collective-permute-start(bf16[64,512]{1,0:T(8,128)(2,1)S(1)} %get-tuple-element.47.p0_ref), channel_id=1, source_target_pairs={{0,3},{1,2},{2,1},{3,0},{4,7},{5,6},{6,5},{7,4},{8,11},{9,10},{10,... | collective-permute-start | bytes 196616 | tf_op jit(solution)/shard_map/ppermute | solution.py:628
  33.4 5.6 %collective-permute-start.1 = (bf16[64,512]{1,0:T(8,128)(2,1)S(1)}, bf16[64,512]{1,0:T(8,128)(2,1)S(1)}, u32[]{:S(2)}, u32[]{:S(2)}) collective-permute-start(bf16[64,512]{1,0:T(8,128)(2,1)S(1)} %get-tuple-element.47.p0_ref), channel_id=1, source_target_pairs={{0,1},{1,0},{2,3},{3,2},{4,5},{5,4},{6,7},{7,6},{8,9},{9,8},{10,11... | collective-permute-start | bytes 196616 | tf_op jit(solution)/shard_map/ppermute | solution.py:628
  33.4 5.6 %collective-permute-start = (bf16[64,512]{1,0:T(8,128)(2,1)S(1)}, bf16[64,512]{1,0:T(8,128)(2,1)S(1)}, u32[]{:S(2)}, u32[]{:S(2)}) collective-permute-start(bf16[64,512]{1,0:T(8,128)(2,1)S(1)} %get-tuple-element.47.p0_ref), channel_id=1, source_target_pairs={{0,2},{1,3},{2,0},{3,1},{4,6},{5,7},{6,4},{7,5},{8,10},{9,11},{10,... | collective-permute-start | bytes 196616 | tf_op jit(solution)/shard_map/ppermute | solution.py:628
  42.1 1.9 %collective-permute-start.3 = (f32[128,384]{1,0:T(8,128)S(1)}, f32[128,384]{1,0:T(8,128)S(1)}, u32[]{:S(2)}, u32[]{:S(2)}) collective-permute-start(f32[128,384]{1,0:T(8,128)S(1)} %get-tuple-element.49), channel_id=1, source_target_pairs={{0,1},{1,0},{2,3},{3,2},{4,5},{5,4},{6,7},{7,6},{8,9},{9,8},{10,11... | collective-permute-start | bytes 589832 | tf_op jit(solution)/shard_map/ppermute | solution.py:628
  44.0 23.0 %all-to-all-start.1 = ((bf16[16,24,896]{2,1,0:T(8,128)(2,1)}), bf16[16,24,896]{2,1,0:T(8,128)(2,1)S(1)}, u32[]{:S(2)}, u32[]{:S(2)}) async-start(bf16[16,24,896]{2,1,0:T(8,128)(2,1)} %bitcast.6), calls=%async_computation.1 | async-start | bytes 1376256 | tf_op jit(solution)/shard_map/all_to_all | solution.py:632
  50.9 5.1 %collective-permute-start.4 = (f32[64,384]{1,0:T(8,128)S(1)}, f32[64,384]{1,0:T(8,128)S(1)}, u32[]{:S(2)}, u32[]{:S(2)}) collective-permute-start(f32[64,384]{1,0:T(8,128)S(1)} %slice_add_fusion.3), channel_id=1, source_target_pairs={{0,2},{2,0},{1,3},{3,1},{4,6},{6,4},{5,7},{7,5},{8,10},{10,8},{9,1... | collective-permute-start | bytes 294920 | tf_op jit(solution)/shard_map/ppermute | solution.py:628
  70.1 9.6 %copy-start.8 = (bf16[384,1536]{1,0:T(8,128)(2,1)S(1)}, bf16[384,1536]{1,0:T(8,128)(2,1)}, u32[]{:S(2)}) copy-start(bf16[384,1536]{1,0:T(8,128)(2,1)} %win_ref.3) | copy-start | bytes 3538948
  70.1 9.6 %copy-start.22 = (bf16[4,1024,384]{2,1,0:T(8,128)(2,1)S(1)}, bf16[4,1024,384]{2,1,0:T(8,128)(2,1)}, u32[]{:S(2)}) copy-start(bf16[4,1024,384]{2,1,0:T(8,128)(2,1)} %copy-done.21) | copy-start | bytes 9437188
  70.1 9.6 %copy-start.30 = (f32[3,1024,128]{2,1,0:T(8,128)S(1)}, f32[3,1024,128]{2,1,0:T(8,128)}, u32[]{:S(2)}) copy-start(f32[3,1024,128]{2,1,0:T(8,128)} %copy-done.29) | copy-start | bytes 4718596
  70.1 9.6 %copy-start.32 = (bf16[3,2,4,128,128]{4,3,2,1,0:T(8,128)(2,1)S(1)}, bf16[3,2,4,128,128]{4,3,2,1,0:T(8,128)(2,1)}, u32[]{:S(2)}) copy-start(bf16[3,2,4,128,128]{4,3,2,1,0:T(8,128)(2,1)} %copy-done.31) | copy-start | bytes 2359300
  73.8 3.0 %collective-permute-start.6 = (bf16[4,24,512]{2,1,0:T(8,128)(2,1)S(1)}, bf16[4,24,512]{2,1,0:T(8,128)(2,1)S(1)}, u32[]{:S(2)}, u32[]{:S(2)}) collective-permute-start(bf16[4,24,512]{2,1,0:T(8,128)(2,1)S(1)} %get-tuple-element.70), channel_id=1, source_target_pairs={{0,1},{1,0},{2,3},{3,2},{4,5},{5,4},{6,7},{7,6},{8,9},{9,8},{10,11... | collective-permute-start | bytes 294920 | tf_op jit(solution)/shard_map/ppermute | solution.py:628
  75.9 14.9 %collective-permute-start.5 = (bf16[1536,384]{1,0:T(8,128)(2,1)S(1)}, bf16[1536,384]{1,0:T(8,128)(2,1)S(1)}, u32[]{:S(2)}, u32[]{:S(2)}) collective-permute-start(bf16[1536,384]{1,0:T(8,128)(2,1)S(1)} %copy-done.10), channel_id=1, source_target_pairs={{0,1},{1,0},{2,3},{3,2},{4,5},{5,4},{6,7},{7,6},{8,9},{9,8},{10,11... | collective-permute-start | bytes 3538952 | tf_op jit(solution)/shard_map/ppermute | solution.py:628
  76.9 13.1 %collective-permute-start.7 = (bf16[2,24,512]{2,1,0:T(8,128)(2,1)S(1)}, bf16[2,24,512]{2,1,0:T(8,128)(2,1)S(1)}, u32[]{:S(2)}, u32[]{:S(2)}) collective-permute-start(bf16[2,24,512]{2,1,0:T(8,128)(2,1)S(1)} %slice.85), channel_id=1, source_target_pairs={{0,2},{2,0},{1,3},{3,1},{4,6},{6,4},{5,7},{7,5},{8,10},{10,8},{9,1... | collective-permute-start | bytes 147464 | tf_op jit(solution)/shard_map/ppermute | solution.py:628
  79.8 11.0 %copy-start.18 = (bf16[1536,384]{1,0:T(8,128)(2,1)S(1)}, bf16[1536,384]{1,0:T(8,128)(2,1)}, u32[]{:S(2)}) copy-start(bf16[1536,384]{1,0:T(8,128)(2,1)} %copy-done.17) | copy-start | bytes 3538948
  90.0 2.8 %collective-permute-start.8 = (bf16[24,512]{1,0:T(8,128)(2,1)S(1)}, bf16[24,512]{1,0:T(8,128)(2,1)S(1)}, u32[]{:S(2)}, u32[]{:S(2)}) collective-permute-start(bf16[24,512]{1,0:T(8,128)(2,1)S(1)} %fusion.3), channel_id=1, source_target_pairs={{0,64},{64,0},{1,65},{65,1},{2,66},{66,2},{3,67},{67,3},{4,68},{68... | collective-permute-start | bytes 73736 | tf_op jit(solution)/shard_map/ppermute | solution.py:628
  92.8 27.1 %all-to-all-start.2 = ((bf16[64,80,128]{2,1,0:T(8,128)(2,1)}), bf16[64,80,128]{2,1,0:T(8,128)(2,1)S(1)}, u32[]{:S(2)}, u32[]{:S(2)}) async-start(bf16[64,80,128]{2,1,0:T(8,128)(2,1)} %shard_map.194), calls=%async_computation.2 | async-start | bytes 2621440 | tf_op jit(solution)/shard_map/all_to_all | solution.py:632
  110.6 17.6 %collective-permute-start.9 = (bf16[128,4096]{1,0:T(8,128)(2,1)}, bf16[128,4096]{1,0:T(8,128)(2,1)}, u32[]{:S(2)}, u32[]{:S(2)}) collective-permute-start(bf16[128,4096]{1,0:T(8,128)(2,1)} %get-tuple-element.77), channel_id=1, source_target_pairs={{0,1},{1,0},{2,3},{3,2},{4,5},{5,4},{6,7},{7,6},{8,9},{9,8},{10,11... | collective-permute-start | bytes 3145736 | tf_op jit(solution)/shard_map/ppermute | solution.py:628
  121.8 50.9 %all-to-all-start.3 = ((bf16[64,176,128]{2,1,0:T(8,128)(2,1)}), bf16[64,176,128]{2,1,0:T(8,128)(2,1)S(1)}, u32[]{:S(2)}, u32[]{:S(2)}) async-start(bf16[64,176,128]{2,1,0:T(8,128)(2,1)} %copy-done.3), calls=%async_computation.3 | async-start | bytes 5767168 | tf_op jit(solution)/shard_map/all_to_all | solution.py:632
  129.8 42.0 %collective-permute-start.10 = (bf16[64,4096]{1,0:T(8,128)(2,1)S(1)}, bf16[64,4096]{1,0:T(8,128)(2,1)S(1)}, u32[]{:S(2)}, u32[]{:S(2)}) collective-permute-start(bf16[64,4096]{1,0:T(8,128)(2,1)S(1)} %fusion), channel_id=1, source_target_pairs={{0,2},{2,0},{1,3},{3,1},{4,6},{6,4},{5,7},{7,5},{8,10},{10,8},{9,1... | collective-permute-start | bytes 1572872 | tf_op jit(solution)/shard_map/ppermute | solution.py:628
  172.7 7.4 %collective-permute-start.11 = (bf16[64,176,128]{2,1,0:T(8,128)(2,1)S(1)}, bf16[64,176,128]{2,1,0:T(8,128)(2,1)S(1)}, u32[]{:S(2)}, u32[]{:S(2)}) collective-permute-start(bf16[64,176,128]{2,1,0:T(8,128)(2,1)S(1)} %all-to-all-done.3.mine_ref), channel_id=1, source_target_pairs={{0,1},{1,0},{2,3},{3,2},{4,5},{5,4},{6,7},{7,6},{8,9},{9,8},{10,11... | collective-permute-start | bytes 8650760 | tf_op jit(solution)/shard_map/ppermute | solution.py:628
  (23 other events, 100.6 us)

commit v3 on v2

--- a/solution.py
+++ b/solution.py
@@ -16,6 +16,7 @@
 BB = ("yh", "co")
 SAME_CORE = ("yl", "z", "x", "yh")
 PLANE = ("z", "x")
+COLS = ("yl", "yh", "co")
 MIB = 1024 * 1024
 
 
@@ -206,7 +207,7 @@
             pltpu.VMEM((64, 1536), F32),
         ],
         [vmem()] * 8,
-        26,
+        22,
         14,
     )(x, k, gain, win, bias, wout, scale, code)
 
@@ -236,7 +237,7 @@
         ],
         out_specs=pl.BlockSpec((384, 896), lambda n: (0, 0)),
         scratch_shapes=[pltpu.VMEM((384, 896), F32)],
-        compiler_params=pltpu.CompilerParams(vmem_limit_bytes=12 * MIB),
+        compiler_params=pltpu.CompilerParams(vmem_limit_bytes=8 * MIB),
         cost_estimate=cost(0),
     )(weight_proj, connector)
 
@@ -258,30 +259,20 @@
             pl.BlockSpec((512, 896), lambda n: (n, 0)),
         ],
         out_specs=[pl.BlockSpec((128, 512), lambda n: (0, n))] * 2,
-        compiler_params=pltpu.CompilerParams(vmem_limit_bytes=12 * MIB),
-        cost_estimate=cost(5),
+        compiler_params=pltpu.CompilerParams(vmem_limit_bytes=8 * MIB),
+        cost_estimate=cost(0),
     )(grad_pre, connector)
 
 
-def proj_kernel(at_ref, parts_ref, conn_ref, send_ref, keep_ref, sum_ref):
-    n = pl.program_id(0)
-
-    @pl.when(n == 0)
+def proj_kernel(at_ref, parts_ref, conn_ref, out_ref, sum_ref):
+    @pl.when(pl.program_id(0) == 0)
     def _():
         total = parts_ref[0].astype(F32)
         for m in range(1, 16):
             total = total + parts_ref[m].astype(F32)
         sum_ref[...] = total.astype(BF)
 
-    out = nt(sum_ref[...], conn_ref[...])
-
-    @pl.when(n < 4)
-    def _():
-        send_ref[0] = out.astype(BF)
-
-    @pl.when(n >= 4)
-    def _():
-        keep_ref[0] = out
+    out_ref[0] = nt(sum_ref[...], conn_ref[...]).astype(BF)
 
 
 def proj_rows(at, parts, connector):
@@ -293,10 +284,7 @@
 
     return pl.pallas_call(
         proj_kernel,
-        out_shape=[
-            jax.ShapeDtypeStruct((4, 24, 512), BF),
-            jax.ShapeDtypeStruct((4, 24, 512), F32),
-        ],
+        out_shape=jax.ShapeDtypeStruct((8, 24, 512), BF),
         grid_spec=pltpu.PrefetchScalarGridSpec(
             num_scalar_prefetch=1,
             grid=(8,),
@@ -304,14 +292,11 @@
                 pl.BlockSpec((16, 24, 896), lambda n, at: (0, 0, 0)),
                 pl.BlockSpec((512, 896), chunk),
             ],
-            out_specs=[
-                pl.BlockSpec((1, 24, 512), lambda n, at: (jnp.minimum(n, 3), 0, 0)),
-                pl.BlockSpec((1, 24, 512), lambda n, at: (jnp.maximum(n - 4, 0), 0, 0)),
-            ],
+            out_specs=pl.BlockSpec((1, 24, 512), lambda n, at: (n, 0, 0)),
             scratch_shapes=[pltpu.VMEM((24, 896), BF)],
         ),
-        compiler_params=pltpu.CompilerParams(vmem_limit_bytes=12 * MIB),
-        cost_estimate=cost(4),
+        compiler_params=pltpu.CompilerParams(vmem_limit_bytes=8 * MIB),
+        cost_estimate=cost(0),
     )(at, parts, connector)
 
 
@@ -356,7 +341,7 @@
         ],
         [pltpu.VMEM((256, 512), BF), pltpu.VMEM((256, 384), BF)],
         [smem()] + [vmem()] * 6,
-        12,
+        6,
         3,
     )(bb, *pays, cot, wc)
 
@@ -418,7 +403,7 @@
         ],
         [pltpu.VMEM((64, 1536), F32)],
         [smem()] + [vmem()] * 10,
-        20,
+        14,
         5,
     )(co, near, part, far, normt, slope, hsum, gsum, bsum, wout, scale)
 
@@ -500,7 +485,7 @@
         jax.ShapeDtypeStruct((56, 384), F32),
         [pltpu.VMEM((3, 3, 2, 4, 16, 8, 128), F32), pltpu.VMEM((3, 49, 8, 128), F32)],
         [vmem()] * 6,
-        20,
+        15,
         10,
     )(dpre, win, xhat, rstd, gain, xp)
 
@@ -528,18 +513,22 @@
 
 def pack(keep, recv, small_a, small_b):
     return call(
-        pack_kernel, jax.ShapeDtypeStruct((64, 80, 128), BF), [], [vmem()] * 4, 12, 2
+        pack_kernel, jax.ShapeDtypeStruct((64, 80, 128), BF), [], [vmem()] * 4, 6, 2
     )(keep, recv, small_a, small_b)
 
 
-def settle_kernel(parts_ref, proj_ref, more_ref, out_ref):
+def settle_kernel(parts_ref, *refs):
+    proj_refs, out_ref = refs[:8], refs[8]
     total = parts_ref[0].astype(F32)
     for n in range(1, 64):
         total = total + parts_ref[n].astype(F32)
     total = total * (1.0 / 128.0)
     small = total[72:75] + total[75:78]
     high = small.astype(BF).astype(F32)
-    proj = (proj_ref[...] + more_ref[...].astype(F32)) * (1.0 / 128.0)
+    proj = proj_refs[0][...].astype(F32)
+    for ref in proj_refs[1:]:
+        proj = proj + ref[...].astype(F32)
+    proj = proj * (1.0 / 128.0)
     shard = jnp.concatenate(
         [total[:72], high, small - high, total[78:80]]
         + [proj[:, q * 128 : q * 128 + 128] for q in range(4)],
@@ -549,13 +538,16 @@
         out_ref[n] = shard
 
 
-def settle(parts, proj, more):
+def settle(parts, proj):
     return call(
-        settle_kernel, jax.ShapeDtypeStruct((64, 176, 128), BF), [], [vmem()] * 3, 12, 2
-    )(parts, proj, more)
-
-
-def place_kernel(co_ref, mine_ref, other_ref, in_ref, out_ref, proj_ref, small_ref):
+        settle_kernel, jax.ShapeDtypeStruct((64, 176, 128), BF), [], [vmem()] * 9, 6, 2
+    )(parts, *proj)
+
+
+def place_kernel(
+    co_ref, mine_ref, other_ref,
+    in_ref, out_ref, proj_ref, kernel_ref, gain_ref, bias_ref, scale_ref,
+):
     def put(src_ref, half):
         def pair(low, high, at):
             return jnp.concatenate(
@@ -600,11 +592,21 @@
         put(other_ref, 0)
         put(mine_ref, 1)
 
-    for n in range(64):
+    for n in range(58):
         small = mine_ref[n, 64:80, :].astype(F32) + other_ref[n, 64:80, :].astype(F32)
         small = small[8:11] + small[11:14]
         for p in range(3):
-            small_ref[n : n + 1, p * 128 : p * 128 + 128] = small[p : p + 1]
+            lanes = slice(p * 128, p * 128 + 128)
+            row = small[p : p + 1]
+            if n == 0:
+                scale_ref[lanes] = row.reshape(128)
+            elif n < 5:
+                bias_ref[(n - 1) * 384 + p * 128 : (n - 1) * 384 + p * 128 + 128] = row.reshape(128)
+            elif n == 57:
+                gain_ref[lanes] = row.reshape(128)
+            elif n >= 8:
+                a, b = (n - 8) // 7, (n - 8) % 7
+                kernel_ref[a, b : b + 1, lanes] = row
 
 
 def place(co, mine, other):
@@ -615,11 +617,14 @@
             shape((384, 1536), BF),
             shape((1536, 384), BF),
             shape((384, 4096), BF),
-            shape((64, 384), F32),
+            shape((7, 7, 384), F32),
+            shape((384,), F32),
+            shape((1536,), F32),
+            shape((384,), F32),
         ],
         [],
         [smem()] + [vmem()] * 2,
-        26,
+        14,
         5,
     )(co, mine, other)
 
@@ -647,12 +652,13 @@
     connector,
     cotangent,
 ):
-    bb = lax.axis_index(BB).astype(jnp.int32)
-    co = lax.axis_index("co").astype(jnp.int32)
-
-    sent = call(arrange_kernel, jax.ShapeDtypeStruct((512, 896), BF), [], [vmem()], 8, 2)(cotangent)
+    at = jnp.stack([lax.axis_index(axis) for axis in ("co", "yh", "yl")]).astype(jnp.int32)
+    bb = lax.axis_index(BB).astype(jnp.int32).reshape(1)
+    sent = call(
+        arrange_kernel, jax.ShapeDtypeStruct((512, 896), BF), [], [vmem()], 4, 2
+    )(cotangent)
     cot = exchange(sent.reshape(32, 16, 896), ENC).reshape(512, 896)
-    image_tiles, sent = lax.optimization_barrier((image_tiles, sent))
+    image_tiles, sent, at, bb = lax.optimization_barrier((image_tiles, sent, at, bb))
 
     live = jnp.arange(32, dtype=jnp.int32) // 16 < image_counts[0]
     code = jnp.where(live, destination[0] * 2 + row_offset[0], -1).astype(BF)
@@ -669,45 +675,49 @@
     )
     pays = [pay] + [swap(pay, BB, 4, d) for d in (2, 1, 3)]
     wc = fold(lax.optimization_barrier((weight_proj, pay))[0], connector)
-    grad_pre, part, give, outer = connector_part(bb.reshape(1), pays, cot, wc)
+    grad_pre, part, give, outer = connector_part(bb, pays, cot, wc)
 
     near = swap(give, "co", 2, 1)
-    tail, outer = lax.optimization_barrier((part[64:] + near[64:], outer))
-    far = swap(tail, "yh", 2, 1)
+    far = swap(part[64:] + near[64:], "yh", 2, 1)
     outer = exchange(outer.reshape(16, 24, 896), PLANE)
-
+    row_part, row_give = token_rows(grad_pre, connector)
+    near, far, outer, row_part, row_give = lax.optimization_barrier(
+        (near, far, outer, row_part, row_give)
+    )
+
+    row_near = swap(row_give, "co", 2, 1).astype(F32)
+    row_far = swap((row_part[64:].astype(F32) + row_near[64:]).astype(BF), "yh", 2, 1)
     keep, send, dpre, small_a = mlp_back(
-        co.reshape(1), near, part, far, normt, slope, hsum, gsum, bsum, weight_out, layer_scale
+        at, near, part, far, normt, slope, hsum, gsum, bsum, weight_out, layer_scale
     )
-    keep, send, outer = lax.optimization_barrier((keep, send, outer))
     recv = swap(send, "co", 2, 1)
-    at = jnp.stack([lax.axis_index(axis) for axis in ("co", "yh", "yl")]).astype(jnp.int32)
-    give, own = proj_rows(at, outer, connector)
-    own = own + swap(give, "co", 2, 1).astype(F32)
-    own = own[2:] + swap(own[:2].astype(BF), "yh", 2, 1).astype(F32)
-    own, more = own[1], swap(own[0].astype(BF), "yl", 2, 1)
-
     small_b = front_back(dpre, weight_in, xhat, rstd, norm_gain, xp)
+    small_b, row_far = lax.optimization_barrier((small_b, row_far))
     packed = pack(keep, recv, small_a, small_b)
-    packed, own, more, grad_pre = lax.optimization_barrier((packed, own, more, grad_pre))
-    shards = settle(exchange(packed, SAME_CORE), own, more)
+    parts = exchange(packed, SAME_CORE)
+    packed, outer = lax.optimization_barrier((packed, outer))
+
+    proj = proj_rows(at, outer, connector)
+    proj = [proj[7]] + [
+        swap(proj[n], COLS, 8, (1 - n % 2) * 4 + (1 - (n % 4) // 2) * 2 + (1 - n // 4))
+        for n in range(7)
+    ]
+    shards = settle(parts, proj)
     whole = exchange(shards, SAME_CORE)
 
-    part, give = token_rows(grad_pre, connector)
-    near = swap(give, "co", 2, 1).astype(F32)
-    far = swap((part[64:].astype(F32) + near[64:]).astype(BF), "yh", 2, 1)
-    token_grads = (part[:64].astype(F32) + near[:64] + far.astype(F32)).astype(BF)
-
+    token_grads = (row_part[:64].astype(F32) + row_near[:64] + row_far.astype(F32)).astype(BF)
     whole, token_grads = lax.optimization_barrier((whole, token_grads))
-    grad_in, grad_out, grad_proj, small = place(co.reshape(1), whole, swap(whole, "co", 2, 1))
+    grad_in, grad_out, grad_proj, grad_kernel, grad_gain, grad_bias, grad_scale = place(
+        at, whole, swap(whole, "co", 2, 1)
+    )
 
     return (
-        small[8:57].reshape(7, 7, 384),
-        small[57],
+        grad_kernel,
+        grad_gain,
         grad_in,
-        small[1:5].reshape(1536),
+        grad_bias,
         grad_out,
-        small[0],
+        grad_scale,
         grad_proj,
         token_grads,
     )

time: 187 us -> 179 us (0.957)
  waiting for transfers between devices: 56.5 us -> 44.8 us
  starting transfers between devices: 51.6 us -> 60.9 us
  local copies, waits for them, and re-layouts: 22.1 us -> 16.1 us
    ppermute x12 -> x16, waiting for transfers between devices: 49 us -> 11.2 us  [swap(): return lax.ppermute(v, axes, [(i, i ^ d) for i in range(size)])]
    all_to_all x4, waiting for transfers between devices: 7.48 us -> 33.6 us  [exchange(): return lax.all_to_all(v, axes, split_axis=0, concat_axis=0, tiled=True)]
    ppermute x12 -> x16, starting transfers between devices: 20 us -> 25.3 us  [swap(): return lax.ppermute(v, axes, [(i, i ^ d) for i in range(size)])]
    unnamed x78 -> x70, local copies, waits for them, and re-layouts: 20 us -> 15.8 us
    all_to_all x4, starting transfers between devices: 31.6 us -> 35.6 us  [exchange(): return lax.all_to_all(v, axes, split_axis=0, concat_axis=0, tiled=True)]
  transfers between devices with their start and end apart: 16 -> 20, of which waited for: 7 -> 6; matrix products, arithmetic and copies ran while one was open for 2% -> 2% of each run, Pallas kernels for 21% -> 23%
where the time goes in v3:
time: 179 us; the launch traced here: 177 us
  starting transfers between devices  60.9 us (34%)
  Pallas kernels  51.2 us (29%)
  waiting for transfers between devices  44.8 us (25%)
  local copies, waits for them, and re-layouts  16.1 us (9%)
  other arithmetic  2.74 us (2%)
    all_to_all x4, starting transfers between devices, exchange(): return lax.all_to_all(v, axes, split_axis=0, concat_axis=0, tiled=True)  35.6 us
    all_to_all x4, waiting for transfers between devices, exchange(): return lax.all_to_all(v, axes, split_axis=0, concat_axis=0, tiled=True)  33.6 us
    ppermute x16, starting transfers between devices, swap(): return lax.ppermute(v, axes, [(i, i ^ d) for i in range(size)])  25.3 us
    unnamed x70, local copies, waits for them, and re-layouts  15.8 us
    pallas_call x1, Pallas kernels, forward(): call(forward_kernel, [shape((64, 512), BF), shape((8, 384, 128), BF), sha...  14 us
    ppermute x16, waiting for transfers between devices, swap(): return lax.ppermute(v, axes, [(i, i ^ d) for i in range(size)])  11.2 us
    pallas_call x1, Pallas kernels, front_back(): call(front_back_kernel, jax.ShapeDtypeStruct((56, 384), F32), [pltpu.VMEM...  10.2 us
    pallas_call x1, Pallas kernels, fold(): pl.pallas_call(fold_kernel, out_shape=jax.ShapeDtypeStruct((384, 896), BF...  5.11 us
  transfers between devices with their start and end apart: 20, of which 6 were waited for; matrix products, arithmetic and copies ran while one was open for 2% of the time, Pallas kernels for 23%

profile of v3, /device:TPU:1, one launch (start us, length us, event | category | flops | bytes accessed | tf_op | source)
XLA Modules:
  0.0 177.5 jit_solution(16741912776895208958)
XLA Ops:
  2.0 1.7 shard_map.188
  3.6 9.7 %all-to-all-start = ((bf16[32,16,896]{2,1,0:T(8,128)(2,1)}), bf16[32,16,896]{2,1,0:T(8,128)(2,1)S(1)}, u32[]{:S(2)}, u32[]{:S(2)}) async-start(bf16[32,16,896]{2,1,0:T(8,128)(2,1)} %bitcast.6), calls=%async_computation | async-start | bytes 1835008 | tf_op jit(solution)/shard_map/all_to_all | solution.py:637
  14.5 1.4 copy-done.7
  15.9 14.0 %shard_map.189 = (bf16[64,512]{1,0:T(8,128)(2,1)S(1)}, bf16[8,384,128]{2,1,0:T(8,128)(2,1)S(1)}, f32[3,1024,128]{2,1,0:T(8,128)S(1)}, f32[1024,128]{1,0:T(8,128)...) custom-call(bf16[2,16,32,384]{3,2,1,0:T(8,128)(2,1)S(1)} %copy-done., ...), custom_call_target="tpu_custom_call" | custom-call | flops 15400000512 | bytes 1 | tf_op jit(solution)/shard_map/pallas_call | solution.py:188
  29.9 3.5 %collective-permute-start.2 = (bf16[64,512]{1,0:T(8,128)(2,1)S(1)}, bf16[64,512]{1,0:T(8,128)(2,1)S(1)}, u32[]{:S(2)}, u32[]{:S(2)}) collective-permute-start(bf16[64,512]{1,0:T(8,128)(2,1)S(1)} %get-tuple-element.51.p0_ref), channel_id=1, source_target_pairs={{0,3},{1,2},{2,1},{3,0},{4,7},{5,6},{6,5},{7,4},{8,11},{9,10},{10,... | collective-permute-start | bytes 196616 | tf_op jit(solution)/shard_map/ppermute | solution.py:633
  33.8 5.1 %shard_map.190.wc_ref = bf16[384,896]{1,0:T(8,128)(2,1)S(1)} custom-call(bf16[384,4096]{1,0:T(8,128)(2,1)S(1)} %copy-done.2, bf16[4096,896]{1,0:T(8,128)(2,1)S(1)} %bitcast.28), custom_call_target="tpu_custom_call" | custom-call | flops 1 | bytes 1 | tf_op jit(solution)/shard_map/pallas_call | solution.py:230
  39.1 2.5 %shard_map.191 = (bf16[256,896]{1,0:T(8,128)(2,1)S(1)}, f32[128,384]{1,0:T(8,128)S(1)}, f32[128,384]{1,0:T(8,128)S(1)}, bf16[384,896]{1,0:T(8,128)(2,1)}) custom-call(s32[1]{0:T(128)} %bitcast.3.bb_ref, bf16[64,512]{1,0:T(8,128)(2,1)S(1)} %get-tuple-element.51.p0_ref, bf16[64,512]{1,0:T(8,128)(2,1)S(1)} %collective-permute-done.p1_ref, ...), custom_call_target="tpu_custom_call" | custom-call | flops 3300000000 | bytes 1 | tf_op jit(solution)/shard_map/pallas_call | solution.py:334
  41.5 6.8 %all-to-all-start.1 = ((bf16[16,24,896]{2,1,0:T(8,128)(2,1)}), bf16[16,24,896]{2,1,0:T(8,128)(2,1)S(1)}, u32[]{:S(2)}, u32[]{:S(2)}) async-start(bf16[16,24,896]{2,1,0:T(8,128)(2,1)} %bitcast.8), calls=%async_computation.1 | async-start | bytes 1376256 | tf_op jit(solution)/shard_map/all_to_all | solution.py:637
  50.6 2.7 %collective-permute-start.4 = (f32[64,384]{1,0:T(8,128)S(1)}, f32[64,384]{1,0:T(8,128)S(1)}, u32[]{:S(2)}, u32[]{:S(2)}) collective-permute-start(f32[64,384]{1,0:T(8,128)S(1)} %slice_add_fusion.2), channel_id=1, source_target_pairs={{0,2},{2,0},{1,3},{3,1},{4,6},{6,4},{5,7},{7,5},{8,10},{10,8},{9,1... | collective-permute-start | bytes 294920 | tf_op jit(solution)/shard_map/ppermute | solution.py:633
  53.3 3.1 %copy-done = bf16[4096,896]{1,0:T(8,128)(2,1)S(1)} copy-done((bf16[4096,896]{1,0:T(8,128)(2,1)S(1)}, bf16[4096,896]{1,0:T(8,128)(2,1)}, u32[]{:S(2)}) %copy-start) | copy-done | bytes 7340056
  56.4 3.9 %shard_map.192 = (bf16[128,4096]{1,0:T(8,128)(2,1)S(1)}, bf16[128,4096]{1,0:T(8,128)(2,1)S(1)}) custom-call(bf16[256,896]{1,0:T(8,128)(2,1)S(1)} %get-tuple-element.56.gp_ref, bf16[4096,896]{1,0:T(8,128)(2,1)S(1)} %copy-done), custom_call_target="tpu_custom_call" | custom-call | flops 1 | bytes 1 | tf_op jit(solution)/shard_map/pallas_call | solution.py:253
  63.9 1.9 %copy-done.17 = bf16[1024,1536]{1,0:T(8,128)(2,1)S(1)} copy-done((bf16[1024,1536]{1,0:T(8,128)(2,1)S(1)}, bf16[1024,1536]{1,0:T(8,128)(2,1)}, u32[]{:S(2)}) %copy-start.17) | copy-done | bytes 3145752
  66.9 3.9 %shard_map.193 = (bf16[1536,384]{1,0:T(8,128)(2,1)S(1)}, bf16[1536,384]{1,0:T(8,128)(2,1)S(1)}, bf16[4,1024,384]{2,1,0:T(8,128)(2,1)S(1)}, f32[8,384]{1,0:T(8,128)S(1)}) custom-call(s32[3]{0:T(128)S(1)} %pad_add_fusion.co_ref.at_ref, f32[128,384]{1,0:T(8,128)S(1)} %collective-permute-done.3.near_ref, f32[128,384]{1,0:T(8,128)S(1)} %get-tuple-element.54.part_ref, ...), custom_call_target="tpu_custom_call" | custom-call | flops 5500000256 | bytes 1 | tf_op jit(solution)/shard_map/pallas_call | solution.py:396
  71.5 2.9 %collective-permute-start.7 = (bf16[64,4096]{1,0:T(8,128)(2,1)S(1)}, bf16[64,4096]{1,0:T(8,128)(2,1)S(1)}, u32[]{:S(2)}, u32[]{:S(2)}) collective-permute-start(bf16[64,4096]{1,0:T(8,128)(2,1)S(1)} %fusion.2), channel_id=1, source_target_pairs={{0,2},{2,0},{1,3},{3,1},{4,6},{6,4},{5,7},{7,5},{8,10},{10,8},{9,1... | collective-permute-start | bytes 1572872 | tf_op jit(solution)/shard_map/ppermute | solution.py:633
  74.4 10.2 %shard_map.194.b_ref = f32[56,384]{1,0:T(8,128)S(1)} custom-call(bf16[4,1024,384]{2,1,0:T(8,128)(2,1)S(1)} %get-tuple-element.69.dpre_ref, bf16[384,1536]{1,0:T(8,128)(2,1)S(1)} %copy-done.8, f32[3,1024,128]{2,1,0:T(8,128)S(1)} %copy-done.21, f32[1024,128]{1,0:T(8,128)S(1)} %copy-done.27, f32[384]{0:T(512)S(1)} %copy-done.15, ...), custom_call_target="tpu_custom_call" | custom-call | flops 11000000512 | bytes 1 | tf_op jit(solution)/shard_map/pallas_call | solution.py:483
  84.6 1.8 %collective-permute-done.7 = bf16[64,4096]{1,0:T(8,128)(2,1)S(1)} collective-permute-done((bf16[64,4096]{1,0:T(8,128)(2,1)S(1)}, bf16[64,4096]{1,0:T(8,128)(2,1)S(1)}, u32[]{:S(2)}, u32[]{:S(2)}) %collective-permute-start.7) | collective-permute-done | bytes 524320 | tf_op jit(solution)/shard_map/ppermute | solution.py:633
  86.4 1.5 shard_map.195
  88.0 8.6 %all-to-all-start.2 = ((bf16[64,80,128]{2,1,0:T(8,128)(2,1)}), bf16[64,80,128]{2,1,0:T(8,128)(2,1)S(1)}, u32[]{:S(2)}, u32[]{:S(2)}) async-start(bf16[64,80,128]{2,1,0:T(8,128)(2,1)} %shard_map.195), calls=%async_computation.2 | async-start | bytes 2621440 | tf_op jit(solution)/shard_map/all_to_all | solution.py:637
  96.5 3.1 %copy-done.1 = bf16[4096,896]{1,0:T(8,128)(2,1)S(1)} copy-done((bf16[4096,896]{1,0:T(8,128)(2,1)S(1)}, bf16[4096,896]{1,0:T(8,128)(2,1)}, u32[]{:S(2)}) %copy-start.1) | copy-done | bytes 7340056
  99.6 3.7 %shard_map.196 = bf16[8,24,512]{2,1,0:T(8,128)(2,1)S(1)} custom-call(s32[3]{0:T(128)S(1)} %pad_add_fusion.co_ref.at_ref, bf16[16,24,896]{2,1,0:T(8,128)(2,1)S(1)} %all-to-all-done.1.parts_ref, bf16[4096,896]{1,0:T(8,128)(2,1)S(1)} %copy-done.1), custom_call_target="tpu_custom_call" | custom-call | flops 1 | bytes 1 | tf_op jit(solution)/shard_map/pallas_call | solution.py:285
  104.6 2.4 %collective-permute-start.13 = (bf16[24,512]{1,0:T(8,128)(2,1)S(1)}, bf16[24,512]{1,0:T(8,128)(2,1)S(1)}, u32[]{:S(2)}, u32[]{:S(2)}) collective-permute-start(bf16[24,512]{1,0:T(8,128)(2,1)S(1)} %get-tuple-element.89), channel_id=1, source_target_pairs={{0,2},{1,3},{2,0},{3,1},{64,66},{65,67},{66,64},{67,65},{4,6},{5,7... | collective-permute-start | bytes 73736 | tf_op jit(solution)/shard_map/ppermute | solution.py:633
  107.3 1.9 %collective-permute-start.11 = (bf16[24,512]{1,0:T(8,128)(2,1)S(1)}, bf16[24,512]{1,0:T(8,128)(2,1)S(1)}, u32[]{:S(2)}, u32[]{:S(2)}) collective-permute-start(bf16[24,512]{1,0:T(8,128)(2,1)S(1)} %get-tuple-element.91), channel_id=1, source_target_pairs={{0,1},{1,0},{2,3},{3,2},{64,65},{65,64},{66,67},{67,66},{4,5},{5,4... | collective-permute-start | bytes 73736 | tf_op jit(solution)/shard_map/ppermute | solution.py:633
  109.3 4.0 %collective-permute-start.9 = (bf16[24,512]{1,0:T(8,128)(2,1)S(1)}, bf16[24,512]{1,0:T(8,128)(2,1)S(1)}, u32[]{:S(2)}, u32[]{:S(2)}) collective-permute-start(bf16[24,512]{1,0:T(8,128)(2,1)S(1)} %get-tuple-element.93), channel_id=1, source_target_pairs={{0,3},{1,2},{2,1},{3,0},{64,67},{65,66},{66,65},{67,64},{4,7},{5,6... | collective-permute-start | bytes 73736 | tf_op jit(solution)/shard_map/ppermute | solution.py:633
  113.3 1.4 collective-permute-start.8
  114.7 2.3 %collective-permute-done.9.refs_2_ = bf16[24,512]{1,0:T(8,128)(2,1)S(1)} collective-permute-done((bf16[24,512]{1,0:T(8,128)(2,1)S(1)}, bf16[24,512]{1,0:T(8,128)(2,1)S(1)}, u32[]{:S(2)}, u32[]{:S(2)}) %collective-permute-start.9) | collective-permute-done | bytes 24608 | tf_op jit(solution)/shard_map/ppermute | solution.py:633
  118.5 1.6 copy-done.3
  120.0 10.5 %all-to-all-start.3 = ((bf16[64,176,128]{2,1,0:T(8,128)(2,1)}), bf16[64,176,128]{2,1,0:T(8,128)(2,1)S(1)}, u32[]{:S(2)}, u32[]{:S(2)}) async-start(bf16[64,176,128]{2,1,0:T(8,128)(2,1)} %copy-done.3), calls=%async_computation.3 | async-start | bytes 5767168 | tf_op jit(solution)/shard_map/all_to_all | solution.py:637
  130.6 2.3 %fusion.1 = bf16[64,4096]{1,0:T(8,128)(2,1)} fusion(f32[128,4096]{1,0:T(8,128)} %copy-done.28, bf16[64,4096]{1,0:T(8,128)(2,1)S(1)} %copy-done.30, bf16[128,4096]{1,0:T(8,128)(2,1)} %copy-done.4), kind=kLoop, calls=%fused_computation.2 | loop fusion | flops 1310720 | bytes 2621440 | tf_op jit(solution)/shard_map/convert_element_type | solution.py:708
  132.9 33.6 %all-to-all-done.3.mine_ref = bf16[64,176,128]{2,1,0:T(8,128)(2,1)S(1)} async-done(((bf16[64,176,128]{2,1,0:T(8,128)(2,1)}), bf16[64,176,128]{2,1,0:T(8,128)(2,1)S(1)}, u32[]{:S(2)}, u32[]{:S(2)}) %all-to-all-start.3) | async-done | bytes 2883616 | tf_op jit(solution)/shard_map/all_to_all | solution.py:637
  166.4 1.8 %collective-permute-start.15 = (bf16[64,176,128]{2,1,0:T(8,128)(2,1)S(1)}, bf16[64,176,128]{2,1,0:T(8,128)(2,1)S(1)}, u32[]{:S(2)}, u32[]{:S(2)}) collective-permute-start(bf16[64,176,128]{2,1,0:T(8,128)(2,1)S(1)} %all-to-all-done.3.mine_ref), channel_id=1, source_target_pairs={{0,1},{1,0},{2,3},{3,2},{4,5},{5,4},{6,7},{7,6},{8,9},{9,8},{10,11... | collective-permute-start | bytes 8650760 | tf_op jit(solution)/shard_map/ppermute | solution.py:633
  168.2 4.9 %collective-permute-done.15.other_ref = bf16[64,176,128]{2,1,0:T(8,128)(2,1)S(1)} collective-permute-done((bf16[64,176,128]{2,1,0:T(8,128)(2,1)S(1)}, bf16[64,176,128]{2,1,0:T(8,128)(2,1)S(1)}, u32[]{:S(2)}, u32[]{:S(2)}) %collective-permute-start.15) | collective-permute-done | bytes 2883616 | tf_op jit(solution)/shard_map/ppermute | solution.py:633
  173.1 4.3 %shard_map.198 = (bf16[384,1536]{1,0:T(8,128)(2,1)}, bf16[1536,384]{1,0:T(8,128)(2,1)}, bf16[384,4096]{1,0:T(8,128)(2,1)}, f32[7,7,384]{2,1,0:T(8,128)}, f32[384]{0:T(512)}, /*index=5*/f32[1536]{0:T(1024)}, f32[384]{0:T(512)}) custom-call(s32[3]{0:T(128)S(1)} %pad_add_fusion.co_ref.at_ref, bf16[64,176,128]{2,1,0:T(8,128)(2,1)S(1)} %all-to-all-done.3.mine_ref, ...), custom_call_target="tpu_custom_call" | custom-call | flops 5500000256 | bytes 1 | tf_op jit(solution)/shard_map/pallas_call | solution.py:614
  (100 shorter events, 12.7 us)
Async XLA Ops:
  0.6 13.8 %copy-start.5 = (bf16[1536,384]{1,0:T(8,128)(2,1)S(1)}, bf16[1536,384]{1,0:T(8,128)(2,1)}, u32[]{:S(2)}) copy-start(bf16[1536,384]{1,0:T(8,128)(2,1)} %wout_ref.3) | copy-start | bytes 3538948
  1.9 12.1 %copy-start.31 = (s32[1,32]{1,0:T(1,128)S(1)}, s32[1,32]{1,0:T(1,128)}, u32[]{:S(2)}) copy-start(s32[1,32]{1,0:T(1,128)} %param.23) | copy-start | bytes 388
  1.9 12.1 %copy-start.32 = (s32[1,32]{1,0:T(1,128)S(1)}, s32[1,32]{1,0:T(1,128)}, u32[]{:S(2)}) copy-start(s32[1,32]{1,0:T(1,128)} %param.22) | copy-start | bytes 388
  1.9 12.5 %copy-start.11 = (bf16[2,16,32,384]{3,2,1,0:T(8,128)(2,1)S(1)}, bf16[2,16,32,384]{3,2,1,0:T(8,128)(2,1)}, u32[]{:S(2)}) copy-start(bf16[2,16,32,384]{3,2,1,0:T(8,128)(2,1)} %x_ref) | copy-start | bytes 2359300
  1.9 12.5 %copy-start.12 = (f32[7,7,384]{2,1,0:T(8,128)S(1)}, f32[7,7,384]{2,1,0:T(8,128)}, u32[]{:S(2)}) copy-start(f32[7,7,384]{2,1,0:T(8,128)} %k_ref.1) | copy-start | bytes 225796
  1.9 12.5 %copy-start.13 = (f32[1536]{0:T(1024)S(1)}, f32[1536]{0:T(1024)}, u32[]{:S(2)}) copy-start(f32[1536]{0:T(1024)} %bias_ref.1) | copy-start | bytes 18436
  1.9 12.5 %copy-start.14 = (f32[384]{0:T(512)S(1)}, f32[384]{0:T(512)}, u32[]{:S(2)}) copy-start(f32[384]{0:T(512)} %scale_ref.3) | copy-start | bytes 4612
  2.0 12.5 %copy-start.15 = (f32[384]{0:T(512)S(1)}, f32[384]{0:T(512)}, u32[]{:S(2)}) copy-start(f32[384]{0:T(512)} %gain_ref.3) | copy-start | bytes 4612
  3.6 35.4 %all-to-all-start = ((bf16[32,16,896]{2,1,0:T(8,128)(2,1)}), bf16[32,16,896]{2,1,0:T(8,128)(2,1)S(1)}, u32[]{:S(2)}, u32[]{:S(2)}) async-start(bf16[32,16,896]{2,1,0:T(8,128)(2,1)} %bitcast.6), calls=%async_computation | async-start | bytes 1835008 | tf_op jit(solution)/shard_map/all_to_all | solution.py:637
  14.3 19.5 %slice-start = ((s8[7340032]{0:T(1024)(128)(4,1)}), s8[4194304]{0:T(1024)(128)(4,1)S(1)}, s32[]{:S(2)}) async-start(s8[7340032]{0:T(1024)(128)(4,1)} %bitcast.27), calls=%async_computation.4 | async-start | bytes 8388608
  15.9 18.0 %slice-start.1 = ((s8[7340032]{0:T(1024)(128)(4,1)}), s8[3145728]{0:T(1024)(128)(4,1)S(1)}, s32[]{:S(2)}) async-start(s8[7340032]{0:T(1024)(128)(4,1)} %bitcast.27), calls=%async_computation.5 | async-start | bytes 6291456
  15.9 18.0 %copy-start.2 = (bf16[384,4096]{1,0:T(8,128)(2,1)S(1)}, bf16[384,4096]{1,0:T(8,128)(2,1)}, u32[]{:S(2)}) copy-start(bf16[384,4096]{1,0:T(8,128)(2,1)} %proj_ref) | copy-start | bytes 9437188
  29.9 9.1 %collective-permute-start.2 = (bf16[64,512]{1,0:T(8,128)(2,1)S(1)}, bf16[64,512]{1,0:T(8,128)(2,1)S(1)}, u32[]{:S(2)}, u32[]{:S(2)}) collective-permute-start(bf16[64,512]{1,0:T(8,128)(2,1)S(1)} %get-tuple-element.51.p0_ref), channel_id=1, source_target_pairs={{0,3},{1,2},{2,1},{3,0},{4,7},{5,6},{6,5},{7,4},{8,11},{9,10},{10,... | collective-permute-start | bytes 196616 | tf_op jit(solution)/shard_map/ppermute | solution.py:633
  33.5 5.6 %collective-permute-start.1 = (bf16[64,512]{1,0:T(8,128)(2,1)S(1)}, bf16[64,512]{1,0:T(8,128)(2,1)S(1)}, u32[]{:S(2)}, u32[]{:S(2)}) collective-permute-start(bf16[64,512]{1,0:T(8,128)(2,1)S(1)} %get-tuple-element.51.p0_ref), channel_id=1, source_target_pairs={{0,1},{1,0},{2,3},{3,2},{4,5},{5,4},{6,7},{7,6},{8,9},{9,8},{10,11... | collective-permute-start | bytes 196616 | tf_op jit(solution)/shard_map/ppermute | solution.py:633
  33.5 5.6 %collective-permute-start = (bf16[64,512]{1,0:T(8,128)(2,1)S(1)}, bf16[64,512]{1,0:T(8,128)(2,1)S(1)}, u32[]{:S(2)}, u32[]{:S(2)}) collective-permute-start(bf16[64,512]{1,0:T(8,128)(2,1)S(1)} %get-tuple-element.51.p0_ref), channel_id=1, source_target_pairs={{0,2},{1,3},{2,0},{3,1},{4,6},{5,7},{6,4},{7,5},{8,10},{9,11},{10,... | collective-permute-start | bytes 196616 | tf_op jit(solution)/shard_map/ppermute | solution.py:633
  41.5 19.8 %all-to-all-start.1 = ((bf16[16,24,896]{2,1,0:T(8,128)(2,1)}), bf16[16,24,896]{2,1,0:T(8,128)(2,1)S(1)}, u32[]{:S(2)}, u32[]{:S(2)}) async-start(bf16[16,24,896]{2,1,0:T(8,128)(2,1)} %bitcast.8), calls=%async_computation.1 | async-start | bytes 1376256 | tf_op jit(solution)/shard_map/all_to_all | solution.py:637
  48.3 2.2 %collective-permute-start.3 = (f32[128,384]{1,0:T(8,128)S(1)}, f32[128,384]{1,0:T(8,128)S(1)}, u32[]{:S(2)}, u32[]{:S(2)}) collective-permute-start(f32[128,384]{1,0:T(8,128)S(1)} %get-tuple-element.53), channel_id=1, source_target_pairs={{0,1},{1,0},{2,3},{3,2},{4,5},{5,4},{6,7},{7,6},{8,9},{9,8},{10,11... | collective-permute-start | bytes 589832 | tf_op jit(solution)/shard_map/ppermute | solution.py:633
  50.6 10.7 %collective-permute-start.4 = (f32[64,384]{1,0:T(8,128)S(1)}, f32[64,384]{1,0:T(8,128)S(1)}, u32[]{:S(2)}, u32[]{:S(2)}) collective-permute-start(f32[64,384]{1,0:T(8,128)S(1)} %slice_add_fusion.2), channel_id=1, source_target_pairs={{0,2},{2,0},{1,3},{3,1},{4,6},{6,4},{5,7},{7,5},{8,10},{10,8},{9,1... | collective-permute-start | bytes 294920 | tf_op jit(solution)/shard_map/ppermute | solution.py:633
  61.3 9.8 %collective-permute-start.6 = (bf16[128,4096]{1,0:T(8,128)(2,1)}, bf16[128,4096]{1,0:T(8,128)(2,1)S(1)}, u32[]{:S(2)}, u32[]{:S(2)}) collective-permute-start(bf16[128,4096]{1,0:T(8,128)(2,1)} %copy-done.9), channel_id=1, source_target_pairs={{0,1},{1,0},{2,3},{3,2},{4,5},{5,4},{6,7},{7,6},{8,9},{9,8},{10,11... | collective-permute-start | bytes 3145736 | tf_op jit(solution)/shard_map/ppermute | solution.py:633
  70.8 15.6 %collective-permute-start.5 = (bf16[1536,384]{1,0:T(8,128)(2,1)S(1)}, bf16[1536,384]{1,0:T(8,128)(2,1)S(1)}, u32[]{:S(2)}, u32[]{:S(2)}) collective-permute-start(bf16[1536,384]{1,0:T(8,128)(2,1)S(1)} %get-tuple-element.67), channel_id=1, source_target_pairs={{0,1},{1,0},{2,3},{3,2},{4,5},{5,4},{6,7},{7,6},{8,9},{9,8},{10,11... | collective-permute-start | bytes 3538952 | tf_op jit(solution)/shard_map/ppermute | solution.py:633
  71.3 13.2 %copy-start.28 = (f32[128,4096]{1,0:T(8,128)}, f32[128,4096]{1,0:T(8,128)S(1)}, u32[]{:S(2)}) copy-start(f32[128,4096]{1,0:T(8,128)S(1)} %convert_element_type.23) | copy-start | bytes 6291460
  71.5 15.0 %collective-permute-start.7 = (bf16[64,4096]{1,0:T(8,128)(2,1)S(1)}, bf16[64,4096]{1,0:T(8,128)(2,1)S(1)}, u32[]{:S(2)}, u32[]{:S(2)}) collective-permute-start(bf16[64,4096]{1,0:T(8,128)(2,1)S(1)} %fusion.2), channel_id=1, source_target_pairs={{0,2},{2,0},{1,3},{3,1},{4,6},{6,4},{5,7},{7,5},{8,10},{10,8},{9,1... | collective-permute-start | bytes 1572872 | tf_op jit(solution)/shard_map/ppermute | solution.py:633
  88.0 30.1 %all-to-all-start.2 = ((bf16[64,80,128]{2,1,0:T(8,128)(2,1)}), bf16[64,80,128]{2,1,0:T(8,128)(2,1)S(1)}, u32[]{:S(2)}, u32[]{:S(2)}) async-start(bf16[64,80,128]{2,1,0:T(8,128)(2,1)} %shard_map.195), calls=%async_computation.2 | async-start | bytes 2621440 | tf_op jit(solution)/shard_map/all_to_all | solution.py:637
  103.4 6.0 %collective-permute-start.14 = (bf16[24,512]{1,0:T(8,128)(2,1)S(1)}, bf16[24,512]{1,0:T(8,128)(2,1)S(1)}, u32[]{:S(2)}, u32[]{:S(2)}) collective-permute-start(bf16[24,512]{1,0:T(8,128)(2,1)S(1)} %get-tuple-element.88), channel_id=1, source_target_pairs={{0,64},{1,65},{2,66},{3,67},{64,0},{65,1},{66,2},{67,3},{4,68},{5,... | collective-permute-start | bytes 73736 | tf_op jit(solution)/shard_map/ppermute | solution.py:633
  104.6 8.8 %collective-permute-start.13 = (bf16[24,512]{1,0:T(8,128)(2,1)S(1)}, bf16[24,512]{1,0:T(8,128)(2,1)S(1)}, u32[]{:S(2)}, u32[]{:S(2)}) collective-permute-start(bf16[24,512]{1,0:T(8,128)(2,1)S(1)} %get-tuple-element.89), channel_id=1, source_target_pairs={{0,2},{1,3},{2,0},{3,1},{64,66},{65,67},{66,64},{67,65},{4,6},{5,7... | collective-permute-start | bytes 73736 | tf_op jit(solution)/shard_map/ppermute | solution.py:633
  107.0 7.7 %collective-permute-start.12 = (bf16[24,512]{1,0:T(8,128)(2,1)S(1)}, bf16[24,512]{1,0:T(8,128)(2,1)S(1)}, u32[]{:S(2)}, u32[]{:S(2)}) collective-permute-start(bf16[24,512]{1,0:T(8,128)(2,1)S(1)} %get-tuple-element.90), channel_id=1, source_target_pairs={{0,66},{1,67},{2,64},{3,65},{64,2},{65,3},{66,0},{67,1},{4,70},{5,... | collective-permute-start | bytes 73736 | tf_op jit(solution)/shard_map/ppermute | solution.py:633
  107.3 7.4 %collective-permute-start.11 = (bf16[24,512]{1,0:T(8,128)(2,1)S(1)}, bf16[24,512]{1,0:T(8,128)(2,1)S(1)}, u32[]{:S(2)}, u32[]{:S(2)}) collective-permute-start(bf16[24,512]{1,0:T(8,128)(2,1)S(1)} %get-tuple-element.91), channel_id=1, source_target_pairs={{0,1},{1,0},{2,3},{3,2},{64,65},{65,64},{66,67},{67,66},{4,5},{5,4... | collective-permute-start | bytes 73736 | tf_op jit(solution)/shard_map/ppermute | solution.py:633
  109.3 5.5 %collective-permute-start.10 = (bf16[24,512]{1,0:T(8,128)(2,1)S(1)}, bf16[24,512]{1,0:T(8,128)(2,1)S(1)}, u32[]{:S(2)}, u32[]{:S(2)}) collective-permute-start(bf16[24,512]{1,0:T(8,128)(2,1)S(1)} %get-tuple-element.92), channel_id=1, source_target_pairs={{0,65},{1,64},{2,67},{3,66},{64,1},{65,0},{66,3},{67,2},{4,69},{5,... | collective-permute-start | bytes 73736 | tf_op jit(solution)/shard_map/ppermute | solution.py:633
  109.3 7.7 %collective-permute-start.9 = (bf16[24,512]{1,0:T(8,128)(2,1)S(1)}, bf16[24,512]{1,0:T(8,128)(2,1)S(1)}, u32[]{:S(2)}, u32[]{:S(2)}) collective-permute-start(bf16[24,512]{1,0:T(8,128)(2,1)S(1)} %get-tuple-element.93), channel_id=1, source_target_pairs={{0,3},{1,2},{2,1},{3,0},{64,67},{65,66},{66,65},{67,64},{4,7},{5,6... | collective-permute-start | bytes 73736 | tf_op jit(solution)/shard_map/ppermute | solution.py:633
  113.3 4.8 %collective-permute-start.8 = (bf16[24,512]{1,0:T(8,128)(2,1)S(1)}, bf16[24,512]{1,0:T(8,128)(2,1)S(1)}, u32[]{:S(2)}, u32[]{:S(2)}) collective-permute-start(bf16[24,512]{1,0:T(8,128)(2,1)S(1)} %get-tuple-element.94), channel_id=1, source_target_pairs={{0,67},{1,66},{2,65},{3,64},{64,3},{65,2},{66,1},{67,0},{4,71},{5,... | collective-permute-start | bytes 73736 | tf_op jit(solution)/shard_map/ppermute | solution.py:633
  120.0 46.4 %all-to-all-start.3 = ((bf16[64,176,128]{2,1,0:T(8,128)(2,1)}), bf16[64,176,128]{2,1,0:T(8,128)(2,1)S(1)}, u32[]{:S(2)}, u32[]{:S(2)}) async-start(bf16[64,176,128]{2,1,0:T(8,128)(2,1)} %copy-done.3), calls=%async_computation.3 | async-start | bytes 5767168 | tf_op jit(solution)/shard_map/all_to_all | solution.py:637
  166.4 6.7 %collective-permute-start.15 = (bf16[64,176,128]{2,1,0:T(8,128)(2,1)S(1)}, bf16[64,176,128]{2,1,0:T(8,128)(2,1)S(1)}, u32[]{:S(2)}, u32[]{:S(2)}) collective-permute-start(bf16[64,176,128]{2,1,0:T(8,128)(2,1)S(1)} %all-to-all-done.3.mine_ref), channel_id=1, source_target_pairs={{0,1},{1,0},{2,3},{3,2},{4,5},{5,4},{6,7},{7,6},{8,9},{9,8},{10,11... | collective-permute-start | bytes 8650760 | tf_op jit(solution)/shard_map/ppermute | solution.py:633
  (23 other events, 112.7 us)

commit v4 on v3

--- a/solution.py
+++ b/solution.py
@@ -15,7 +15,6 @@
 ENC = ("yl", "z", "x")
 BB = ("yh", "co")
 SAME_CORE = ("yl", "z", "x", "yh")
-PLANE = ("z", "x")
 COLS = ("yl", "yh", "co")
 MIB = 1024 * 1024
 
@@ -43,6 +42,10 @@
 
 def vmem():
     return pl.BlockSpec(memory_space=pltpu.VMEM)
+
+
+def hbm():
+    return pl.BlockSpec(memory_space=pltpu.HBM)
 
 
 def smem():
@@ -78,16 +81,23 @@
 
 
 def forward_kernel(
-    x_ref, k_ref, gain_ref, win_ref, bias_ref, wout_ref, scale_ref, code_ref,
+    x_hbm, k_ref, gain_ref, win_hbm, bias_ref, wout_hbm, scale_ref, code_ref,
     pay_ref, normt_ref, xhat_ref, rstd_ref, slope_ref, hsum_ref, gsum_ref, bsum_ref, xp_ref,
-    xf_ref, xs_ref, kb_ref, conv_ref, norm_ref, hs_ref,
+    xf_ref, xs_ref, kb_ref, conv_ref, norm_ref, hs_ref, x_ref, win_ref, wout_ref, sem,
 ):
+    load_x = [pltpu.make_async_copy(x_hbm.at[t], x_ref.at[t], sem.at[t]) for t in range(2)]
+    load_win = pltpu.make_async_copy(win_hbm, win_ref, sem.at[2])
+    load_wout = pltpu.make_async_copy(wout_hbm, wout_ref, sem.at[3])
+    for load in load_x + [load_win, load_wout]:
+        load.start()
     for lt in range(3):
         lanes = slice(lt * 128, lt * 128 + 128)
         for a in range(7):
             kb_ref[lt, a] = k_ref[a, :, lanes]
-        for t in range(2):
-            xf_ref[lt, t] = x_ref[t, :, :, lanes].astype(F32)
+    for t in range(2):
+        load_x[t].wait()
+        for lt in range(3):
+            xf_ref[lt, t] = x_ref[t, :, :, lt * 128 : lt * 128 + 128].astype(F32)
 
     def split(n, carry):
         lt = n // 2
@@ -146,12 +156,12 @@
             xhat = c[lt] * rstd
             xhat_ref[lt, rows, :] = xhat
             normed = xhat * gain_ref[lanes].reshape(1, 128)
-            norm_ref[:, lanes] = normed.astype(BF)
+            norm_ref[n, :, lanes] = normed.astype(BF)
             normt_ref[n, lanes, :] = normed.T.astype(BF)
         toks = pl.ds(pl.multiple_of(n * 8, 8), 8)
         for h in range(6):
             hid = slice(h * 256, h * 256 + 256)
-            u = nn(norm_ref[...], win_ref[:, hid]) + bias_ref[hid].reshape(1, 256)
+            u = nn(norm_ref[n], win_ref[:, hid]) + bias_ref[hid].reshape(1, 256)
             value, slope = gelu_parts(u)
             value = value.astype(BF).astype(F32)
             hs_ref[toks, hid] = jnp.sum(value.reshape(16, 8, 256), axis=0)
@@ -159,7 +169,9 @@
             slope_ref[rows, hid] = slope.astype(BF)
         return carry
 
-    lax.fori_loop(0, 8, block, 0)
+    load_win.wait()
+    lax.fori_loop(0, 8, block, 0, unroll=8)
+    load_wout.wait()
 
     hs = hs_ref[...]
     hi = hs.astype(BF)
@@ -203,106 +215,89 @@
             pltpu.VMEM((3, 3, 2, 4, 16, 8, 128), F32),
             pltpu.VMEM((3, 7, 7, 128), F32),
             pltpu.VMEM((3, 2, 4, 4, 4, 8, 128), F32),
-            pltpu.VMEM((128, 384), BF),
+            pltpu.VMEM((8, 128, 384), BF),
             pltpu.VMEM((64, 1536), F32),
+            pltpu.VMEM((2, 16, 32, 384), BF),
+            pltpu.VMEM((384, 1536), BF),
+            pltpu.VMEM((1536, 384), BF),
+            pltpu.SemaphoreType.DMA((4,)),
         ],
-        [vmem()] * 8,
-        22,
+        [hbm(), vmem(), vmem(), hbm(), vmem(), hbm(), vmem(), vmem()],
+        26,
         14,
     )(x, k, gain, win, bias, wout, scale, code)
 
 
-def fold_kernel(proj_ref, conn_ref, out_ref, acc_ref):
-    n = pl.program_id(0)
-
-    @pl.when(n == 0)
-    def _():
-        acc_ref[...] = jnp.zeros_like(acc_ref)
-
-    acc_ref[...] += nn(proj_ref[...], conn_ref[...])
-
-    @pl.when(n == pl.num_programs(0) - 1)
-    def _():
-        out_ref[...] = acc_ref[...].astype(BF)
+def fold_kernel(proj_ref, conn_ref, out_ref):
+    for at, size in ((0, 512), (512, 384)):
+        out_ref[:, at : at + size] = nn(proj_ref[...], conn_ref[:, at : at + size]).astype(BF)
 
 
 def fold(weight_proj, connector):
-    return pl.pallas_call(
-        fold_kernel,
-        out_shape=jax.ShapeDtypeStruct((384, 896), BF),
-        grid=(8,),
-        in_specs=[
-            pl.BlockSpec((384, 512), lambda n: (0, n)),
-            pl.BlockSpec((512, 896), lambda n: (n, 0)),
-        ],
-        out_specs=pl.BlockSpec((384, 896), lambda n: (0, 0)),
-        scratch_shapes=[pltpu.VMEM((384, 896), F32)],
-        compiler_params=pltpu.CompilerParams(vmem_limit_bytes=8 * MIB),
-        cost_estimate=cost(0),
+    return call(
+        fold_kernel, jax.ShapeDtypeStruct((384, 896), BF), [], [vmem()] * 2, 16, 0
     )(weight_proj, connector)
 
 
 def rows_kernel(gp_ref, conn_ref, keep_ref, send_ref):
-    out = nt(gp_ref[...], conn_ref[...]).astype(BF)
-    keep_ref[...] = out[:128]
-    send_ref[...] = out[128:]
+    for n in range(8):
+        cols = slice(n * 512, n * 512 + 512)
+        out = nt(gp_ref[...], conn_ref[cols, :]).astype(BF)
+        keep_ref[:, cols] = out[:128]
+        send_ref[:, cols] = out[128:]
 
 
 def token_rows(grad_pre, connector):
     shape = jax.ShapeDtypeStruct((128, 4096), BF)
-    return pl.pallas_call(
-        rows_kernel,
-        out_shape=[shape, shape],
-        grid=(8,),
-        in_specs=[
-            pl.BlockSpec((256, 896), lambda n: (0, 0)),
-            pl.BlockSpec((512, 896), lambda n: (n, 0)),
-        ],
-        out_specs=[pl.BlockSpec((128, 512), lambda n: (0, n))] * 2,
-        compiler_params=pltpu.CompilerParams(vmem_limit_bytes=8 * MIB),
-        cost_estimate=cost(0),
-    )(grad_pre, connector)
-
-
-def proj_kernel(at_ref, parts_ref, conn_ref, out_ref, sum_ref):
-    @pl.when(pl.program_id(0) == 0)
-    def _():
-        total = parts_ref[0].astype(F32)
-        for m in range(1, 16):
-            total = total + parts_ref[m].astype(F32)
-        sum_ref[...] = total.astype(BF)
-
-    out_ref[0] = nt(sum_ref[...], conn_ref[...]).astype(BF)
+    return call(rows_kernel, [shape, shape], [], [vmem()] * 2, 14, 0)(grad_pre, connector)
+
+
+def outer_kernel(at_ref, r0_ref, r1_ref, r2_ref, r3_ref, o0_ref, o1_ref, o2_ref, o3_ref, sum_ref):
+    total = r0_ref[...].astype(F32) + r1_ref[...].astype(F32)
+    sum_ref[...] = total + r2_ref[...].astype(F32) + r3_ref[...].astype(F32)
+    for d, o_ref in enumerate((o0_ref, o1_ref, o2_ref, o3_ref)):
+        rows = pl.ds(pl.multiple_of(((at_ref[4] + d) & 3) * 24, 8), 24)
+        o_ref[...] = sum_ref[rows, :].astype(BF)
+
+
+def outer_rows(at, parts):
+    return call(
+        outer_kernel,
+        [jax.ShapeDtypeStruct((24, 896), BF)] * 4,
+        [pltpu.VMEM((96, 896), F32)],
+        [smem()] + [vmem()] * 4,
+        4,
+        1,
+    )(at, *parts)
+
+
+def proj_kernel(at_ref, r0_ref, r1_ref, r2_ref, r3_ref, conn_ref, out_ref):
+    total = r0_ref[...].astype(F32) + r1_ref[...].astype(F32)
+    total = (total + r2_ref[...].astype(F32) + r3_ref[...].astype(F32)).astype(BF)
+    for n in range(8):
+        chunk = (
+            (at_ref[0] ^ (1 - n // 4)) * 4
+            + (at_ref[1] ^ (1 - (n % 4) // 2)) * 2
+            + (at_ref[2] ^ (1 - n % 2))
+        )
+        rows = pl.ds(pl.multiple_of(chunk * 512, 512), 512)
+        out_ref[n] = nt(total, conn_ref[rows, :]).astype(BF)
 
 
 def proj_rows(at, parts, connector):
-    def chunk(n, at):
-        return (
-            (at[0] ^ (1 - n // 4)) * 4 + (at[1] ^ (1 - (n % 4) // 2)) * 2 + (at[2] ^ (1 - n % 2)),
-            0,
-        )
-
-    return pl.pallas_call(
+    return call(
         proj_kernel,
-        out_shape=jax.ShapeDtypeStruct((8, 24, 512), BF),
-        grid_spec=pltpu.PrefetchScalarGridSpec(
-            num_scalar_prefetch=1,
-            grid=(8,),
-            in_specs=[
-                pl.BlockSpec((16, 24, 896), lambda n, at: (0, 0, 0)),
-                pl.BlockSpec((512, 896), chunk),
-            ],
-            out_specs=pl.BlockSpec((1, 24, 512), lambda n, at: (n, 0, 0)),
-            scratch_shapes=[pltpu.VMEM((24, 896), BF)],
-        ),
-        compiler_params=pltpu.CompilerParams(vmem_limit_bytes=8 * MIB),
-        cost_estimate=cost(0),
-    )(at, parts, connector)
+        jax.ShapeDtypeStruct((8, 24, 512), BF),
+        [],
+        [smem()] + [vmem()] * 5,
+        14,
+        0,
+    )(at, *parts, connector)
 
 
 def connector_kernel(
-    bb_ref, p0_ref, p1_ref, p2_ref, p3_ref, cot_ref, wc_ref,
-    gp_ref, keep_ref, send_ref, s_ref, pick_ref, pool_ref,
+    at_ref, p0_ref, p1_ref, p2_ref, p3_ref, cot_ref, wc_ref,
+    gp_ref, keep_ref, send_ref, s0_ref, s1_ref, s2_ref, s3_ref, pick_ref, pool_ref, poolt_ref,
 ):
     row = lax.broadcasted_iota(jnp.int32, (64, 128), 0)
     lane = lax.broadcasted_iota(jnp.int32, (64, 128), 1)
@@ -310,7 +305,7 @@
         tok = slice(n * 64, n * 64 + 64)
         pool_ref[tok, :] = p_ref[:, 0:384]
         code = p_ref[:, 384:512].astype(F32).astype(jnp.int32)
-        src = bb_ref[0] ^ d
+        src = at_ref[5] ^ d
         want = (code >> 1) * 16 + src * 4 + (code & 1) * 2 + (row & 1)
         want = jnp.where(code < 0, -1, want)
         for q in range(4):
@@ -325,11 +320,13 @@
     tok = nt(gp_ref[...], wc_ref[...])
     keep_ref[...] = tok[:128]
     send_ref[...] = tok[128:]
-    pool_t = pool_ref[...].astype(F32).T.astype(BF)
-    s_ref[...] = nn(pool_t, gp_ref[...]).astype(BF)
-
-
-def connector_part(bb, pays, cot, wc):
+    poolt_ref[...] = pool_ref[...].astype(F32).T.astype(BF)
+    for d, s_ref in enumerate((s0_ref, s1_ref, s2_ref, s3_ref)):
+        rows = pl.ds(pl.multiple_of(((at_ref[3] + d) & 3) * 96, 96), 96)
+        s_ref[...] = nn(poolt_ref[rows, :], gp_ref[...]).astype(BF)
+
+
+def connector_part(at, pays, cot, wc):
     shape = jax.ShapeDtypeStruct
     return call(
         connector_kernel,
@@ -337,13 +334,17 @@
             shape((256, 896), BF),
             shape((128, 384), F32),
             shape((128, 384), F32),
-            shape((384, 896), BF),
+        ]
+        + [shape((96, 896), BF)] * 4,
+        [
+            pltpu.VMEM((256, 512), BF),
+            pltpu.VMEM((256, 384), BF),
+            pltpu.VMEM((384, 256), BF),
         ],
-        [pltpu.VMEM((256, 512), BF), pltpu.VMEM((256, 384), BF)],
         [smem()] + [vmem()] * 6,
         6,
         3,
-    )(bb, *pays, cot, wc)
+    )(at, *pays, cot, wc)
 
 
 def mlp_back_kernel(
@@ -369,7 +370,7 @@
             dpre_ref[h, rows, :] = d.reshape(128, 384).astype(BF)
         return carry
 
-    lax.fori_loop(0, 8, block, 0)
+    lax.fori_loop(0, 8, block, 0, unroll=8)
     hsum_t = hsum_ref[...].astype(F32).T.astype(BF)
     normt = jnp.concatenate([normt_ref[n] for n in range(8)], axis=1)
     mine = co_ref[0] == 0
@@ -404,7 +405,7 @@
         [pltpu.VMEM((64, 1536), F32)],
         [smem()] + [vmem()] * 10,
         14,
-        5,
+        3,
     )(co, near, part, far, normt, slope, hsum, gsum, bsum, wout, scale)
 
 
@@ -443,7 +444,7 @@
         return tuple(c + g for c, g in zip(carry, gains))
 
     zero = jnp.zeros((8, 128), F32)
-    gains = lax.fori_loop(0, 8, block, (zero, zero, zero))
+    gains = lax.fori_loop(0, 8, block, (zero, zero, zero), unroll=8)
     for lt in range(3):
         lanes = slice(lt * 128, lt * 128 + 128)
         out_ref[49:50, lanes] = jnp.sum(gains[lt], axis=0, keepdims=True)
@@ -486,7 +487,7 @@
         [pltpu.VMEM((3, 3, 2, 4, 16, 8, 128), F32), pltpu.VMEM((3, 49, 8, 128), F32)],
         [vmem()] * 6,
         15,
-        10,
+        2,
     )(dpre, win, xhat, rstd, gain, xp)
 
 
@@ -633,6 +634,12 @@
     return lax.ppermute(v, axes, [(i, i ^ d) for i in range(size)])
 
 
+def turn(parts, axis):
+    return [parts[0]] + [
+        lax.ppermute(parts[d], axis, [(i, (i + d) % 4) for i in range(4)]) for d in (1, 2, 3)
+    ]
+
+
 def exchange(v, axes):
     return lax.all_to_all(v, axes, split_axis=0, concat_axis=0, tiled=True)
 
@@ -652,13 +659,18 @@
     connector,
     cotangent,
 ):
-    at = jnp.stack([lax.axis_index(axis) for axis in ("co", "yh", "yl")]).astype(jnp.int32)
-    bb = lax.axis_index(BB).astype(jnp.int32).reshape(1)
+    at = ("co", "yh", "yl", "z", "x", BB)
+    at = jnp.stack([lax.axis_index(axis) for axis in at]).astype(jnp.int32)
     sent = call(
-        arrange_kernel, jax.ShapeDtypeStruct((512, 896), BF), [], [vmem()], 4, 2
+        arrange_kernel,
+        jax.ShapeDtypeStruct((512, 896), BF),
+        [],
+        [vmem()],
+        4,
+        2,
     )(cotangent)
     cot = exchange(sent.reshape(32, 16, 896), ENC).reshape(512, 896)
-    image_tiles, sent, at, bb = lax.optimization_barrier((image_tiles, sent, at, bb))
+    image_tiles, sent, at = lax.optimization_barrier((image_tiles, sent, at))
 
     live = jnp.arange(32, dtype=jnp.int32) // 16 < image_counts[0]
     code = jnp.where(live, destination[0] * 2 + row_offset[0], -1).astype(BF)
@@ -675,24 +687,24 @@
     )
     pays = [pay] + [swap(pay, BB, 4, d) for d in (2, 1, 3)]
     wc = fold(lax.optimization_barrier((weight_proj, pay))[0], connector)
-    grad_pre, part, give, outer = connector_part(bb, pays, cot, wc)
+    grad_pre, part, give, *outer = connector_part(at, pays, cot, wc)
 
     near = swap(give, "co", 2, 1)
     far = swap(part[64:] + near[64:], "yh", 2, 1)
-    outer = exchange(outer.reshape(16, 24, 896), PLANE)
+    outer = turn(outer, "z")
     row_part, row_give = token_rows(grad_pre, connector)
-    near, far, outer, row_part, row_give = lax.optimization_barrier(
-        (near, far, outer, row_part, row_give)
-    )
-
     row_near = swap(row_give, "co", 2, 1).astype(F32)
-    row_far = swap((row_part[64:].astype(F32) + row_near[64:]).astype(BF), "yh", 2, 1)
+    row_tail = (row_part[64:].astype(F32) + row_near[64:]).astype(BF)
+    near, far, row_tail = lax.optimization_barrier((near, far, row_tail))
+    row_far = swap(row_tail, "yh", 2, 1)
     keep, send, dpre, small_a = mlp_back(
         at, near, part, far, normt, slope, hsum, gsum, bsum, weight_out, layer_scale
     )
+    send, dpre, *outer = lax.optimization_barrier((send, dpre, *outer))
     recv = swap(send, "co", 2, 1)
+    outer = turn(outer_rows(at, outer), "x")
     small_b = front_back(dpre, weight_in, xhat, rstd, norm_gain, xp)
-    small_b, row_far = lax.optimization_barrier((small_b, row_far))
+    small_b, row_far, outer = lax.optimization_barrier((small_b, row_far, outer))
     packed = pack(keep, recv, small_a, small_b)
     parts = exchange(packed, SAME_CORE)
     packed, outer = lax.optimization_barrier((packed, outer))

time: 179 us -> 166 us (0.927)
  local copies, waits for them, and re-layouts: 16.1 us -> 8.47 us
  Pallas kernels: 51.2 us -> 45.5 us
  starting transfers between devices: 60.9 us -> 62.7 us
    ppermute x0 -> x6, starting transfers between devices: none -> 10.1 us  [turn(): lax.ppermute(parts[d], axis, [(i, (i + d) % 4) for i in range(4)])]
    all_to_all x4 -> x3, starting transfers between devices: 35.6 us -> 26.5 us  [exchange(): return lax.all_to_all(v, axes, split_axis=0, concat_axis=0, tiled=True)]
    unnamed x70 -> x74, local copies, waits for them, and re-layouts: 15.8 us -> 8.08 us
    pallas_call x3 -> x4, Pallas kernels: 12.8 us -> 9.23 us  [the longest x1 3.4 us: fold(): call(fold_kernel, jax.ShapeDtypeStruct((384, 896), BF), [], [vmem()] * 2,...]
    all_to_all x4 -> x3, waiting for transfers between devices: 33.6 us -> 33.4 us  [exchange(): return lax.all_to_all(v, axes, split_axis=0, concat_axis=0, tiled=True)]
  transfers between devices with their start and end apart: 20 -> 25, of which waited for: 6 -> 5; matrix products, arithmetic and copies ran while one was open for 2% -> 2% of each run, Pallas kernels for 23% -> 20%
where the time goes in v4:
time: 166 us; the launch traced here: 165 us
  starting transfers between devices  62.7 us (38%)
  Pallas kernels  45.5 us (27%)
  waiting for transfers between devices  43.7 us (26%)
  local copies, waits for them, and re-layouts  8.47 us (5%)
  other arithmetic  2.78 us (2%)
  between operations  1.94 us (1%)
    all_to_all x3, waiting for transfers between devices, exchange(): return lax.all_to_all(v, axes, split_axis=0, concat_axis=0, tiled=True)  33.4 us
    all_to_all x3, starting transfers between devices, exchange(): return lax.all_to_all(v, axes, split_axis=0, concat_axis=0, tiled=True)  26.5 us
    ppermute x16, starting transfers between devices, swap(): return lax.ppermute(v, axes, [(i, i ^ d) for i in range(size)])  26.1 us
    pallas_call x1, Pallas kernels, forward(): call(forward_kernel, [shape((64, 512), BF), shape((8, 384, 128), BF), sha...  13.2 us
    ppermute x16, waiting for transfers between devices, swap(): return lax.ppermute(v, axes, [(i, i ^ d) for i in range(size)])  10.3 us
    ppermute x6, starting transfers between devices, turn(): lax.ppermute(parts[d], axis, [(i, (i + d) % 4) for i in range(4)])  10.1 us
    pallas_call x1, Pallas kernels, front_back(): call(front_back_kernel, jax.ShapeDtypeStruct((56, 384), F32), [pltpu.VMEM...  8.57 us
    unnamed x74, local copies, waits for them, and re-layouts  8.08 us
  transfers between devices with their start and end apart: 25, of which 5 were waited for; matrix products, arithmetic and copies ran while one was open for 2% of the time, Pallas kernels for 20%

profile of v4, /device:TPU:1, one launch (start us, length us, event | category | flops | bytes accessed | tf_op | source)
XLA Modules:
  0.0 165.1 jit_solution(14774784978769507874)
XLA Ops:
  2.0 1.7 shard_map.188
  3.7 9.8 %all-to-all-start = ((bf16[32,16,896]{2,1,0:T(8,128)(2,1)}), bf16[32,16,896]{2,1,0:T(8,128)(2,1)}, u32[]{:S(2)}, u32[]{:S(2)}) async-start(bf16[32,16,896]{2,1,0:T(8,128)(2,1)} %bitcast.8), calls=%async_computation | async-start | bytes 1835008 | tf_op jit(solution)/shard_map/all_to_all | solution.py:644
  14.7 13.2 %shard_map.189 = (bf16[64,512]{1,0:T(8,128)(2,1)S(1)}, bf16[8,384,128]{2,1,0:T(8,128)(2,1)S(1)}, f32[3,1024,128]{2,1,0:T(8,128)S(1)}, f32[1024,128]{1,0:T(8,128)...) custom-call(bf16[2,16,32,384]{3,2,1,0:T(8,128)(2,1)S(1)} %copy-done., ...), custom_call_target="tpu_custom_call" | custom-call | flops 15400000512 | bytes 1 | tf_op jit(solution)/shard_map/pallas_call | solution.py:200
  28.0 3.5 %collective-permute-start.2 = (bf16[64,512]{1,0:T(8,128)(2,1)S(1)}, bf16[64,512]{1,0:T(8,128)(2,1)S(1)}, u32[]{:S(2)}, u32[]{:S(2)}) collective-permute-start(bf16[64,512]{1,0:T(8,128)(2,1)S(1)} %get-tuple-element.67.p0_ref), channel_id=1, source_target_pairs={{0,3},{1,2},{2,1},{3,0},{4,7},{5,6},{6,5},{7,4},{8,11},{9,10},{10,... | collective-permute-start | bytes 196616 | tf_op jit(solution)/shard_map/ppermute | solution.py:634
  31.9 3.4 %shard_map.190.wc_ref = bf16[384,896]{1,0:T(8,128)(2,1)S(1)} custom-call(bf16[384,4096]{1,0:T(8,128)(2,1)S(1)} %copy-done.1, bf16[4096,896]{1,0:T(8,128)(2,1)S(1)} %bitcast.29), custom_call_target="tpu_custom_call" | custom-call | flops 1 | bytes 1 | tf_op jit(solution)/shard_map/pallas_call | solution.py:237
  37.3 2.9 %shard_map.191 = (bf16[256,896]{1,0:T(8,128)(2,1)S(1)}, f32[128,384]{1,0:T(8,128)S(1)}, f32[128,384]{1,0:T(8,128)S(1)}, bf16[96,896]{1,0:T(8,128)(2,1)S(1)}, bf1...) custom-call(s32[6]{0:T(128)S(1)} %stack.27.at_ref.co_ref, ...), custom_call_target="tpu_custom_call" | custom-call | flops 3300000000 | bytes 1 | tf_op jit(solution)/shard_map/pallas_call | solution.py:331
  40.3 2.4 %shard_map.192 = (bf16[128,4096]{1,0:T(8,128)(2,1)S(1)}, bf16[128,4096]{1,0:T(8,128)(2,1)S(1)}) custom-call(bf16[256,896]{1,0:T(8,128)(2,1)S(1)} %get-tuple-element.71.gp_ref, bf16[4096,896]{1,0:T(8,128)(2,1)S(1)} %bitcast.31), custom_call_target="tpu_custom_call" | custom-call | flops 1 | bytes 1 | tf_op jit(solution)/shard_map/pallas_call | solution.py:252
  42.7 1.6 collective-permute-start.5
  45.9 2.4 %collective-permute-start.7 = (bf16[96,896]{1,0:T(8,128)(2,1)S(1)}, bf16[96,896]{1,0:T(8,128)(2,1)S(1)}, u32[]{:S(2)}, u32[]{:S(2)}) collective-permute-start(bf16[96,896]{1,0:T(8,128)(2,1)S(1)} %get-tuple-element.86), channel_id=1, source_target_pairs={{0,32},{16,48},{32,0},{48,16},{1,33},{17,49},{33,1},{49,17},{2,34}... | collective-permute-start | bytes 516104 | tf_op jit(solution)/shard_map/ppermute | solution.py:639
  49.5 1.9 %collective-permute-start.4 = (f32[64,384]{1,0:T(8,128)S(1)}, f32[64,384]{1,0:T(8,128)S(1)}, u32[]{:S(2)}, u32[]{:S(2)}) collective-permute-start(f32[64,384]{1,0:T(8,128)S(1)} %slice_add_fusion.2), channel_id=1, source_target_pairs={{0,2},{2,0},{1,3},{3,1},{4,6},{6,4},{5,7},{7,5},{8,10},{10,8},{9,1... | collective-permute-start | bytes 294920 | tf_op jit(solution)/shard_map/ppermute | solution.py:634
  51.8 3.1 %collective-permute-done.4.far_ref = f32[64,384]{1,0:T(8,128)S(1)} collective-permute-done((f32[64,384]{1,0:T(8,128)S(1)}, f32[64,384]{1,0:T(8,128)S(1)}, u32[]{:S(2)}, u32[]{:S(2)}) %collective-permute-start.4) | collective-permute-done | bytes 98336 | tf_op jit(solution)/shard_map/ppermute | solution.py:634
  54.9 3.7 %shard_map.193 = (bf16[1536,384]{1,0:T(8,128)(2,1)S(1)}, bf16[1536,384]{1,0:T(8,128)(2,1)S(1)}, bf16[4,1024,384]{2,1,0:T(8,128)(2,1)S(1)}, f32[8,384]{1,0:T(8,128)S(1)}) custom-call(s32[6]{0:T(128)S(1)} %stack.27.at_ref.co_ref, f32[128,384]{1,0:T(8,128)S(1)} %collective-permute-done.3.near_ref, f32[128,384]{1,0:T(8,128)S(1)} %get-tuple-element.70.part_ref, ...), custom_call_target="tpu_custom_call" | custom-call | flops 3300000000 | bytes 1 | tf_op jit(solution)/shard_map/pallas_call | solution.py:397
  58.7 2.4 %collective-permute-start.9 = (bf16[1536,384]{1,0:T(8,128)(2,1)S(1)}, bf16[1536,384]{1,0:T(8,128)(2,1)S(1)}, u32[]{:S(2)}, u32[]{:S(2)}) collective-permute-start(bf16[1536,384]{1,0:T(8,128)(2,1)S(1)} %get-tuple-element.88), channel_id=1, source_target_pairs={{0,1},{1,0},{2,3},{3,2},{4,5},{5,4},{6,7},{7,6},{8,9},{9,8},{10,11... | collective-permute-start | bytes 3538952 | tf_op jit(solution)/shard_map/ppermute | solution.py:634
  61.1 1.9 %collective-permute-start.10 = (bf16[64,4096]{1,0:T(8,128)(2,1)S(1)}, bf16[64,4096]{1,0:T(8,128)(2,1)}, u32[]{:S(2)}, u32[]{:S(2)}) collective-permute-start(bf16[64,4096]{1,0:T(8,128)(2,1)S(1)} %fusion.2), channel_id=1, source_target_pairs={{0,2},{2,0},{1,3},{3,1},{4,6},{6,4},{5,7},{7,5},{8,10},{10,8},{9,1... | collective-permute-start | bytes 1572872 | tf_op jit(solution)/shard_map/ppermute | solution.py:634
  65.1 2.4 %collective-permute-start.12 = (bf16[24,896]{1,0:T(8,128)(2,1)S(1)}, bf16[24,896]{1,0:T(8,128)(2,1)S(1)}, u32[]{:S(2)}, u32[]{:S(2)}) collective-permute-start(bf16[24,896]{1,0:T(8,128)(2,1)S(1)} %get-tuple-element.101), channel_id=1, source_target_pairs={{0,8},{4,12},{8,0},{12,4},{1,9},{5,13},{9,1},{13,5},{2,10},{6,14},... | collective-permute-start | bytes 129032 | tf_op jit(solution)/shard_map/ppermute | solution.py:639
  68.7 8.6 %shard_map.194.b_ref = f32[56,384]{1,0:T(8,128)S(1)} custom-call(bf16[4,1024,384]{2,1,0:T(8,128)(2,1)S(1)} %get-tuple-element.90.dpre_ref, bf16[384,1536]{1,0:T(8,128)(2,1)S(1)} %copy-done.9, f32[3,1024,128]{2,1,0:T(8,128)S(1)} %copy-done.17, f32[1024,128]{1,0:T(8,128)S(1)} %copy-done.21, f32[384]{0:T(512)S(1)} %copy-done.15, ...), custom_call_target="tpu_custom_call" | custom-call | flops 2200000000 | bytes 1 | tf_op jit(solution)/shard_map/pallas_call | solution.py:484
  77.3 1.5 shard_map.196
  78.9 5.5 %all-to-all-start.1 = ((bf16[64,80,128]{2,1,0:T(8,128)(2,1)}), bf16[64,80,128]{2,1,0:T(8,128)(2,1)S(1)}, u32[]{:S(2)}, u32[]{:S(2)}) async-start(bf16[64,80,128]{2,1,0:T(8,128)(2,1)} %shard_map.196), calls=%async_computation.1 | async-start | bytes 2621440 | tf_op jit(solution)/shard_map/all_to_all | solution.py:644
  84.4 3.1 %copy-done = bf16[4096,896]{1,0:T(8,128)(2,1)S(1)} copy-done((bf16[4096,896]{1,0:T(8,128)(2,1)S(1)}, bf16[4096,896]{1,0:T(8,128)(2,1)}, u32[]{:S(2)}) %copy-start) | copy-done | bytes 7340056
  87.4 2.8 %shard_map.197 = bf16[8,24,512]{2,1,0:T(8,128)(2,1)S(1)} custom-call(s32[6]{0:T(128)S(1)} %stack.27.at_ref.co_ref, bf16[24,896]{1,0:T(8,128)(2,1)S(1)} %get-tuple-element.108.r0_ref, bf16[24,896]{1,0:T(8,128)(2,1)S(1)} %collective-permute-done.11.r1_ref, bf16[24,896]{1,0:T(8,128)(2,1)S(1)} %collective-permute-done.12.r2_ref, ...), custom_call_target="tpu_custom_call" | custom-call | flops 1 | bytes 1 | tf_op jit(solution)/shard_map/pallas_call | solution.py:288
  91.5 2.4 %collective-permute-start.19 = (bf16[24,512]{1,0:T(8,128)(2,1)S(1)}, bf16[24,512]{1,0:T(8,128)(2,1)S(1)}, u32[]{:S(2)}, u32[]{:S(2)}) collective-permute-start(bf16[24,512]{1,0:T(8,128)(2,1)S(1)} %get-tuple-element.123), channel_id=1, source_target_pairs={{0,2},{1,3},{2,0},{3,1},{64,66},{65,67},{66,64},{67,65},{4,6},{5,7... | collective-permute-start | bytes 73736 | tf_op jit(solution)/shard_map/ppermute | solution.py:634
  94.2 2.0 %collective-permute-start.17 = (bf16[24,512]{1,0:T(8,128)(2,1)S(1)}, bf16[24,512]{1,0:T(8,128)(2,1)S(1)}, u32[]{:S(2)}, u32[]{:S(2)}) collective-permute-start(bf16[24,512]{1,0:T(8,128)(2,1)S(1)} %get-tuple-element.125), channel_id=1, source_target_pairs={{0,1},{1,0},{2,3},{3,2},{64,65},{65,64},{66,67},{67,66},{4,5},{5,4... | collective-permute-start | bytes 73736 | tf_op jit(solution)/shard_map/ppermute | solution.py:634
  96.3 4.0 %collective-permute-start.15 = (bf16[24,512]{1,0:T(8,128)(2,1)S(1)}, bf16[24,512]{1,0:T(8,128)(2,1)S(1)}, u32[]{:S(2)}, u32[]{:S(2)}) collective-permute-start(bf16[24,512]{1,0:T(8,128)(2,1)S(1)} %get-tuple-element.127), channel_id=1, source_target_pairs={{0,3},{1,2},{2,1},{3,0},{64,67},{65,66},{66,65},{67,64},{4,7},{5,6... | collective-permute-start | bytes 73736 | tf_op jit(solution)/shard_map/ppermute | solution.py:634
  100.3 2.6 %collective-permute-start.14 = (bf16[24,512]{1,0:T(8,128)(2,1)S(1)}, bf16[24,512]{1,0:T(8,128)(2,1)S(1)}, u32[]{:S(2)}, u32[]{:S(2)}) collective-permute-start(bf16[24,512]{1,0:T(8,128)(2,1)S(1)} %get-tuple-element.128), channel_id=1, source_target_pairs={{0,67},{1,66},{2,65},{3,64},{64,3},{65,2},{66,1},{67,0},{4,71},{5,... | collective-permute-start | bytes 73736 | tf_op jit(solution)/shard_map/ppermute | solution.py:634
  102.9 1.7 %collective-permute-done.15.refs_2_ = bf16[24,512]{1,0:T(8,128)(2,1)S(1)} collective-permute-done((bf16[24,512]{1,0:T(8,128)(2,1)S(1)}, bf16[24,512]{1,0:T(8,128)(2,1)S(1)}, u32[]{:S(2)}, u32[]{:S(2)}) %collective-permute-start.15) | collective-permute-done | bytes 24608 | tf_op jit(solution)/shard_map/ppermute | solution.py:634
  105.5 1.6 copy-done.2
  107.1 11.2 %all-to-all-start.2 = ((bf16[64,176,128]{2,1,0:T(8,128)(2,1)}), bf16[64,176,128]{2,1,0:T(8,128)(2,1)S(1)}, u32[]{:S(2)}, u32[]{:S(2)}) async-start(bf16[64,176,128]{2,1,0:T(8,128)(2,1)} %copy-done.2), calls=%async_computation.2 | async-start | bytes 5767168 | tf_op jit(solution)/shard_map/all_to_all | solution.py:644
  118.2 2.5 %fusion.1 = bf16[64,4096]{1,0:T(8,128)(2,1)} fusion(f32[128,4096]{1,0:T(8,128)} %copy-done.30, bf16[64,4096]{1,0:T(8,128)(2,1)} %collective-permute-done.10, bf16[128,4096]{1,0:T(8,128)(2,1)} %copy-done.3), kind=kLoop, calls=%fused_computation.2 | loop fusion | flops 1310720 | bytes 2621440 | tf_op jit(solution)/shard_map/convert_element_type | solution.py:720
  120.7 33.4 %all-to-all-done.2.mine_ref = bf16[64,176,128]{2,1,0:T(8,128)(2,1)S(1)} async-done(((bf16[64,176,128]{2,1,0:T(8,128)(2,1)}), bf16[64,176,128]{2,1,0:T(8,128)(2,1)S(1)}, u32[]{:S(2)}, u32[]{:S(2)}) %all-to-all-start.2) | async-done | bytes 2883616 | tf_op jit(solution)/shard_map/all_to_all | solution.py:644
  154.1 1.8 %collective-permute-start.21 = (bf16[64,176,128]{2,1,0:T(8,128)(2,1)S(1)}, bf16[64,176,128]{2,1,0:T(8,128)(2,1)S(1)}, u32[]{:S(2)}, u32[]{:S(2)}) collective-permute-start(bf16[64,176,128]{2,1,0:T(8,128)(2,1)S(1)} %all-to-all-done.2.mine_ref), channel_id=1, source_target_pairs={{0,1},{1,0},{2,3},{3,2},{4,5},{5,4},{6,7},{7,6},{8,9},{9,8},{10,11... | collective-permute-start | bytes 8650760 | tf_op jit(solution)/shard_map/ppermute | solution.py:634
  155.9 4.9 %collective-permute-done.21.other_ref = bf16[64,176,128]{2,1,0:T(8,128)(2,1)S(1)} collective-permute-done((bf16[64,176,128]{2,1,0:T(8,128)(2,1)S(1)}, bf16[64,176,128]{2,1,0:T(8,128)(2,1)S(1)}, u32[]{:S(2)}, u32[]{:S(2)}) %collective-permute-start.21) | collective-permute-done | bytes 2883616 | tf_op jit(solution)/shard_map/ppermute | solution.py:634
  160.8 4.3 %shard_map.199 = (bf16[384,1536]{1,0:T(8,128)(2,1)}, bf16[1536,384]{1,0:T(8,128)(2,1)}, bf16[384,4096]{1,0:T(8,128)(2,1)}, f32[7,7,384]{2,1,0:T(8,128)}, f32[384]{0:T(512)}, /*index=5*/f32[1536]{0:T(1024)}, f32[384]{0:T(512)}) custom-call(s32[6]{0:T(128)S(1)} %stack.27.at_ref.co_ref, bf16[64,176,128]{2,1,0:T(8,128)(2,1)S(1)} %all-to-all-done.2.mine_ref, ...), custom_call_target="tpu_custom_call" | custom-call | flops 5500000256 | bytes 1 | tf_op jit(solution)/shard_map/pallas_call | solution.py:615
  (116 shorter events, 13.1 us)
Async XLA Ops:
  0.6 13.9 %copy-start.6 = (bf16[1536,384]{1,0:T(8,128)(2,1)S(1)}, bf16[1536,384]{1,0:T(8,128)(2,1)}, u32[]{:S(2)}) copy-start(bf16[1536,384]{1,0:T(8,128)(2,1)} %wout_ref.1) | copy-start | bytes 3538948
  0.6 13.9 %copy-start.8 = (bf16[384,1536]{1,0:T(8,128)(2,1)S(1)}, bf16[384,1536]{1,0:T(8,128)(2,1)}, u32[]{:S(2)}) copy-start(bf16[384,1536]{1,0:T(8,128)(2,1)} %win_ref.1) | copy-start | bytes 3538948
  2.0 12.6 %copy-start.13 = (f32[1536]{0:T(1024)S(1)}, f32[1536]{0:T(1024)}, u32[]{:S(2)}) copy-start(f32[1536]{0:T(1024)} %bias_ref.1) | copy-start | bytes 18436
  3.7 32.6 %all-to-all-start = ((bf16[32,16,896]{2,1,0:T(8,128)(2,1)}), bf16[32,16,896]{2,1,0:T(8,128)(2,1)}, u32[]{:S(2)}, u32[]{:S(2)}) async-start(bf16[32,16,896]{2,1,0:T(8,128)(2,1)} %bitcast.8), calls=%async_computation | async-start | bytes 1835008 | tf_op jit(solution)/shard_map/all_to_all | solution.py:644
  14.5 17.4 %slice-start = ((s8[7340032]{0:T(1024)(128)(4,1)}), s8[4194304]{0:T(1024)(128)(4,1)S(1)}, s32[]{:S(2)}) async-start(s8[7340032]{0:T(1024)(128)(4,1)} %bitcast.28), calls=%async_computation.3 | async-start | bytes 8388608
  14.6 17.2 %slice-start.1 = ((s8[7340032]{0:T(1024)(128)(4,1)}), s8[3145728]{0:T(1024)(128)(4,1)S(1)}, s32[]{:S(2)}) async-start(s8[7340032]{0:T(1024)(128)(4,1)} %bitcast.28), calls=%async_computation.4 | async-start | bytes 6291456
  14.7 17.2 %copy-start.1 = (bf16[384,4096]{1,0:T(8,128)(2,1)S(1)}, bf16[384,4096]{1,0:T(8,128)(2,1)}, u32[]{:S(2)}) copy-start(bf16[384,4096]{1,0:T(8,128)(2,1)} %proj_ref) | copy-start | bytes 9437188
  28.0 8.3 %collective-permute-start.2 = (bf16[64,512]{1,0:T(8,128)(2,1)S(1)}, bf16[64,512]{1,0:T(8,128)(2,1)S(1)}, u32[]{:S(2)}, u32[]{:S(2)}) collective-permute-start(bf16[64,512]{1,0:T(8,128)(2,1)S(1)} %get-tuple-element.67.p0_ref), channel_id=1, source_target_pairs={{0,3},{1,2},{2,1},{3,0},{4,7},{5,6},{6,5},{7,4},{8,11},{9,10},{10,... | collective-permute-start | bytes 196616 | tf_op jit(solution)/shard_map/ppermute | solution.py:634
  31.5 4.7 %collective-permute-start.1 = (bf16[64,512]{1,0:T(8,128)(2,1)S(1)}, bf16[64,512]{1,0:T(8,128)(2,1)S(1)}, u32[]{:S(2)}, u32[]{:S(2)}) collective-permute-start(bf16[64,512]{1,0:T(8,128)(2,1)S(1)} %get-tuple-element.67.p0_ref), channel_id=1, source_target_pairs={{0,1},{1,0},{2,3},{3,2},{4,5},{5,4},{6,7},{7,6},{8,9},{9,8},{10,11... | collective-permute-start | bytes 196616 | tf_op jit(solution)/shard_map/ppermute | solution.py:634
  31.5 4.7 %collective-permute-start = (bf16[64,512]{1,0:T(8,128)(2,1)S(1)}, bf16[64,512]{1,0:T(8,128)(2,1)S(1)}, u32[]{:S(2)}, u32[]{:S(2)}) collective-permute-start(bf16[64,512]{1,0:T(8,128)(2,1)S(1)} %get-tuple-element.67.p0_ref), channel_id=1, source_target_pairs={{0,2},{1,3},{2,0},{3,1},{4,6},{5,7},{6,4},{7,5},{8,10},{9,11},{10,... | collective-permute-start | bytes 196616 | tf_op jit(solution)/shard_map/ppermute | solution.py:634
  40.3 14.5 %copy-start.29 = (bf16[64,1536]{1,0:T(8,128)(2,1)S(1)}, bf16[64,1536]{1,0:T(8,128)(2,1)}, u32[]{:S(2)}) copy-start(bf16[64,1536]{1,0:T(8,128)(2,1)} %copy-done.28) | copy-start | bytes 589828
  42.7 8.7 %collective-permute-start.5 = (bf16[128,4096]{1,0:T(8,128)(2,1)S(1)}, bf16[128,4096]{1,0:T(8,128)(2,1)S(1)}, u32[]{:S(2)}, u32[]{:S(2)}) collective-permute-start(bf16[128,4096]{1,0:T(8,128)(2,1)S(1)} %get-tuple-element.73), channel_id=1, source_target_pairs={{0,1},{1,0},{2,3},{3,2},{4,5},{5,4},{6,7},{7,6},{8,9},{9,8},{10,11... | collective-permute-start | bytes 3145736 | tf_op jit(solution)/shard_map/ppermute | solution.py:634
  44.3 5.1 %collective-permute-start.3 = (f32[128,384]{1,0:T(8,128)S(1)}, f32[128,384]{1,0:T(8,128)S(1)}, u32[]{:S(2)}, u32[]{:S(2)}) collective-permute-start(f32[128,384]{1,0:T(8,128)S(1)} %get-tuple-element.69), channel_id=1, source_target_pairs={{0,1},{1,0},{2,3},{3,2},{4,5},{5,4},{6,7},{7,6},{8,9},{9,8},{10,11... | collective-permute-start | bytes 589832 | tf_op jit(solution)/shard_map/ppermute | solution.py:634
  44.4 14.2 %collective-permute-start.6 = (bf16[96,896]{1,0:T(8,128)(2,1)S(1)}, bf16[96,896]{1,0:T(8,128)(2,1)S(1)}, u32[]{:S(2)}, u32[]{:S(2)}) collective-permute-start(bf16[96,896]{1,0:T(8,128)(2,1)S(1)} %get-tuple-element.85), channel_id=1, source_target_pairs={{0,16},{16,32},{32,48},{48,0},{1,17},{17,33},{33,49},{49,1},{2,18}... | collective-permute-start | bytes 516104 | tf_op jit(solution)/shard_map/ppermute | solution.py:639
  45.9 12.8 %collective-permute-start.7 = (bf16[96,896]{1,0:T(8,128)(2,1)S(1)}, bf16[96,896]{1,0:T(8,128)(2,1)S(1)}, u32[]{:S(2)}, u32[]{:S(2)}) collective-permute-start(bf16[96,896]{1,0:T(8,128)(2,1)S(1)} %get-tuple-element.86), channel_id=1, source_target_pairs={{0,32},{16,48},{32,0},{48,16},{1,33},{17,49},{33,1},{49,17},{2,34}... | collective-permute-start | bytes 516104 | tf_op jit(solution)/shard_map/ppermute | solution.py:639
  48.3 10.4 %collective-permute-start.8 = (bf16[96,896]{1,0:T(8,128)(2,1)S(1)}, bf16[96,896]{1,0:T(8,128)(2,1)S(1)}, u32[]{:S(2)}, u32[]{:S(2)}) collective-permute-start(bf16[96,896]{1,0:T(8,128)(2,1)S(1)} %get-tuple-element.87), channel_id=1, source_target_pairs={{0,48},{16,0},{32,16},{48,32},{1,49},{17,1},{33,17},{49,33},{2,50}... | collective-permute-start | bytes 516104 | tf_op jit(solution)/shard_map/ppermute | solution.py:639
  49.5 5.3 %collective-permute-start.4 = (f32[64,384]{1,0:T(8,128)S(1)}, f32[64,384]{1,0:T(8,128)S(1)}, u32[]{:S(2)}, u32[]{:S(2)}) collective-permute-start(f32[64,384]{1,0:T(8,128)S(1)} %slice_add_fusion.2), channel_id=1, source_target_pairs={{0,2},{2,0},{1,3},{3,1},{4,6},{6,4},{5,7},{7,5},{8,10},{10,8},{9,1... | collective-permute-start | bytes 294920 | tf_op jit(solution)/shard_map/ppermute | solution.py:634
  58.7 18.6 %collective-permute-start.9 = (bf16[1536,384]{1,0:T(8,128)(2,1)S(1)}, bf16[1536,384]{1,0:T(8,128)(2,1)S(1)}, u32[]{:S(2)}, u32[]{:S(2)}) collective-permute-start(bf16[1536,384]{1,0:T(8,128)(2,1)S(1)} %get-tuple-element.88), channel_id=1, source_target_pairs={{0,1},{1,0},{2,3},{3,2},{4,5},{5,4},{6,7},{7,6},{8,9},{9,8},{10,11... | collective-permute-start | bytes 3538952 | tf_op jit(solution)/shard_map/ppermute | solution.py:634
  61.1 16.2 %collective-permute-start.10 = (bf16[64,4096]{1,0:T(8,128)(2,1)S(1)}, bf16[64,4096]{1,0:T(8,128)(2,1)}, u32[]{:S(2)}, u32[]{:S(2)}) collective-permute-start(bf16[64,4096]{1,0:T(8,128)(2,1)S(1)} %fusion.2), channel_id=1, source_target_pairs={{0,2},{2,0},{1,3},{3,1},{4,6},{6,4},{5,7},{7,5},{8,10},{10,8},{9,1... | collective-permute-start | bytes 1572872 | tf_op jit(solution)/shard_map/ppermute | solution.py:634
  63.6 13.6 %collective-permute-start.11 = (bf16[24,896]{1,0:T(8,128)(2,1)S(1)}, bf16[24,896]{1,0:T(8,128)(2,1)S(1)}, u32[]{:S(2)}, u32[]{:S(2)}) collective-permute-start(bf16[24,896]{1,0:T(8,128)(2,1)S(1)} %get-tuple-element.100), channel_id=1, source_target_pairs={{0,4},{4,8},{8,12},{12,0},{1,5},{5,9},{9,13},{13,1},{2,6},{6,10},{... | collective-permute-start | bytes 129032 | tf_op jit(solution)/shard_map/ppermute | solution.py:639
  65.1 12.2 %collective-permute-start.12 = (bf16[24,896]{1,0:T(8,128)(2,1)S(1)}, bf16[24,896]{1,0:T(8,128)(2,1)S(1)}, u32[]{:S(2)}, u32[]{:S(2)}) collective-permute-start(bf16[24,896]{1,0:T(8,128)(2,1)S(1)} %get-tuple-element.101), channel_id=1, source_target_pairs={{0,8},{4,12},{8,0},{12,4},{1,9},{5,13},{9,1},{13,5},{2,10},{6,14},... | collective-permute-start | bytes 129032 | tf_op jit(solution)/shard_map/ppermute | solution.py:639
  67.5 9.8 %collective-permute-start.13 = (bf16[24,896]{1,0:T(8,128)(2,1)S(1)}, bf16[24,896]{1,0:T(8,128)(2,1)S(1)}, u32[]{:S(2)}, u32[]{:S(2)}) collective-permute-start(bf16[24,896]{1,0:T(8,128)(2,1)S(1)} %get-tuple-element.102), channel_id=1, source_target_pairs={{0,12},{4,0},{8,4},{12,8},{1,13},{5,1},{9,5},{13,9},{2,14},{6,2},{... | collective-permute-start | bytes 129032 | tf_op jit(solution)/shard_map/ppermute | solution.py:639
  78.9 26.3 %all-to-all-start.1 = ((bf16[64,80,128]{2,1,0:T(8,128)(2,1)}), bf16[64,80,128]{2,1,0:T(8,128)(2,1)S(1)}, u32[]{:S(2)}, u32[]{:S(2)}) async-start(bf16[64,80,128]{2,1,0:T(8,128)(2,1)} %shard_map.196), calls=%async_computation.1 | async-start | bytes 2621440 | tf_op jit(solution)/shard_map/all_to_all | solution.py:644
  90.3 6.0 %collective-permute-start.20 = (bf16[24,512]{1,0:T(8,128)(2,1)S(1)}, bf16[24,512]{1,0:T(8,128)(2,1)S(1)}, u32[]{:S(2)}, u32[]{:S(2)}) collective-permute-start(bf16[24,512]{1,0:T(8,128)(2,1)S(1)} %get-tuple-element.122), channel_id=1, source_target_pairs={{0,64},{1,65},{2,66},{3,67},{64,0},{65,1},{66,2},{67,3},{4,68},{5,... | collective-permute-start | bytes 73736 | tf_op jit(solution)/shard_map/ppermute | solution.py:634
  91.5 8.8 %collective-permute-start.19 = (bf16[24,512]{1,0:T(8,128)(2,1)S(1)}, bf16[24,512]{1,0:T(8,128)(2,1)S(1)}, u32[]{:S(2)}, u32[]{:S(2)}) collective-permute-start(bf16[24,512]{1,0:T(8,128)(2,1)S(1)} %get-tuple-element.123), channel_id=1, source_target_pairs={{0,2},{1,3},{2,0},{3,1},{64,66},{65,67},{66,64},{67,65},{4,6},{5,7... | collective-permute-start | bytes 73736 | tf_op jit(solution)/shard_map/ppermute | solution.py:634
  93.9 9.0 %collective-permute-start.18 = (bf16[24,512]{1,0:T(8,128)(2,1)S(1)}, bf16[24,512]{1,0:T(8,128)(2,1)S(1)}, u32[]{:S(2)}, u32[]{:S(2)}) collective-permute-start(bf16[24,512]{1,0:T(8,128)(2,1)S(1)} %get-tuple-element.124), channel_id=1, source_target_pairs={{0,66},{1,67},{2,64},{3,65},{64,2},{65,3},{66,0},{67,1},{4,70},{5,... | collective-permute-start | bytes 73736 | tf_op jit(solution)/shard_map/ppermute | solution.py:634
  94.2 8.6 %collective-permute-start.17 = (bf16[24,512]{1,0:T(8,128)(2,1)S(1)}, bf16[24,512]{1,0:T(8,128)(2,1)S(1)}, u32[]{:S(2)}, u32[]{:S(2)}) collective-permute-start(bf16[24,512]{1,0:T(8,128)(2,1)S(1)} %get-tuple-element.125), channel_id=1, source_target_pairs={{0,1},{1,0},{2,3},{3,2},{64,65},{65,64},{66,67},{67,66},{4,5},{5,4... | collective-permute-start | bytes 73736 | tf_op jit(solution)/shard_map/ppermute | solution.py:634
  96.2 6.6 %collective-permute-start.16 = (bf16[24,512]{1,0:T(8,128)(2,1)S(1)}, bf16[24,512]{1,0:T(8,128)(2,1)S(1)}, u32[]{:S(2)}, u32[]{:S(2)}) collective-permute-start(bf16[24,512]{1,0:T(8,128)(2,1)S(1)} %get-tuple-element.126), channel_id=1, source_target_pairs={{0,65},{1,64},{2,67},{3,66},{64,1},{65,0},{66,3},{67,2},{4,69},{5,... | collective-permute-start | bytes 73736 | tf_op jit(solution)/shard_map/ppermute | solution.py:634
  96.3 8.3 %collective-permute-start.15 = (bf16[24,512]{1,0:T(8,128)(2,1)S(1)}, bf16[24,512]{1,0:T(8,128)(2,1)S(1)}, u32[]{:S(2)}, u32[]{:S(2)}) collective-permute-start(bf16[24,512]{1,0:T(8,128)(2,1)S(1)} %get-tuple-element.127), channel_id=1, source_target_pairs={{0,3},{1,2},{2,1},{3,0},{64,67},{65,66},{66,65},{67,64},{4,7},{5,6... | collective-permute-start | bytes 73736 | tf_op jit(solution)/shard_map/ppermute | solution.py:634
  100.3 4.8 %collective-permute-start.14 = (bf16[24,512]{1,0:T(8,128)(2,1)S(1)}, bf16[24,512]{1,0:T(8,128)(2,1)S(1)}, u32[]{:S(2)}, u32[]{:S(2)}) collective-permute-start(bf16[24,512]{1,0:T(8,128)(2,1)S(1)} %get-tuple-element.128), channel_id=1, source_target_pairs={{0,67},{1,66},{2,65},{3,64},{64,3},{65,2},{66,1},{67,0},{4,71},{5,... | collective-permute-start | bytes 73736 | tf_op jit(solution)/shard_map/ppermute | solution.py:634
  107.1 47.1 %all-to-all-start.2 = ((bf16[64,176,128]{2,1,0:T(8,128)(2,1)}), bf16[64,176,128]{2,1,0:T(8,128)(2,1)S(1)}, u32[]{:S(2)}, u32[]{:S(2)}) async-start(bf16[64,176,128]{2,1,0:T(8,128)(2,1)} %copy-done.2), calls=%async_computation.2 | async-start | bytes 5767168 | tf_op jit(solution)/shard_map/all_to_all | solution.py:644
  154.1 6.7 %collective-permute-start.21 = (bf16[64,176,128]{2,1,0:T(8,128)(2,1)S(1)}, bf16[64,176,128]{2,1,0:T(8,128)(2,1)S(1)}, u32[]{:S(2)}, u32[]{:S(2)}) collective-permute-start(bf16[64,176,128]{2,1,0:T(8,128)(2,1)S(1)} %all-to-all-done.2.mine_ref), channel_id=1, source_target_pairs={{0,1},{1,0},{2,3},{3,2},{4,5},{5,4},{6,7},{7,6},{8,9},{9,8},{10,11... | collective-permute-start | bytes 8650760 | tf_op jit(solution)/shard_map/ppermute | solution.py:634
  (30 other events, 223.9 us)

commit v5 on v4

--- a/solution.py
+++ b/solution.py
@@ -34,9 +34,9 @@
 def gelu_parts(u):
     u2 = u * u
     t = jnp.tanh(u * (GELU_A + (GELU_A * GELU_B) * u2))
-    half = 0.5 * (1.0 + t)
+    half = 0.5 * t + 0.5
     value = u * half
-    slope = half + 0.5 * u * (1.0 - t * t) * (GELU_A + (3.0 * GELU_A * GELU_B) * u2)
+    slope = half + value * (1.0 - half) * (2.0 * GELU_A + (6.0 * GELU_A * GELU_B) * u2)
     return value, slope
 
 
@@ -154,23 +154,29 @@
         for lt in range(3):
             lanes = slice(lt * 128, lt * 128 + 128)
             xhat = c[lt] * rstd
-            xhat_ref[lt, rows, :] = xhat
+            xhat_ref[lt, rows, :] = xhat.astype(BF)
             normed = xhat * gain_ref[lanes].reshape(1, 128)
-            norm_ref[n, :, lanes] = normed.astype(BF)
+            norm_ref[n // 2, (n % 2) * 128 : (n % 2) * 128 + 128, lanes] = normed.astype(BF)
             normt_ref[n, lanes, :] = normed.T.astype(BF)
-        toks = pl.ds(pl.multiple_of(n * 8, 8), 8)
+        return carry
+
+    def widen(m, carry):
         for h in range(6):
             hid = slice(h * 256, h * 256 + 256)
-            u = nn(norm_ref[n], win_ref[:, hid]) + bias_ref[hid].reshape(1, 256)
+            u = nn(norm_ref[m], win_ref[:, hid]) + bias_ref[hid].reshape(1, 256)
             value, slope = gelu_parts(u)
-            value = value.astype(BF).astype(F32)
-            hs_ref[toks, hid] = jnp.sum(value.reshape(16, 8, 256), axis=0)
-            gsum_ref[toks, hid] = jnp.sum(slope.reshape(16, 8, 256), axis=0)
+            toks = pl.ds(pl.multiple_of(m * 16, 8), 16)
+            rows = pl.ds(pl.multiple_of(m * 256, 256), 256)
+            hs_ref[toks, hid] = jnp.sum(value.reshape(2, 16, 8, 256), axis=1).reshape(16, 256)
+            gsum_ref[toks, hid] = jnp.sum(slope.reshape(2, 16, 8, 256), axis=1).reshape(16, 256)
             slope_ref[rows, hid] = slope.astype(BF)
         return carry
 
     load_win.wait()
-    lax.fori_loop(0, 8, block, 0, unroll=8)
+    for m in range(4):
+        block(2 * m, 0)
+        block(2 * m + 1, 0)
+        widen(m, 0)
     load_wout.wait()
 
     hs = hs_ref[...]
@@ -202,7 +208,7 @@
         [
             shape((64, 512), BF),
             shape((8, 384, 128), BF),
-            shape((3, 1024, 128), F32),
+            shape((3, 1024, 128), BF),
             shape((1024, 128), F32),
             shape((1024, 1536), BF),
             shape((64, 1536), BF),
@@ -215,7 +221,7 @@
             pltpu.VMEM((3, 3, 2, 4, 16, 8, 128), F32),
             pltpu.VMEM((3, 7, 7, 128), F32),
             pltpu.VMEM((3, 2, 4, 4, 4, 8, 128), F32),
-            pltpu.VMEM((8, 128, 384), BF),
+            pltpu.VMEM((4, 256, 384), BF),
             pltpu.VMEM((64, 1536), F32),
             pltpu.VMEM((2, 16, 32, 384), BF),
             pltpu.VMEM((384, 1536), BF),
@@ -312,8 +318,8 @@
             pick_ref[tok, q * 128 : q * 128 + 128] = jnp.where(
                 lane + q * 128 == want, 1.0, 0.0
             ).astype(BF)
-    for h in range(7):
-        cols = slice(h * 128, h * 128 + 128)
+    for low, high in ((0, 256), (256, 512), (512, 768), (768, 896)):
+        cols = slice(low, high)
         cot = nn(pick_ref[...], cot_ref[:, cols])
         pre = nn(pool_ref[...], wc_ref[:, cols])
         gp_ref[:, cols] = (cot * gelu_parts(pre)[1]).astype(BF)
@@ -351,7 +357,7 @@
     co_ref, near_ref, part_ref, far_ref, normt_ref, slope_ref, hsum_ref, gsum_ref, bsum_ref, wout_ref, scale_ref,
     keep_ref, send_ref, dpre_ref, small_ref, dh_ref,
 ):
-    dtok = (part_ref[0:64, :] + near_ref[0:64, :] + far_ref[...]) * (1.0 / 16.0)
+    dtok = (part_ref[0:64, :] + near_ref[0:64, :] + far_ref[...].astype(F32)) * (1.0 / 16.0)
     small_ref[0:1, :] = jnp.sum(dtok * bsum_ref[...], axis=0, keepdims=True)
     dbr = (dtok * scale_ref[...].reshape(1, 384)).astype(BF)
     dh_ref[...] = nt(dbr, wout_ref[...])
@@ -405,7 +411,7 @@
         [pltpu.VMEM((64, 1536), F32)],
         [smem()] + [vmem()] * 10,
         14,
-        3,
+        12,
     )(co, near, part, far, normt, slope, hsum, gsum, bsum, wout, scale)
 
 
@@ -416,16 +422,14 @@
         t = n // 4
         q = n % 4
         rows = pl.ds(pl.multiple_of(n * 128, 128), 128)
-        dn = nt(dpre_ref[0, rows, :], win_ref[:, 0:384])
-        for h in range(1, 4):
-            dn = dn + nt(dpre_ref[h, rows, :], win_ref[:, h * 384 : h * 384 + 384])
+        dn = dns[n // 2][(n % 2) * 128 : (n % 2) * 128 + 128]
         rstd = rstd_ref[rows, :]
         dx = []
         xh = []
         gains = []
         for lt in range(3):
             lanes = slice(lt * 128, lt * 128 + 128)
-            xhat = xhat_ref[lt, rows, :]
+            xhat = xhat_ref[lt, rows, :].astype(F32)
             part = dn[:, lanes]
             gains.append(jnp.sum((part * xhat).reshape(16, 8, 128), axis=0))
             dx.append(part * gain_ref[lanes].reshape(1, 128))
@@ -444,7 +448,16 @@
         return tuple(c + g for c, g in zip(carry, gains))
 
     zero = jnp.zeros((8, 128), F32)
-    gains = lax.fori_loop(0, 8, block, (zero, zero, zero), unroll=8)
+    gains = (zero, zero, zero)
+    dns = []
+    for m in range(4):
+        part = slice(m * 256, m * 256 + 256)
+        dn = nt(dpre_ref[0, part, :], win_ref[:, 0:384])
+        for h in range(1, 4):
+            dn = dn + nt(dpre_ref[h, part, :], win_ref[:, h * 384 : h * 384 + 384])
+        dns.append(dn)
+        gains = block(2 * m, gains)
+        gains = block(2 * m + 1, gains)
     for lt in range(3):
         lanes = slice(lt * 128, lt * 128 + 128)
         out_ref[49:50, lanes] = jnp.sum(gains[lt], axis=0, keepdims=True)
@@ -545,60 +558,82 @@
     )(parts, *proj)
 
 
-def place_kernel(
-    co_ref, mine_ref, other_ref,
-    in_ref, out_ref, proj_ref, kernel_ref, gain_ref, bias_ref, scale_ref,
+def place_half(src_ref, half, refs, outs, sem):
+    in_ref, out_ref, proj_ref = refs
+
+    def pair(low, high, at):
+        return jnp.concatenate(
+            [
+                src_ref[low, at : at + 24, :].astype(F32),
+                src_ref[high, at : at + 24, :].astype(F32),
+            ],
+            axis=0,
+        ).astype(BF)
+
+    wide = pl.ds(pl.multiple_of(half * 768, 128), 768)
+    tall = pl.ds(pl.multiple_of(half * 768, 128), 768)
+    cols = pl.ds(pl.multiple_of(half * 2048, 128), 2048)
+    copies = [
+        pltpu.make_async_copy(in_ref, outs[0].at[:, wide], sem.at[0]),
+        pltpu.make_async_copy(out_ref, outs[1].at[tall, :], sem.at[1]),
+        pltpu.make_async_copy(proj_ref, outs[2].at[:, cols], sem.at[2]),
+    ]
+    for yl in range(2):
+        for yh in range(2):
+            for p in range(4):
+                col = (yh * 2 + yl) * 512 + p * 128
+                for m in range(8):
+                    n = yl * 32 + 4 * m + yh
+                    proj_ref[m * 48 : m * 48 + 48, col : col + 128] = pair(n, n + 2, 80 + p * 24)
+    copies[2].start()
+    for p in range(3):
+        for m in range(16):
+            out_ref[m * 48 : m * 48 + 48, p * 128 : p * 128 + 128] = pair(
+                32 + 2 * m, 33 + 2 * m, p * 24
+            )
+    copies[1].start()
+    for p in range(3):
+        for m in range(8):
+            for q in range(2):
+                n = q * 16 + 2 * m
+                col = q * 384 + p * 128
+                in_ref[m * 48 : m * 48 + 48, col : col + 128] = pair(n, n + 1, p * 24)
+    copies[0].start()
+    return copies
+
+
+def small_rows(src_ref, n):
+    rows = src_ref[n, 64:80, :].astype(F32)
+    return rows[8:11] + rows[11:14]
+
+
+def place_own_kernel(
+    co_ref, mine_ref, in_hbm, out_hbm, proj_hbm, small_ref, in_ref, out_ref, proj_ref, sem
 ):
-    def put(src_ref, half):
-        def pair(low, high, at):
-            return jnp.concatenate(
-                [
-                    src_ref[low, at : at + 24, :].astype(F32),
-                    src_ref[high, at : at + 24, :].astype(F32),
-                ],
-                axis=0,
-            ).astype(BF)
-
+    copies = place_half(
+        mine_ref, co_ref[0], (in_ref, out_ref, proj_ref), (in_hbm, out_hbm, proj_hbm), sem
+    )
+    for n in range(64):
+        small = small_rows(mine_ref, n)
         for p in range(3):
-            for m in range(8):
-                rows = slice(m * 48, m * 48 + 48)
-                for q in range(2):
-                    n = q * 16 + 2 * m
-                    col = half * 768 + q * 384 + p * 128
-                    in_ref[rows, col : col + 128] = pair(n, n + 1, p * 24)
-            for m in range(16):
-                at = half * 768 + m * 48
-                out_ref[at : at + 48, p * 128 : p * 128 + 128] = pair(
-                    32 + 2 * m, 33 + 2 * m, p * 24
-                )
-        for yl in range(2):
-            for yh in range(2):
-                for p in range(4):
-                    col = (half * 4 + yh * 2 + yl) * 512 + p * 128
-                    for m in range(8):
-                        n = yl * 32 + 4 * m + yh
-                        proj_ref[m * 48 : m * 48 + 48, col : col + 128] = pair(
-                            n, n + 2, 80 + p * 24
-                        )
-
-    low = co_ref[0] == 0
-
-    @pl.when(low)
-    def _():
-        put(mine_ref, 0)
-        put(other_ref, 1)
-
-    @pl.when(jnp.logical_not(low))
-    def _():
-        put(other_ref, 0)
-        put(mine_ref, 1)
-
+            small_ref[n : n + 1, p * 128 : p * 128 + 128] = small[p : p + 1]
+    for copy in copies:
+        copy.wait()
+
+
+def place_other_kernel(
+    co_ref, other_ref, small_ref, in_from, out_from, proj_from,
+    in_hbm, out_hbm, proj_hbm, kernel_ref, gain_ref, bias_ref, scale_ref,
+    in_ref, out_ref, proj_ref, sem,
+):
+    copies = place_half(
+        other_ref, 1 - co_ref[0], (in_ref, out_ref, proj_ref), (in_hbm, out_hbm, proj_hbm), sem
+    )
     for n in range(58):
-        small = mine_ref[n, 64:80, :].astype(F32) + other_ref[n, 64:80, :].astype(F32)
-        small = small[8:11] + small[11:14]
+        small = small_rows(other_ref, n)
         for p in range(3):
             lanes = slice(p * 128, p * 128 + 128)
-            row = small[p : p + 1]
+            row = small[p : p + 1] + small_ref[n : n + 1, lanes]
             if n == 0:
                 scale_ref[lanes] = row.reshape(128)
             elif n < 5:
@@ -608,26 +643,40 @@
             elif n >= 8:
                 a, b = (n - 8) // 7, (n - 8) % 7
                 kernel_ref[a, b : b + 1, lanes] = row
+    for copy in copies:
+        copy.wait()
 
 
 def place(co, mine, other):
     shape = jax.ShapeDtypeStruct
-    return call(
-        place_kernel,
-        [
-            shape((384, 1536), BF),
-            shape((1536, 384), BF),
-            shape((384, 4096), BF),
-            shape((7, 7, 384), F32),
-            shape((384,), F32),
-            shape((1536,), F32),
-            shape((384,), F32),
-        ],
-        [],
-        [smem()] + [vmem()] * 2,
-        14,
-        5,
-    )(co, mine, other)
+    large = [shape((384, 1536), BF), shape((1536, 384), BF), shape((384, 4096), BF)]
+    scratch = [
+        pltpu.VMEM((384, 768), BF),
+        pltpu.VMEM((768, 384), BF),
+        pltpu.VMEM((384, 2048), BF),
+        pltpu.SemaphoreType.DMA((3,)),
+    ]
+    params = pltpu.CompilerParams(vmem_limit_bytes=10 * MIB)
+    *held, small = pl.pallas_call(
+        place_own_kernel,
+        out_shape=large + [shape((64, 384), F32)],
+        in_specs=[smem(), vmem()],
+        out_specs=[hbm()] * 3 + [vmem()],
+        scratch_shapes=scratch,
+        compiler_params=params,
+        cost_estimate=cost(3),
+    )(co, mine)
+    return pl.pallas_call(
+        place_other_kernel,
+        out_shape=large
+        + [shape((7, 7, 384), F32), shape((384,), F32), shape((1536,), F32), shape((384,), F32)],
+        in_specs=[smem(), vmem(), vmem()] + [hbm()] * 3,
+        out_specs=[hbm()] * 3 + [vmem()] * 4,
+        scratch_shapes=scratch,
+        input_output_aliases={3: 0, 4: 1, 5: 2},
+        compiler_params=params,
+        cost_estimate=cost(3),
+    )(co, other, small, *held)
 
 
 def swap(v, axes, size, d):
@@ -690,7 +739,7 @@
     grad_pre, part, give, *outer = connector_part(at, pays, cot, wc)
 
     near = swap(give, "co", 2, 1)
-    far = swap(part[64:] + near[64:], "yh", 2, 1)
+    far = swap((part[64:] + near[64:]).astype(BF), "yh", 2, 1)
     outer = turn(outer, "z")
     row_part, row_give = token_rows(grad_pre, connector)
     row_near = swap(row_give, "co", 2, 1).astype(F32)

time: 166 us -> 164 us (0.988)
  waiting for transfers between devices: 43.7 us -> 40.7 us
    ppermute x16, waiting for transfers between devices: 10.3 us -> 7.21 us  [swap(): return lax.ppermute(v, axes, [(i, i ^ d) for i in range(size)])]
    pallas_call x1 -> x2, Pallas kernels: 4.32 us -> 5.73 us  [the longest x1 3.19 us: place(): pl.pallas_call(place_other_kernel, out_shape=large + [shape((7, 7, 384),...]
where the time goes in v5:
time: 164 us; the launch traced here: 162 us
  starting transfers between devices  63.5 us (39%)
  Pallas kernels  44.8 us (27%)
  waiting for transfers between devices  40.7 us (25%)
  local copies, waits for them, and re-layouts  8.47 us (5%)
  other arithmetic  2.78 us (2%)
  between operations  2.13 us (1%)
    all_to_all x3, waiting for transfers between devices, exchange(): return lax.all_to_all(v, axes, split_axis=0, concat_axis=0, tiled=True)  33.4 us
    all_to_all x3, starting transfers between devices, exchange(): return lax.all_to_all(v, axes, split_axis=0, concat_axis=0, tiled=True)  27.5 us
    ppermute x16, starting transfers between devices, swap(): return lax.ppermute(v, axes, [(i, i ^ d) for i in range(size)])  26.1 us
    pallas_call x1, Pallas kernels, forward(): call(forward_kernel, [shape((64, 512), BF), shape((8, 384, 128), BF), sha...  12.1 us
    ppermute x6, starting transfers between devices, turn(): lax.ppermute(parts[d], axis, [(i, (i + d) % 4) for i in range(4)])  9.84 us
    unnamed x74, local copies, waits for them, and re-layouts  8.08 us
    pallas_call x1, Pallas kernels, front_back(): call(front_back_kernel, jax.ShapeDtypeStruct((56, 384), F32), [pltpu.VMEM...  7.79 us
    ppermute x16, waiting for transfers between devices, swap(): return lax.ppermute(v, axes, [(i, i ^ d) for i in range(size)])  7.21 us
  transfers between devices with their start and end apart: 25, of which 5 were waited for; matrix products, arithmetic and copies ran while one was open for 2% of the time, Pallas kernels for 20%

profile of v5, /device:TPU:1, one launch (start us, length us, event | category | flops | bytes accessed | tf_op | source)
XLA Modules:
  0.0 162.3 jit_solution(8984064672277398907)
XLA Ops:
  2.0 1.7 %shard_map.188 = bf16[512,896]{1,0:T(8,128)(2,1)} custom-call(bf16[512,896]{1,0:T(8,128)(2,1)S(1)} %copy-done.10), custom_call_target="tpu_custom_call" | custom-call | flops 2200000000 | bytes 1 | tf_op jit(solution)/shard_map/pallas_call | solution.py:713
  3.7 9.8 %all-to-all-start = ((bf16[32,16,896]{2,1,0:T(8,128)(2,1)}), bf16[32,16,896]{2,1,0:T(8,128)(2,1)}, u32[]{:S(2)}, u32[]{:S(2)}) async-start(bf16[32,16,896]{2,1,0:T(8,128)(2,1)} %bitcast.8), calls=%async_computation | async-start | bytes 1835008 | tf_op jit(solution)/shard_map/all_to_all | solution.py:693
  14.7 12.1 %shard_map.189 = (bf16[64,512]{1,0:T(8,128)(2,1)S(1)}, bf16[8,384,128]{2,1,0:T(8,128)(2,1)S(1)}, bf16[3,1024,128]{2,1,0:T(8,128)(2,1)S(1)}, f32[1024,128]{1,0:T(...) custom-call(bf16[2,16,32,384]{3,2,1,0:T(8,128)(2,1)S(1)} %copy-done., ...), custom_call_target="tpu_custom_call" | custom-call | flops 15400000512 | bytes 1 | tf_op jit(solution)/shard_map/pallas_call | solution.py:206
  26.9 3.5 %collective-permute-start.2 = (bf16[64,512]{1,0:T(8,128)(2,1)S(1)}, bf16[64,512]{1,0:T(8,128)(2,1)S(1)}, u32[]{:S(2)}, u32[]{:S(2)}) collective-permute-start(bf16[64,512]{1,0:T(8,128)(2,1)S(1)} %get-tuple-element.71.p0_ref), channel_id=1, source_target_pairs={{0,3},{1,2},{2,1},{3,0},{4,7},{5,6},{6,5},{7,4},{8,11},{9,10},{10,... | collective-permute-start | bytes 196616 | tf_op jit(solution)/shard_map/ppermute | solution.py:683
  30.8 3.4 %shard_map.190.wc_ref = bf16[384,896]{1,0:T(8,128)(2,1)S(1)} custom-call(bf16[384,4096]{1,0:T(8,128)(2,1)S(1)} %copy-done.1, bf16[4096,896]{1,0:T(8,128)(2,1)S(1)} %bitcast.29), custom_call_target="tpu_custom_call" | custom-call | flops 1 | bytes 1 | tf_op jit(solution)/shard_map/pallas_call | solution.py:243
  36.3 2.6 %shard_map.191 = (bf16[256,896]{1,0:T(8,128)(2,1)S(1)}, f32[128,384]{1,0:T(8,128)S(1)}, f32[128,384]{1,0:T(8,128)S(1)}, bf16[96,896]{1,0:T(8,128)(2,1)S(1)}, bf1...) custom-call(s32[6]{0:T(128)S(1)} %stack.27.at_ref.co_ref, ...), custom_call_target="tpu_custom_call" | custom-call | flops 3300000000 | bytes 1 | tf_op jit(solution)/shard_map/pallas_call | solution.py:337
  38.9 2.4 %shard_map.192 = (bf16[128,4096]{1,0:T(8,128)(2,1)S(1)}, bf16[128,4096]{1,0:T(8,128)(2,1)S(1)}) custom-call(bf16[256,896]{1,0:T(8,128)(2,1)S(1)} %get-tuple-element.75.gp_ref, bf16[4096,896]{1,0:T(8,128)(2,1)S(1)} %bitcast.31), custom_call_target="tpu_custom_call" | custom-call | flops 1 | bytes 1 | tf_op jit(solution)/shard_map/pallas_call | solution.py:258
  41.3 1.6 collective-permute-start.5
  44.5 2.4 %collective-permute-start.7 = (bf16[96,896]{1,0:T(8,128)(2,1)S(1)}, bf16[96,896]{1,0:T(8,128)(2,1)S(1)}, u32[]{:S(2)}, u32[]{:S(2)}) collective-permute-start(bf16[96,896]{1,0:T(8,128)(2,1)S(1)} %get-tuple-element.90), channel_id=1, source_target_pairs={{0,32},{16,48},{32,0},{48,16},{1,33},{17,49},{33,1},{49,17},{2,34}... | collective-permute-start | bytes 516104 | tf_op jit(solution)/shard_map/ppermute | solution.py:688
  48.1 1.9 %collective-permute-start.4 = (bf16[64,384]{1,0:T(8,128)(2,1)S(1)}, bf16[64,384]{1,0:T(8,128)(2,1)S(1)}, u32[]{:S(2)}, u32[]{:S(2)}) collective-permute-start(bf16[64,384]{1,0:T(8,128)(2,1)S(1)} %fusion.3), channel_id=1, source_target_pairs={{0,2},{2,0},{1,3},{3,1},{4,6},{6,4},{5,7},{7,5},{8,10},{10,8},{9,1... | collective-permute-start | bytes 147464 | tf_op jit(solution)/shard_map/ppermute | solution.py:683
  50.4 2.6 %collective-permute-done.4.far_ref = bf16[64,384]{1,0:T(8,128)(2,1)S(1)} collective-permute-done((bf16[64,384]{1,0:T(8,128)(2,1)S(1)}, bf16[64,384]{1,0:T(8,128)(2,1)S(1)}, u32[]{:S(2)}, u32[]{:S(2)}) %collective-permute-start.4) | collective-permute-done | bytes 49184 | tf_op jit(solution)/shard_map/ppermute | solution.py:683
  53.0 3.7 %shard_map.193 = (bf16[1536,384]{1,0:T(8,128)(2,1)S(1)}, bf16[1536,384]{1,0:T(8,128)(2,1)S(1)}, bf16[4,1024,384]{2,1,0:T(8,128)(2,1)S(1)}, f32[8,384]{1,0:T(8,128)S(1)}) custom-call(s32[6]{0:T(128)S(1)} %stack.27.at_ref.co_ref, f32[128,384]{1,0:T(8,128)S(1)} %collective-permute-done.3.near_ref, f32[128,384]{1,0:T(8,128)S(1)} %get-tuple-element.74.part_ref, ...), custom_call_target="tpu_custom_call" | custom-call | flops 13200000000 | bytes 1 | tf_op jit(solution)/shard_map/pallas_call | solution.py:403
  56.7 2.4 %collective-permute-start.9 = (bf16[1536,384]{1,0:T(8,128)(2,1)S(1)}, bf16[1536,384]{1,0:T(8,128)(2,1)S(1)}, u32[]{:S(2)}, u32[]{:S(2)}) collective-permute-start(bf16[1536,384]{1,0:T(8,128)(2,1)S(1)} %get-tuple-element.92), channel_id=1, source_target_pairs={{0,1},{1,0},{2,3},{3,2},{4,5},{5,4},{6,7},{7,6},{8,9},{9,8},{10,11... | collective-permute-start | bytes 3538952 | tf_op jit(solution)/shard_map/ppermute | solution.py:683
  59.1 1.9 %collective-permute-start.10 = (bf16[64,4096]{1,0:T(8,128)(2,1)S(1)}, bf16[64,4096]{1,0:T(8,128)(2,1)}, u32[]{:S(2)}, u32[]{:S(2)}) collective-permute-start(bf16[64,4096]{1,0:T(8,128)(2,1)S(1)} %fusion.2), channel_id=1, source_target_pairs={{0,2},{2,0},{1,3},{3,1},{4,6},{6,4},{5,7},{7,5},{8,10},{10,8},{9,1... | collective-permute-start | bytes 1572872 | tf_op jit(solution)/shard_map/ppermute | solution.py:683
  62.9 2.4 %collective-permute-start.12 = (bf16[24,896]{1,0:T(8,128)(2,1)S(1)}, bf16[24,896]{1,0:T(8,128)(2,1)S(1)}, u32[]{:S(2)}, u32[]{:S(2)}) collective-permute-start(bf16[24,896]{1,0:T(8,128)(2,1)S(1)} %get-tuple-element.105), channel_id=1, source_target_pairs={{0,8},{4,12},{8,0},{12,4},{1,9},{5,13},{9,1},{13,5},{2,10},{6,14},... | collective-permute-start | bytes 129032 | tf_op jit(solution)/shard_map/ppermute | solution.py:688
  66.5 7.8 %shard_map.194.b_ref = f32[56,384]{1,0:T(8,128)S(1)} custom-call(bf16[4,1024,384]{2,1,0:T(8,128)(2,1)S(1)} %get-tuple-element.94.dpre_ref, bf16[384,1536]{1,0:T(8,128)(2,1)S(1)} %copy-done.9, bf16[3,1024,128]{2,1,0:T(8,128)(2,1)S(1)} %copy-done.17, f32[1024,128]{1,0:T(8,128)S(1)} %copy-done.21, f32[384]{0:T(512)S(1)} %copy-done.15, ...), custom_call_target="tpu_custom_call" | custom-call | flops 2200000000 | bytes 1 | tf_op jit(solution)/shard_map/pallas_call | solution.py:497
  75.9 6.5 %all-to-all-start.1 = ((bf16[64,80,128]{2,1,0:T(8,128)(2,1)}), bf16[64,80,128]{2,1,0:T(8,128)(2,1)S(1)}, u32[]{:S(2)}, u32[]{:S(2)}) async-start(bf16[64,80,128]{2,1,0:T(8,128)(2,1)} %shard_map.196), calls=%async_computation.1 | async-start | bytes 2621440 | tf_op jit(solution)/shard_map/all_to_all | solution.py:693
  82.4 3.1 %copy-done = bf16[4096,896]{1,0:T(8,128)(2,1)S(1)} copy-done((bf16[4096,896]{1,0:T(8,128)(2,1)S(1)}, bf16[4096,896]{1,0:T(8,128)(2,1)}, u32[]{:S(2)}) %copy-start) | copy-done | bytes 7340056
  85.5 2.8 %shard_map.197 = bf16[8,24,512]{2,1,0:T(8,128)(2,1)S(1)} custom-call(s32[6]{0:T(128)S(1)} %stack.27.at_ref.co_ref, bf16[24,896]{1,0:T(8,128)(2,1)S(1)} %get-tuple-element.112.r0_ref, bf16[24,896]{1,0:T(8,128)(2,1)S(1)} %collective-permute-done.11.r1_ref, bf16[24,896]{1,0:T(8,128)(2,1)S(1)} %collective-permute-done.12.r2_ref, ...), custom_call_target="tpu_custom_call" | custom-call | flops 1 | bytes 1 | tf_op jit(solution)/shard_map/pallas_call | solution.py:294
  89.5 2.4 %collective-permute-start.19 = (bf16[24,512]{1,0:T(8,128)(2,1)S(1)}, bf16[24,512]{1,0:T(8,128)(2,1)S(1)}, u32[]{:S(2)}, u32[]{:S(2)}) collective-permute-start(bf16[24,512]{1,0:T(8,128)(2,1)S(1)} %get-tuple-element.131), channel_id=1, source_target_pairs={{0,2},{1,3},{2,0},{3,1},{64,66},{65,67},{66,64},{67,65},{4,6},{5,7... | collective-permute-start | bytes 73736 | tf_op jit(solution)/shard_map/ppermute | solution.py:683
  92.3 2.0 %collective-permute-start.17 = (bf16[24,512]{1,0:T(8,128)(2,1)S(1)}, bf16[24,512]{1,0:T(8,128)(2,1)S(1)}, u32[]{:S(2)}, u32[]{:S(2)}) collective-permute-start(bf16[24,512]{1,0:T(8,128)(2,1)S(1)} %get-tuple-element.133), channel_id=1, source_target_pairs={{0,1},{1,0},{2,3},{3,2},{64,65},{65,64},{66,67},{67,66},{4,5},{5,4... | collective-permute-start | bytes 73736 | tf_op jit(solution)/shard_map/ppermute | solution.py:683
  94.4 4.0 %collective-permute-start.15 = (bf16[24,512]{1,0:T(8,128)(2,1)S(1)}, bf16[24,512]{1,0:T(8,128)(2,1)S(1)}, u32[]{:S(2)}, u32[]{:S(2)}) collective-permute-start(bf16[24,512]{1,0:T(8,128)(2,1)S(1)} %get-tuple-element.135), channel_id=1, source_target_pairs={{0,3},{1,2},{2,1},{3,0},{64,67},{65,66},{66,65},{67,64},{4,7},{5,6... | collective-permute-start | bytes 73736 | tf_op jit(solution)/shard_map/ppermute | solution.py:683
  98.4 2.6 %collective-permute-start.14 = (bf16[24,512]{1,0:T(8,128)(2,1)S(1)}, bf16[24,512]{1,0:T(8,128)(2,1)S(1)}, u32[]{:S(2)}, u32[]{:S(2)}) collective-permute-start(bf16[24,512]{1,0:T(8,128)(2,1)S(1)} %get-tuple-element.136), channel_id=1, source_target_pairs={{0,67},{1,66},{2,65},{3,64},{64,3},{65,2},{66,1},{67,0},{4,71},{5,... | collective-permute-start | bytes 73736 | tf_op jit(solution)/shard_map/ppermute | solution.py:683
  100.9 1.7 %collective-permute-done.15.refs_2_ = bf16[24,512]{1,0:T(8,128)(2,1)S(1)} collective-permute-done((bf16[24,512]{1,0:T(8,128)(2,1)S(1)}, bf16[24,512]{1,0:T(8,128)(2,1)S(1)}, u32[]{:S(2)}, u32[]{:S(2)}) %collective-permute-start.15) | collective-permute-done | bytes 24608 | tf_op jit(solution)/shard_map/ppermute | solution.py:683
  103.6 1.6 copy-done.2
  105.2 11.2 %all-to-all-start.2 = ((bf16[64,176,128]{2,1,0:T(8,128)(2,1)}), bf16[64,176,128]{2,1,0:T(8,128)(2,1)S(1)}, u32[]{:S(2)}, u32[]{:S(2)}) async-start(bf16[64,176,128]{2,1,0:T(8,128)(2,1)} %copy-done.2), calls=%async_computation.2 | async-start | bytes 5767168 | tf_op jit(solution)/shard_map/all_to_all | solution.py:693
  116.3 2.5 %fusion.1 = bf16[64,4096]{1,0:T(8,128)(2,1)} fusion(f32[128,4096]{1,0:T(8,128)} %copy-done.30, bf16[64,4096]{1,0:T(8,128)(2,1)} %collective-permute-done.10, bf16[128,4096]{1,0:T(8,128)(2,1)} %copy-done.3), kind=kLoop, calls=%fused_computation.2 | loop fusion | flops 1310720 | bytes 2621440 | tf_op jit(solution)/shard_map/convert_element_type | solution.py:769
  118.8 33.4 %all-to-all-done.2.mine_ref = bf16[64,176,128]{2,1,0:T(8,128)(2,1)S(1)} async-done(((bf16[64,176,128]{2,1,0:T(8,128)(2,1)}), bf16[64,176,128]{2,1,0:T(8,128)(2,1)S(1)}, u32[]{:S(2)}, u32[]{:S(2)}) %all-to-all-start.2) | async-done | bytes 2883616 | tf_op jit(solution)/shard_map/all_to_all | solution.py:693
  152.2 1.8 %collective-permute-start.21 = (bf16[64,176,128]{2,1,0:T(8,128)(2,1)S(1)}, bf16[64,176,128]{2,1,0:T(8,128)(2,1)S(1)}, u32[]{:S(2)}, u32[]{:S(2)}) collective-permute-start(bf16[64,176,128]{2,1,0:T(8,128)(2,1)S(1)} %all-to-all-done.2.mine_ref), channel_id=1, source_target_pairs={{0,1},{1,0},{2,3},{3,2},{4,5},{5,4},{6,7},{7,6},{8,9},{9,8},{10,11... | collective-permute-start | bytes 8650760 | tf_op jit(solution)/shard_map/ppermute | solution.py:683
  154.0 2.5 %shard_map.199 = (bf16[384,1536]{1,0:T(8,128)(2,1)}, bf16[1536,384]{1,0:T(8,128)(2,1)}, bf16[384,4096]{1,0:T(8,128)(2,1)}, f32[64,384]{1,0:T(8,128)S(1)}) custom-call(s32[6]{0:T(128)S(1)} %stack.27.at_ref.co_ref, bf16[64,176,128]{2,1,0:T(8,128)(2,1)S(1)} %all-to-all-done.2.mine_ref), custom_call_target="tpu_custom_call" | custom-call | flops 3300000000 | bytes 1 | tf_op jit(solution)/shard_map/pallas_call | solution.py:660
  156.5 2.4 %collective-permute-done.21.other_ref = bf16[64,176,128]{2,1,0:T(8,128)(2,1)S(1)} collective-permute-done((bf16[64,176,128]{2,1,0:T(8,128)(2,1)S(1)}, bf16[64,176,128]{2,1,0:T(8,128)(2,1)S(1)}, u32[]{:S(2)}, u32[]{:S(2)}) %collective-permute-start.21) | collective-permute-done | bytes 2883616 | tf_op jit(solution)/shard_map/ppermute | solution.py:683
  158.9 3.2 %shard_map.200 = (bf16[384,1536]{1,0:T(8,128)(2,1)}, bf16[1536,384]{1,0:T(8,128)(2,1)}, bf16[384,4096]{1,0:T(8,128)(2,1)}, f32[7,7,384]{2,1,0:T(8,128)}, f32[384]{0:T(512)}, /*index=5*/f32[1536]{0:T(1024)}, f32[384]{0:T(512)}) custom-call(s32[6]{0:T(128)S(1)} %stack.27.at_ref.co_ref, ...), custom_call_target="tpu_custom_call", output_to_operand_aliasing={{0}: (3, {}), {1}: (4, {}), {2}: (5, {})} | custom-call | flops 3300000000 | bytes 1 | tf_op jit(solution)/shard_map/pallas_call | solution.py:669
  (117 shorter events, 14.4 us)
Async XLA Ops:
  0.6 13.9 %copy-start.6 = (bf16[1536,384]{1,0:T(8,128)(2,1)S(1)}, bf16[1536,384]{1,0:T(8,128)(2,1)}, u32[]{:S(2)}) copy-start(bf16[1536,384]{1,0:T(8,128)(2,1)} %wout_ref.1) | copy-start | bytes 3538948
  0.6 13.9 %copy-start.8 = (bf16[384,1536]{1,0:T(8,128)(2,1)S(1)}, bf16[384,1536]{1,0:T(8,128)(2,1)}, u32[]{:S(2)}) copy-start(bf16[384,1536]{1,0:T(8,128)(2,1)} %win_ref.1) | copy-start | bytes 3538948
  2.0 12.6 %copy-start.13 = (f32[1536]{0:T(1024)S(1)}, f32[1536]{0:T(1024)}, u32[]{:S(2)}) copy-start(f32[1536]{0:T(1024)} %bias_ref.1) | copy-start | bytes 18436
  3.7 31.5 %all-to-all-start = ((bf16[32,16,896]{2,1,0:T(8,128)(2,1)}), bf16[32,16,896]{2,1,0:T(8,128)(2,1)}, u32[]{:S(2)}, u32[]{:S(2)}) async-start(bf16[32,16,896]{2,1,0:T(8,128)(2,1)} %bitcast.8), calls=%async_computation | async-start | bytes 1835008 | tf_op jit(solution)/shard_map/all_to_all | solution.py:693
  14.5 16.3 %slice-start = ((s8[7340032]{0:T(1024)(128)(4,1)}), s8[4194304]{0:T(1024)(128)(4,1)S(1)}, s32[]{:S(2)}) async-start(s8[7340032]{0:T(1024)(128)(4,1)} %bitcast.28), calls=%async_computation.3 | async-start | bytes 8388608
  14.6 16.2 %slice-start.1 = ((s8[7340032]{0:T(1024)(128)(4,1)}), s8[3145728]{0:T(1024)(128)(4,1)S(1)}, s32[]{:S(2)}) async-start(s8[7340032]{0:T(1024)(128)(4,1)} %bitcast.28), calls=%async_computation.4 | async-start | bytes 6291456
  14.7 16.1 %copy-start.1 = (bf16[384,4096]{1,0:T(8,128)(2,1)S(1)}, bf16[384,4096]{1,0:T(8,128)(2,1)}, u32[]{:S(2)}) copy-start(bf16[384,4096]{1,0:T(8,128)(2,1)} %proj_ref) | copy-start | bytes 9437188
  26.9 8.3 %collective-permute-start.2 = (bf16[64,512]{1,0:T(8,128)(2,1)S(1)}, bf16[64,512]{1,0:T(8,128)(2,1)S(1)}, u32[]{:S(2)}, u32[]{:S(2)}) collective-permute-start(bf16[64,512]{1,0:T(8,128)(2,1)S(1)} %get-tuple-element.71.p0_ref), channel_id=1, source_target_pairs={{0,3},{1,2},{2,1},{3,0},{4,7},{5,6},{6,5},{7,4},{8,11},{9,10},{10,... | collective-permute-start | bytes 196616 | tf_op jit(solution)/shard_map/ppermute | solution.py:683
  30.4 4.7 %collective-permute-start.1 = (bf16[64,512]{1,0:T(8,128)(2,1)S(1)}, bf16[64,512]{1,0:T(8,128)(2,1)S(1)}, u32[]{:S(2)}, u32[]{:S(2)}) collective-permute-start(bf16[64,512]{1,0:T(8,128)(2,1)S(1)} %get-tuple-element.71.p0_ref), channel_id=1, source_target_pairs={{0,1},{1,0},{2,3},{3,2},{4,5},{5,4},{6,7},{7,6},{8,9},{9,8},{10,11... | collective-permute-start | bytes 196616 | tf_op jit(solution)/shard_map/ppermute | solution.py:683
  30.4 4.7 %collective-permute-start = (bf16[64,512]{1,0:T(8,128)(2,1)S(1)}, bf16[64,512]{1,0:T(8,128)(2,1)S(1)}, u32[]{:S(2)}, u32[]{:S(2)}) collective-permute-start(bf16[64,512]{1,0:T(8,128)(2,1)S(1)} %get-tuple-element.71.p0_ref), channel_id=1, source_target_pairs={{0,2},{1,3},{2,0},{3,1},{4,6},{5,7},{6,4},{7,5},{8,10},{9,11},{10,... | collective-permute-start | bytes 196616 | tf_op jit(solution)/shard_map/ppermute | solution.py:683
  38.9 14.0 %copy-start.27 = (f32[64,1536]{1,0:T(8,128)S(1)}, f32[64,1536]{1,0:T(8,128)}, u32[]{:S(2)}) copy-start(f32[64,1536]{1,0:T(8,128)} %copy-done.26) | copy-start | bytes 1179652
  41.3 8.7 %collective-permute-start.5 = (bf16[128,4096]{1,0:T(8,128)(2,1)S(1)}, bf16[128,4096]{1,0:T(8,128)(2,1)S(1)}, u32[]{:S(2)}, u32[]{:S(2)}) collective-permute-start(bf16[128,4096]{1,0:T(8,128)(2,1)S(1)} %get-tuple-element.77), channel_id=1, source_target_pairs={{0,1},{1,0},{2,3},{3,2},{4,5},{5,4},{6,7},{7,6},{8,9},{9,8},{10,11... | collective-permute-start | bytes 3145736 | tf_op jit(solution)/shard_map/ppermute | solution.py:683
  42.9 5.1 %collective-permute-start.3 = (f32[128,384]{1,0:T(8,128)S(1)}, f32[128,384]{1,0:T(8,128)S(1)}, u32[]{:S(2)}, u32[]{:S(2)}) collective-permute-start(f32[128,384]{1,0:T(8,128)S(1)} %get-tuple-element.73), channel_id=1, source_target_pairs={{0,1},{1,0},{2,3},{3,2},{4,5},{5,4},{6,7},{7,6},{8,9},{9,8},{10,11... | collective-permute-start | bytes 589832 | tf_op jit(solution)/shard_map/ppermute | solution.py:683
  43.0 13.7 %collective-permute-start.6 = (bf16[96,896]{1,0:T(8,128)(2,1)S(1)}, bf16[96,896]{1,0:T(8,128)(2,1)S(1)}, u32[]{:S(2)}, u32[]{:S(2)}) collective-permute-start(bf16[96,896]{1,0:T(8,128)(2,1)S(1)} %get-tuple-element.89), channel_id=1, source_target_pairs={{0,16},{16,32},{32,48},{48,0},{1,17},{17,33},{33,49},{49,1},{2,18}... | collective-permute-start | bytes 516104 | tf_op jit(solution)/shard_map/ppermute | solution.py:688
  44.5 12.3 %collective-permute-start.7 = (bf16[96,896]{1,0:T(8,128)(2,1)S(1)}, bf16[96,896]{1,0:T(8,128)(2,1)S(1)}, u32[]{:S(2)}, u32[]{:S(2)}) collective-permute-start(bf16[96,896]{1,0:T(8,128)(2,1)S(1)} %get-tuple-element.90), channel_id=1, source_target_pairs={{0,32},{16,48},{32,0},{48,16},{1,33},{17,49},{33,1},{49,17},{2,34}... | collective-permute-start | bytes 516104 | tf_op jit(solution)/shard_map/ppermute | solution.py:688
  46.9 9.9 %collective-permute-start.8 = (bf16[96,896]{1,0:T(8,128)(2,1)S(1)}, bf16[96,896]{1,0:T(8,128)(2,1)S(1)}, u32[]{:S(2)}, u32[]{:S(2)}) collective-permute-start(bf16[96,896]{1,0:T(8,128)(2,1)S(1)} %get-tuple-element.91), channel_id=1, source_target_pairs={{0,48},{16,0},{32,16},{48,32},{1,49},{17,1},{33,17},{49,33},{2,50}... | collective-permute-start | bytes 516104 | tf_op jit(solution)/shard_map/ppermute | solution.py:688
  48.1 4.8 %collective-permute-start.4 = (bf16[64,384]{1,0:T(8,128)(2,1)S(1)}, bf16[64,384]{1,0:T(8,128)(2,1)S(1)}, u32[]{:S(2)}, u32[]{:S(2)}) collective-permute-start(bf16[64,384]{1,0:T(8,128)(2,1)S(1)} %fusion.3), channel_id=1, source_target_pairs={{0,2},{2,0},{1,3},{3,1},{4,6},{6,4},{5,7},{7,5},{8,10},{10,8},{9,1... | collective-permute-start | bytes 147464 | tf_op jit(solution)/shard_map/ppermute | solution.py:683
  56.7 17.6 %collective-permute-start.9 = (bf16[1536,384]{1,0:T(8,128)(2,1)S(1)}, bf16[1536,384]{1,0:T(8,128)(2,1)S(1)}, u32[]{:S(2)}, u32[]{:S(2)}) collective-permute-start(bf16[1536,384]{1,0:T(8,128)(2,1)S(1)} %get-tuple-element.92), channel_id=1, source_target_pairs={{0,1},{1,0},{2,3},{3,2},{4,5},{5,4},{6,7},{7,6},{8,9},{9,8},{10,11... | collective-permute-start | bytes 3538952 | tf_op jit(solution)/shard_map/ppermute | solution.py:683
  59.1 15.2 %collective-permute-start.10 = (bf16[64,4096]{1,0:T(8,128)(2,1)S(1)}, bf16[64,4096]{1,0:T(8,128)(2,1)}, u32[]{:S(2)}, u32[]{:S(2)}) collective-permute-start(bf16[64,4096]{1,0:T(8,128)(2,1)S(1)} %fusion.2), channel_id=1, source_target_pairs={{0,2},{2,0},{1,3},{3,1},{4,6},{6,4},{5,7},{7,5},{8,10},{10,8},{9,1... | collective-permute-start | bytes 1572872 | tf_op jit(solution)/shard_map/ppermute | solution.py:683
  61.7 12.6 %collective-permute-start.11 = (bf16[24,896]{1,0:T(8,128)(2,1)S(1)}, bf16[24,896]{1,0:T(8,128)(2,1)S(1)}, u32[]{:S(2)}, u32[]{:S(2)}) collective-permute-start(bf16[24,896]{1,0:T(8,128)(2,1)S(1)} %get-tuple-element.104), channel_id=1, source_target_pairs={{0,4},{4,8},{8,12},{12,0},{1,5},{5,9},{9,13},{13,1},{2,6},{6,10},{... | collective-permute-start | bytes 129032 | tf_op jit(solution)/shard_map/ppermute | solution.py:688
  62.9 11.4 %collective-permute-start.12 = (bf16[24,896]{1,0:T(8,128)(2,1)S(1)}, bf16[24,896]{1,0:T(8,128)(2,1)S(1)}, u32[]{:S(2)}, u32[]{:S(2)}) collective-permute-start(bf16[24,896]{1,0:T(8,128)(2,1)S(1)} %get-tuple-element.105), channel_id=1, source_target_pairs={{0,8},{4,12},{8,0},{12,4},{1,9},{5,13},{9,1},{13,5},{2,10},{6,14},... | collective-permute-start | bytes 129032 | tf_op jit(solution)/shard_map/ppermute | solution.py:688
  65.3 9.0 %collective-permute-start.13 = (bf16[24,896]{1,0:T(8,128)(2,1)S(1)}, bf16[24,896]{1,0:T(8,128)(2,1)S(1)}, u32[]{:S(2)}, u32[]{:S(2)}) collective-permute-start(bf16[24,896]{1,0:T(8,128)(2,1)S(1)} %get-tuple-element.106), channel_id=1, source_target_pairs={{0,12},{4,0},{8,4},{12,8},{1,13},{5,1},{9,5},{13,9},{2,14},{6,2},{... | collective-permute-start | bytes 129032 | tf_op jit(solution)/shard_map/ppermute | solution.py:688
  75.9 27.3 %all-to-all-start.1 = ((bf16[64,80,128]{2,1,0:T(8,128)(2,1)}), bf16[64,80,128]{2,1,0:T(8,128)(2,1)S(1)}, u32[]{:S(2)}, u32[]{:S(2)}) async-start(bf16[64,80,128]{2,1,0:T(8,128)(2,1)} %shard_map.196), calls=%async_computation.1 | async-start | bytes 2621440 | tf_op jit(solution)/shard_map/all_to_all | solution.py:693
  88.4 6.0 %collective-permute-start.20 = (bf16[24,512]{1,0:T(8,128)(2,1)S(1)}, bf16[24,512]{1,0:T(8,128)(2,1)S(1)}, u32[]{:S(2)}, u32[]{:S(2)}) collective-permute-start(bf16[24,512]{1,0:T(8,128)(2,1)S(1)} %get-tuple-element.130), channel_id=1, source_target_pairs={{0,64},{1,65},{2,66},{3,67},{64,0},{65,1},{66,2},{67,3},{4,68},{5,... | collective-permute-start | bytes 73736 | tf_op jit(solution)/shard_map/ppermute | solution.py:683
  89.5 8.8 %collective-permute-start.19 = (bf16[24,512]{1,0:T(8,128)(2,1)S(1)}, bf16[24,512]{1,0:T(8,128)(2,1)S(1)}, u32[]{:S(2)}, u32[]{:S(2)}) collective-permute-start(bf16[24,512]{1,0:T(8,128)(2,1)S(1)} %get-tuple-element.131), channel_id=1, source_target_pairs={{0,2},{1,3},{2,0},{3,1},{64,66},{65,67},{66,64},{67,65},{4,6},{5,7... | collective-permute-start | bytes 73736 | tf_op jit(solution)/shard_map/ppermute | solution.py:683
  91.9 9.0 %collective-permute-start.18 = (bf16[24,512]{1,0:T(8,128)(2,1)S(1)}, bf16[24,512]{1,0:T(8,128)(2,1)S(1)}, u32[]{:S(2)}, u32[]{:S(2)}) collective-permute-start(bf16[24,512]{1,0:T(8,128)(2,1)S(1)} %get-tuple-element.132), channel_id=1, source_target_pairs={{0,66},{1,67},{2,64},{3,65},{64,2},{65,3},{66,0},{67,1},{4,70},{5,... | collective-permute-start | bytes 73736 | tf_op jit(solution)/shard_map/ppermute | solution.py:683
  92.3 8.6 %collective-permute-start.17 = (bf16[24,512]{1,0:T(8,128)(2,1)S(1)}, bf16[24,512]{1,0:T(8,128)(2,1)S(1)}, u32[]{:S(2)}, u32[]{:S(2)}) collective-permute-start(bf16[24,512]{1,0:T(8,128)(2,1)S(1)} %get-tuple-element.133), channel_id=1, source_target_pairs={{0,1},{1,0},{2,3},{3,2},{64,65},{65,64},{66,67},{67,66},{4,5},{5,4... | collective-permute-start | bytes 73736 | tf_op jit(solution)/shard_map/ppermute | solution.py:683
  94.3 6.6 %collective-permute-start.16 = (bf16[24,512]{1,0:T(8,128)(2,1)S(1)}, bf16[24,512]{1,0:T(8,128)(2,1)S(1)}, u32[]{:S(2)}, u32[]{:S(2)}) collective-permute-start(bf16[24,512]{1,0:T(8,128)(2,1)S(1)} %get-tuple-element.134), channel_id=1, source_target_pairs={{0,65},{1,64},{2,67},{3,66},{64,1},{65,0},{66,3},{67,2},{4,69},{5,... | collective-permute-start | bytes 73736 | tf_op jit(solution)/shard_map/ppermute | solution.py:683
  94.4 8.3 %collective-permute-start.15 = (bf16[24,512]{1,0:T(8,128)(2,1)S(1)}, bf16[24,512]{1,0:T(8,128)(2,1)S(1)}, u32[]{:S(2)}, u32[]{:S(2)}) collective-permute-start(bf16[24,512]{1,0:T(8,128)(2,1)S(1)} %get-tuple-element.135), channel_id=1, source_target_pairs={{0,3},{1,2},{2,1},{3,0},{64,67},{65,66},{66,65},{67,64},{4,7},{5,6... | collective-permute-start | bytes 73736 | tf_op jit(solution)/shard_map/ppermute | solution.py:683
  98.4 4.8 %collective-permute-start.14 = (bf16[24,512]{1,0:T(8,128)(2,1)S(1)}, bf16[24,512]{1,0:T(8,128)(2,1)S(1)}, u32[]{:S(2)}, u32[]{:S(2)}) collective-permute-start(bf16[24,512]{1,0:T(8,128)(2,1)S(1)} %get-tuple-element.136), channel_id=1, source_target_pairs={{0,67},{1,66},{2,65},{3,64},{64,3},{65,2},{66,1},{67,0},{4,71},{5,... | collective-permute-start | bytes 73736 | tf_op jit(solution)/shard_map/ppermute | solution.py:683
  105.2 47.0 %all-to-all-start.2 = ((bf16[64,176,128]{2,1,0:T(8,128)(2,1)}), bf16[64,176,128]{2,1,0:T(8,128)(2,1)S(1)}, u32[]{:S(2)}, u32[]{:S(2)}) async-start(bf16[64,176,128]{2,1,0:T(8,128)(2,1)} %copy-done.2), calls=%async_computation.2 | async-start | bytes 5767168 | tf_op jit(solution)/shard_map/all_to_all | solution.py:693
  152.2 6.7 %collective-permute-start.21 = (bf16[64,176,128]{2,1,0:T(8,128)(2,1)S(1)}, bf16[64,176,128]{2,1,0:T(8,128)(2,1)S(1)}, u32[]{:S(2)}, u32[]{:S(2)}) collective-permute-start(bf16[64,176,128]{2,1,0:T(8,128)(2,1)S(1)} %all-to-all-done.2.mine_ref), channel_id=1, source_target_pairs={{0,1},{1,0},{2,3},{3,2},{4,5},{5,4},{6,7},{7,6},{8,9},{9,8},{10,11... | collective-permute-start | bytes 8650760 | tf_op jit(solution)/shard_map/ppermute | solution.py:683
  (30 other events, 215.9 us)

commit v6 on v5

--- a/solution.py
+++ b/solution.py
@@ -742,10 +742,10 @@
     far = swap((part[64:] + near[64:]).astype(BF), "yh", 2, 1)
     outer = turn(outer, "z")
     row_part, row_give = token_rows(grad_pre, connector)
-    row_near = swap(row_give, "co", 2, 1).astype(F32)
-    row_tail = (row_part[64:].astype(F32) + row_near[64:]).astype(BF)
-    near, far, row_tail = lax.optimization_barrier((near, far, row_tail))
-    row_far = swap(row_tail, "yh", 2, 1)
+    near, far, row_part, row_give = lax.optimization_barrier((near, far, row_part, row_give))
+    row_near = swap(row_give, "co", 2, 1)
+    row_tail = row_part[64:].astype(F32) + row_near[64:].astype(F32)
+    row_far = swap(row_tail.astype(BF), "yh", 2, 1)
     keep, send, dpre, small_a = mlp_back(
         at, near, part, far, normt, slope, hsum, gsum, bsum, weight_out, layer_scale
     )
@@ -766,7 +766,8 @@
     shards = settle(parts, proj)
     whole = exchange(shards, SAME_CORE)
 
-    token_grads = (row_part[:64].astype(F32) + row_near[:64] + row_far.astype(F32)).astype(BF)
+    token_grads = row_part[:64].astype(F32) + row_near[:64].astype(F32) + row_far.astype(F32)
+    token_grads = token_grads.astype(BF)
     whole, token_grads = lax.optimization_barrier((whole, token_grads))
     grad_in, grad_out, grad_proj, grad_kernel, grad_gain, grad_bias, grad_scale = place(
         at, whole, swap(whole, "co", 2, 1)

time: 164 us -> 162 us (0.988)
    all_to_all x3, starting transfers between devices: 27.5 us -> 29.1 us  [exchange(): return lax.all_to_all(v, axes, split_axis=0, concat_axis=0, tiled=True)]
  transfers between devices with their start and end apart: 25 -> 25, of which waited for: 5 -> 6; matrix products, arithmetic and copies ran while one was open for 2% -> 2% of each run, Pallas kernels for 20% -> 22%
where the time goes in v6:
time: 162 us; the launch traced here: 161 us
  starting transfers between devices  63.8 us (39%)
  Pallas kernels  44.8 us (28%)
  waiting for transfers between devices  39.8 us (25%)
  local copies, waits for them, and re-layouts  8.3 us (5%)
  other arithmetic  2.49 us (2%)
  between operations  2.05 us (1%)
    all_to_all x3, waiting for transfers between devices, exchange(): return lax.all_to_all(v, axes, split_axis=0, concat_axis=0, tiled=True)  33.5 us
    all_to_all x3, starting transfers between devices, exchange(): return lax.all_to_all(v, axes, split_axis=0, concat_axis=0, tiled=True)  29.1 us
    ppermute x16, starting transfers between devices, swap(): return lax.ppermute(v, axes, [(i, i ^ d) for i in range(size)])  24.8 us
    pallas_call x1, Pallas kernels, forward(): call(forward_kernel, [shape((64, 512), BF), shape((8, 384, 128), BF), sha...  12.1 us
    ppermute x6, starting transfers between devices, turn(): lax.ppermute(parts[d], axis, [(i, (i + d) % 4) for i in range(4)])  9.85 us
    unnamed x74, local copies, waits for them, and re-layouts  7.92 us
    pallas_call x1, Pallas kernels, front_back(): call(front_back_kernel, jax.ShapeDtypeStruct((56, 384), F32), [pltpu.VMEM...  7.8 us
    ppermute x16, waiting for transfers between devices, swap(): return lax.ppermute(v, axes, [(i, i ^ d) for i in range(size)])  6.19 us
  transfers between devices with their start and end apart: 25, of which 6 were waited for; matrix products, arithmetic and copies ran while one was open for 2% of the time, Pallas kernels for 22%

profile of v6, /device:TPU:1, one launch (start us, length us, event | category | flops | bytes accessed | tf_op | source)
XLA Modules:
  0.0 161.2 jit_solution(6196314238182860293)
XLA Ops:
  1.8 1.7 %shard_map.188 = bf16[512,896]{1,0:T(8,128)(2,1)} custom-call(bf16[512,896]{1,0:T(8,128)(2,1)S(1)} %copy-done.10), custom_call_target="tpu_custom_call" | custom-call | flops 2200000000 | bytes 1 | tf_op jit(solution)/shard_map/pallas_call | solution.py:713
  3.5 10.0 %all-to-all-start = ((bf16[32,16,896]{2,1,0:T(8,128)(2,1)}), bf16[32,16,896]{2,1,0:T(8,128)(2,1)}, u32[]{:S(2)}, u32[]{:S(2)}) async-start(bf16[32,16,896]{2,1,0:T(8,128)(2,1)} %bitcast.8), calls=%async_computation | async-start | bytes 1835008 | tf_op jit(solution)/shard_map/all_to_all | solution.py:693
  14.6 12.1 %shard_map.189 = (bf16[64,512]{1,0:T(8,128)(2,1)S(1)}, bf16[8,384,128]{2,1,0:T(8,128)(2,1)S(1)}, bf16[3,1024,128]{2,1,0:T(8,128)(2,1)S(1)}, f32[1024,128]{1,0:T(...) custom-call(bf16[2,16,32,384]{3,2,1,0:T(8,128)(2,1)S(1)} %copy-done., ...), custom_call_target="tpu_custom_call" | custom-call | flops 15400000512 | bytes 1 | tf_op jit(solution)/shard_map/pallas_call | solution.py:206
  26.9 3.5 %collective-permute-start.2 = (bf16[64,512]{1,0:T(8,128)(2,1)S(1)}, bf16[64,512]{1,0:T(8,128)(2,1)S(1)}, u32[]{:S(2)}, u32[]{:S(2)}) collective-permute-start(bf16[64,512]{1,0:T(8,128)(2,1)S(1)} %get-tuple-element.72.p0_ref), channel_id=1, source_target_pairs={{0,3},{1,2},{2,1},{3,0},{4,7},{5,6},{6,5},{7,4},{8,11},{9,10},{10,... | collective-permute-start | bytes 196616 | tf_op jit(solution)/shard_map/ppermute | solution.py:683
  30.8 3.4 %shard_map.190.wc_ref = bf16[384,896]{1,0:T(8,128)(2,1)S(1)} custom-call(bf16[384,4096]{1,0:T(8,128)(2,1)S(1)} %copy-done.1, bf16[4096,896]{1,0:T(8,128)(2,1)S(1)} %bitcast.29), custom_call_target="tpu_custom_call" | custom-call | flops 1 | bytes 1 | tf_op jit(solution)/shard_map/pallas_call | solution.py:243
  36.2 2.6 %shard_map.191 = (bf16[256,896]{1,0:T(8,128)(2,1)S(1)}, f32[128,384]{1,0:T(8,128)S(1)}, f32[128,384]{1,0:T(8,128)S(1)}, bf16[96,896]{1,0:T(8,128)(2,1)S(1)}, bf1...) custom-call(s32[6]{0:T(128)S(1)} %stack.27.at_ref.co_ref, ...), custom_call_target="tpu_custom_call" | custom-call | flops 3300000000 | bytes 1 | tf_op jit(solution)/shard_map/pallas_call | solution.py:337
  38.8 1.6 %collective-permute-start.3 = (f32[128,384]{1,0:T(8,128)S(1)}, f32[128,384]{1,0:T(8,128)S(1)}, u32[]{:S(2)}, u32[]{:S(2)}) collective-permute-start(f32[128,384]{1,0:T(8,128)S(1)} %get-tuple-element.74), channel_id=1, source_target_pairs={{0,1},{1,0},{2,3},{3,2},{4,5},{5,4},{6,7},{7,6},{8,9},{9,8},{10,11... | collective-permute-start | bytes 589832 | tf_op jit(solution)/shard_map/ppermute | solution.py:683
  41.6 1.9 %collective-permute-start.4 = (bf16[64,384]{1,0:T(8,128)(2,1)S(1)}, bf16[64,384]{1,0:T(8,128)(2,1)S(1)}, u32[]{:S(2)}, u32[]{:S(2)}) collective-permute-start(bf16[64,384]{1,0:T(8,128)(2,1)S(1)} %fusion), channel_id=1, source_target_pairs={{0,2},{2,0},{1,3},{3,1},{4,6},{6,4},{5,7},{7,5},{8,10},{10,8},{9,1... | collective-permute-start | bytes 147464 | tf_op jit(solution)/shard_map/ppermute | solution.py:683
  43.5 1.4 collective-permute-start.5
  44.9 2.4 %collective-permute-start.6 = (bf16[96,896]{1,0:T(8,128)(2,1)S(1)}, bf16[96,896]{1,0:T(8,128)(2,1)S(1)}, u32[]{:S(2)}, u32[]{:S(2)}) collective-permute-start(bf16[96,896]{1,0:T(8,128)(2,1)S(1)} %get-tuple-element.91), channel_id=1, source_target_pairs={{0,32},{16,48},{32,0},{48,16},{1,33},{17,49},{33,1},{49,17},{2,34}... | collective-permute-start | bytes 516104 | tf_op jit(solution)/shard_map/ppermute | solution.py:688
  48.6 2.4 %shard_map.192 = (bf16[128,4096]{1,0:T(8,128)(2,1)S(1)}, bf16[128,4096]{1,0:T(8,128)(2,1)S(1)}) custom-call(bf16[256,896]{1,0:T(8,128)(2,1)S(1)} %get-tuple-element.76.gp_ref, bf16[4096,896]{1,0:T(8,128)(2,1)S(1)} %bitcast.31), custom_call_target="tpu_custom_call" | custom-call | flops 1 | bytes 1 | tf_op jit(solution)/shard_map/pallas_call | solution.py:258
  51.0 1.6 collective-permute-start.9
  52.6 3.7 %shard_map.193 = (bf16[1536,384]{1,0:T(8,128)(2,1)S(1)}, bf16[1536,384]{1,0:T(8,128)(2,1)S(1)}, bf16[4,1024,384]{2,1,0:T(8,128)(2,1)S(1)}, f32[8,384]{1,0:T(8,128)S(1)}) custom-call(s32[6]{0:T(128)S(1)} %stack.27.at_ref.co_ref, f32[128,384]{1,0:T(8,128)S(1)} %collective-permute-done.3.near_ref, f32[128,384]{1,0:T(8,128)S(1)} %get-tuple-element.75.part_ref, ...), custom_call_target="tpu_custom_call" | custom-call | flops 13200000000 | bytes 1 | tf_op jit(solution)/shard_map/pallas_call | solution.py:403
  59.9 2.4 %collective-permute-start.12 = (bf16[24,896]{1,0:T(8,128)(2,1)S(1)}, bf16[24,896]{1,0:T(8,128)(2,1)S(1)}, u32[]{:S(2)}, u32[]{:S(2)}) collective-permute-start(bf16[24,896]{1,0:T(8,128)(2,1)S(1)} %get-tuple-element.107), channel_id=1, source_target_pairs={{0,8},{4,12},{8,0},{12,4},{1,9},{5,13},{9,1},{13,5},{2,10},{6,14},... | collective-permute-start | bytes 129032 | tf_op jit(solution)/shard_map/ppermute | solution.py:688
  63.5 7.8 %shard_map.194.b_ref = f32[56,384]{1,0:T(8,128)S(1)} custom-call(bf16[4,1024,384]{2,1,0:T(8,128)(2,1)S(1)} %get-tuple-element.95.dpre_ref, bf16[384,1536]{1,0:T(8,128)(2,1)S(1)} %copy-done.9, bf16[3,1024,128]{2,1,0:T(8,128)(2,1)S(1)} %copy-done.17, f32[1024,128]{1,0:T(8,128)S(1)} %copy-done.21, f32[384]{0:T(512)S(1)} %copy-done.15, ...), custom_call_target="tpu_custom_call" | custom-call | flops 2200000000 | bytes 1 | tf_op jit(solution)/shard_map/pallas_call | solution.py:497
  71.7 1.6 shard_map.196
  73.3 8.0 %all-to-all-start.1 = ((bf16[64,80,128]{2,1,0:T(8,128)(2,1)}), bf16[64,80,128]{2,1,0:T(8,128)(2,1)S(1)}, u32[]{:S(2)}, u32[]{:S(2)}) async-start(bf16[64,80,128]{2,1,0:T(8,128)(2,1)} %shard_map.196), calls=%async_computation.1 | async-start | bytes 2621440 | tf_op jit(solution)/shard_map/all_to_all | solution.py:693
  81.3 3.1 %copy-done = bf16[4096,896]{1,0:T(8,128)(2,1)S(1)} copy-done((bf16[4096,896]{1,0:T(8,128)(2,1)S(1)}, bf16[4096,896]{1,0:T(8,128)(2,1)}, u32[]{:S(2)}) %copy-start) | copy-done | bytes 7340056
  84.4 2.8 %shard_map.197 = bf16[8,24,512]{2,1,0:T(8,128)(2,1)S(1)} custom-call(s32[6]{0:T(128)S(1)} %stack.27.at_ref.co_ref, bf16[24,896]{1,0:T(8,128)(2,1)S(1)} %get-tuple-element.114.r0_ref, bf16[24,896]{1,0:T(8,128)(2,1)S(1)} %collective-permute-done.11.r1_ref, bf16[24,896]{1,0:T(8,128)(2,1)S(1)} %collective-permute-done.12.r2_ref, ...), custom_call_target="tpu_custom_call" | custom-call | flops 1 | bytes 1 | tf_op jit(solution)/shard_map/pallas_call | solution.py:294
  88.4 2.4 %collective-permute-start.19 = (bf16[24,512]{1,0:T(8,128)(2,1)S(1)}, bf16[24,512]{1,0:T(8,128)(2,1)S(1)}, u32[]{:S(2)}, u32[]{:S(2)}) collective-permute-start(bf16[24,512]{1,0:T(8,128)(2,1)S(1)} %get-tuple-element.133), channel_id=1, source_target_pairs={{0,2},{1,3},{2,0},{3,1},{64,66},{65,67},{66,64},{67,65},{4,6},{5,7... | collective-permute-start | bytes 73736 | tf_op jit(solution)/shard_map/ppermute | solution.py:683
  91.2 1.9 %collective-permute-start.17 = (bf16[24,512]{1,0:T(8,128)(2,1)S(1)}, bf16[24,512]{1,0:T(8,128)(2,1)S(1)}, u32[]{:S(2)}, u32[]{:S(2)}) collective-permute-start(bf16[24,512]{1,0:T(8,128)(2,1)S(1)} %get-tuple-element.135), channel_id=1, source_target_pairs={{0,1},{1,0},{2,3},{3,2},{64,65},{65,64},{66,67},{67,66},{4,5},{5,4... | collective-permute-start | bytes 73736 | tf_op jit(solution)/shard_map/ppermute | solution.py:683
  93.2 4.0 %collective-permute-start.15 = (bf16[24,512]{1,0:T(8,128)(2,1)S(1)}, bf16[24,512]{1,0:T(8,128)(2,1)S(1)}, u32[]{:S(2)}, u32[]{:S(2)}) collective-permute-start(bf16[24,512]{1,0:T(8,128)(2,1)S(1)} %get-tuple-element.137), channel_id=1, source_target_pairs={{0,3},{1,2},{2,1},{3,0},{64,67},{65,66},{66,65},{67,64},{4,7},{5,6... | collective-permute-start | bytes 73736 | tf_op jit(solution)/shard_map/ppermute | solution.py:683
  97.2 2.5 %collective-permute-start.14 = (bf16[24,512]{1,0:T(8,128)(2,1)S(1)}, bf16[24,512]{1,0:T(8,128)(2,1)S(1)}, u32[]{:S(2)}, u32[]{:S(2)}) collective-permute-start(bf16[24,512]{1,0:T(8,128)(2,1)S(1)} %get-tuple-element.138), channel_id=1, source_target_pairs={{0,67},{1,66},{2,65},{3,64},{64,3},{65,2},{66,1},{67,0},{4,71},{5,... | collective-permute-start | bytes 73736 | tf_op jit(solution)/shard_map/ppermute | solution.py:683
  99.7 1.8 %collective-permute-done.15.refs_2_ = bf16[24,512]{1,0:T(8,128)(2,1)S(1)} collective-permute-done((bf16[24,512]{1,0:T(8,128)(2,1)S(1)}, bf16[24,512]{1,0:T(8,128)(2,1)S(1)}, u32[]{:S(2)}, u32[]{:S(2)}) %collective-permute-start.15) | collective-permute-done | bytes 24608 | tf_op jit(solution)/shard_map/ppermute | solution.py:683
  102.5 1.6 copy-done.2
  104.0 11.2 %all-to-all-start.2 = ((bf16[64,176,128]{2,1,0:T(8,128)(2,1)}), bf16[64,176,128]{2,1,0:T(8,128)(2,1)S(1)}, u32[]{:S(2)}, u32[]{:S(2)}) async-start(bf16[64,176,128]{2,1,0:T(8,128)(2,1)} %copy-done.2), calls=%async_computation.2 | async-start | bytes 5767168 | tf_op jit(solution)/shard_map/all_to_all | solution.py:693
  115.2 2.3 %add_convert_fusion = bf16[64,4096]{1,0:T(8,128)(2,1)} fusion(bf16[64,4096]{1,0:T(8,128)(2,1)} %collective-permute-done.10, bf16[128,4096]{1,0:T(8,128)(2,1)} %copy-done.30, bf16[128,4096]{1,0:T(8,128)(2,1)} %copy-done.3), kind=kLoop, calls=%fused_computation | loop fusion | flops 1572864 | bytes 2097152 | tf_op jit(solution)/shard_map/convert_element_type | solution.py:770
  117.6 33.5 %all-to-all-done.2.mine_ref = bf16[64,176,128]{2,1,0:T(8,128)(2,1)S(1)} async-done(((bf16[64,176,128]{2,1,0:T(8,128)(2,1)}), bf16[64,176,128]{2,1,0:T(8,128)(2,1)S(1)}, u32[]{:S(2)}, u32[]{:S(2)}) %all-to-all-start.2) | async-done | bytes 2883616 | tf_op jit(solution)/shard_map/all_to_all | solution.py:693
  151.1 1.8 %collective-permute-start.21 = (bf16[64,176,128]{2,1,0:T(8,128)(2,1)S(1)}, bf16[64,176,128]{2,1,0:T(8,128)(2,1)S(1)}, u32[]{:S(2)}, u32[]{:S(2)}) collective-permute-start(bf16[64,176,128]{2,1,0:T(8,128)(2,1)S(1)} %all-to-all-done.2.mine_ref), channel_id=1, source_target_pairs={{0,1},{1,0},{2,3},{3,2},{4,5},{5,4},{6,7},{7,6},{8,9},{9,8},{10,11... | collective-permute-start | bytes 8650760 | tf_op jit(solution)/shard_map/ppermute | solution.py:683
  152.9 2.5 %shard_map.199 = (bf16[384,1536]{1,0:T(8,128)(2,1)}, bf16[1536,384]{1,0:T(8,128)(2,1)}, bf16[384,4096]{1,0:T(8,128)(2,1)}, f32[64,384]{1,0:T(8,128)S(1)}) custom-call(s32[6]{0:T(128)S(1)} %stack.27.at_ref.co_ref, bf16[64,176,128]{2,1,0:T(8,128)(2,1)S(1)} %all-to-all-done.2.mine_ref), custom_call_target="tpu_custom_call" | custom-call | flops 3300000000 | bytes 1 | tf_op jit(solution)/shard_map/pallas_call | solution.py:660
  155.4 2.4 %collective-permute-done.21.other_ref = bf16[64,176,128]{2,1,0:T(8,128)(2,1)S(1)} collective-permute-done((bf16[64,176,128]{2,1,0:T(8,128)(2,1)S(1)}, bf16[64,176,128]{2,1,0:T(8,128)(2,1)S(1)}, u32[]{:S(2)}, u32[]{:S(2)}) %collective-permute-start.21) | collective-permute-done | bytes 2883616 | tf_op jit(solution)/shard_map/ppermute | solution.py:683
  157.8 3.2 %shard_map.200 = (bf16[384,1536]{1,0:T(8,128)(2,1)}, bf16[1536,384]{1,0:T(8,128)(2,1)}, bf16[384,4096]{1,0:T(8,128)(2,1)}, f32[7,7,384]{2,1,0:T(8,128)}, f32[384]{0:T(512)}, /*index=5*/f32[1536]{0:T(1024)}, f32[384]{0:T(512)}) custom-call(s32[6]{0:T(128)S(1)} %stack.27.at_ref.co_ref, ...), custom_call_target="tpu_custom_call", output_to_operand_aliasing={{0}: (3, {}), {1}: (4, {}), {2}: (5, {})} | custom-call | flops 3300000000 | bytes 1 | tf_op jit(solution)/shard_map/pallas_call | solution.py:669
  (116 shorter events, 13.9 us)
Async XLA Ops:
  1.8 12.7 %copy-start.8 = (bf16[384,1536]{1,0:T(8,128)(2,1)S(1)}, bf16[384,1536]{1,0:T(8,128)(2,1)}, u32[]{:S(2)}) copy-start(bf16[384,1536]{1,0:T(8,128)(2,1)} %win_ref.1) | copy-start | bytes 3538948
  1.8 12.7 %copy-start.11 = (bf16[2,16,32,384]{3,2,1,0:T(8,128)(2,1)S(1)}, bf16[2,16,32,384]{3,2,1,0:T(8,128)(2,1)}, u32[]{:S(2)}) copy-start(bf16[2,16,32,384]{3,2,1,0:T(8,128)(2,1)} %x_hbm) | copy-start | bytes 2359300
  3.5 31.6 %all-to-all-start = ((bf16[32,16,896]{2,1,0:T(8,128)(2,1)}), bf16[32,16,896]{2,1,0:T(8,128)(2,1)}, u32[]{:S(2)}, u32[]{:S(2)}) async-start(bf16[32,16,896]{2,1,0:T(8,128)(2,1)} %bitcast.8), calls=%async_computation | async-start | bytes 1835008 | tf_op jit(solution)/shard_map/all_to_all | solution.py:693
  14.5 16.3 %slice-start = ((s8[7340032]{0:T(1024)(128)(4,1)}), s8[4194304]{0:T(1024)(128)(4,1)S(1)}, s32[]{:S(2)}) async-start(s8[7340032]{0:T(1024)(128)(4,1)} %bitcast.28), calls=%async_computation.3 | async-start | bytes 8388608
  14.6 16.1 %slice-start.1 = ((s8[7340032]{0:T(1024)(128)(4,1)}), s8[3145728]{0:T(1024)(128)(4,1)S(1)}, s32[]{:S(2)}) async-start(s8[7340032]{0:T(1024)(128)(4,1)} %bitcast.28), calls=%async_computation.4 | async-start | bytes 6291456
  14.6 16.1 %copy-start.1 = (bf16[384,4096]{1,0:T(8,128)(2,1)S(1)}, bf16[384,4096]{1,0:T(8,128)(2,1)}, u32[]{:S(2)}) copy-start(bf16[384,4096]{1,0:T(8,128)(2,1)} %proj_ref) | copy-start | bytes 9437188
  26.9 8.2 %collective-permute-start.2 = (bf16[64,512]{1,0:T(8,128)(2,1)S(1)}, bf16[64,512]{1,0:T(8,128)(2,1)S(1)}, u32[]{:S(2)}, u32[]{:S(2)}) collective-permute-start(bf16[64,512]{1,0:T(8,128)(2,1)S(1)} %get-tuple-element.72.p0_ref), channel_id=1, source_target_pairs={{0,3},{1,2},{2,1},{3,0},{4,7},{5,6},{6,5},{7,4},{8,11},{9,10},{10,... | collective-permute-start | bytes 196616 | tf_op jit(solution)/shard_map/ppermute | solution.py:683
  30.4 4.7 %collective-permute-start.1 = (bf16[64,512]{1,0:T(8,128)(2,1)S(1)}, bf16[64,512]{1,0:T(8,128)(2,1)S(1)}, u32[]{:S(2)}, u32[]{:S(2)}) collective-permute-start(bf16[64,512]{1,0:T(8,128)(2,1)S(1)} %get-tuple-element.72.p0_ref), channel_id=1, source_target_pairs={{0,1},{1,0},{2,3},{3,2},{4,5},{5,4},{6,7},{7,6},{8,9},{9,8},{10,11... | collective-permute-start | bytes 196616 | tf_op jit(solution)/shard_map/ppermute | solution.py:683
  30.4 4.7 %collective-permute-start = (bf16[64,512]{1,0:T(8,128)(2,1)S(1)}, bf16[64,512]{1,0:T(8,128)(2,1)S(1)}, u32[]{:S(2)}, u32[]{:S(2)}) collective-permute-start(bf16[64,512]{1,0:T(8,128)(2,1)S(1)} %get-tuple-element.72.p0_ref), channel_id=1, source_target_pairs={{0,2},{1,3},{2,0},{3,1},{4,6},{5,7},{6,4},{7,5},{8,10},{9,11},{10,... | collective-permute-start | bytes 196616 | tf_op jit(solution)/shard_map/ppermute | solution.py:683
  30.8 17.7 %slice-start.2 = ((s8[7340032]{0:T(1024)(128)(4,1)}), s8[3145728]{0:T(1024)(128)(4,1)S(1)}, s32[]{:S(2)}) async-start(s8[7340032]{0:T(1024)(128)(4,1)} %bitcast.30), calls=%async_computation.5 | async-start | bytes 6291456
  38.8 2.7 %collective-permute-start.3 = (f32[128,384]{1,0:T(8,128)S(1)}, f32[128,384]{1,0:T(8,128)S(1)}, u32[]{:S(2)}, u32[]{:S(2)}) collective-permute-start(f32[128,384]{1,0:T(8,128)S(1)} %get-tuple-element.74), channel_id=1, source_target_pairs={{0,1},{1,0},{2,3},{3,2},{4,5},{5,4},{6,7},{7,6},{8,9},{9,8},{10,11... | collective-permute-start | bytes 589832 | tf_op jit(solution)/shard_map/ppermute | solution.py:683
  41.6 9.4 %collective-permute-start.4 = (bf16[64,384]{1,0:T(8,128)(2,1)S(1)}, bf16[64,384]{1,0:T(8,128)(2,1)S(1)}, u32[]{:S(2)}, u32[]{:S(2)}) collective-permute-start(bf16[64,384]{1,0:T(8,128)(2,1)S(1)} %fusion), channel_id=1, source_target_pairs={{0,2},{2,0},{1,3},{3,1},{4,6},{6,4},{5,7},{7,5},{8,10},{10,8},{9,1... | collective-permute-start | bytes 147464 | tf_op jit(solution)/shard_map/ppermute | solution.py:683
  43.5 12.8 %collective-permute-start.5 = (bf16[96,896]{1,0:T(8,128)(2,1)S(1)}, bf16[96,896]{1,0:T(8,128)(2,1)S(1)}, u32[]{:S(2)}, u32[]{:S(2)}) collective-permute-start(bf16[96,896]{1,0:T(8,128)(2,1)S(1)} %get-tuple-element.90), channel_id=1, source_target_pairs={{0,16},{16,32},{32,48},{48,0},{1,17},{17,33},{33,49},{49,1},{2,18}... | collective-permute-start | bytes 516104 | tf_op jit(solution)/shard_map/ppermute | solution.py:688
  44.9 11.4 %collective-permute-start.6 = (bf16[96,896]{1,0:T(8,128)(2,1)S(1)}, bf16[96,896]{1,0:T(8,128)(2,1)S(1)}, u32[]{:S(2)}, u32[]{:S(2)}) collective-permute-start(bf16[96,896]{1,0:T(8,128)(2,1)S(1)} %get-tuple-element.91), channel_id=1, source_target_pairs={{0,32},{16,48},{32,0},{48,16},{1,33},{17,49},{33,1},{49,17},{2,34}... | collective-permute-start | bytes 516104 | tf_op jit(solution)/shard_map/ppermute | solution.py:688
  47.3 9.0 %collective-permute-start.7 = (bf16[96,896]{1,0:T(8,128)(2,1)S(1)}, bf16[96,896]{1,0:T(8,128)(2,1)S(1)}, u32[]{:S(2)}, u32[]{:S(2)}) collective-permute-start(bf16[96,896]{1,0:T(8,128)(2,1)S(1)} %get-tuple-element.92), channel_id=1, source_target_pairs={{0,48},{16,0},{32,16},{48,32},{1,49},{17,1},{33,17},{49,33},{2,50}... | collective-permute-start | bytes 516104 | tf_op jit(solution)/shard_map/ppermute | solution.py:688
  51.0 5.7 %collective-permute-start.9 = (bf16[128,4096]{1,0:T(8,128)(2,1)S(1)}, bf16[128,4096]{1,0:T(8,128)(2,1)S(1)}, u32[]{:S(2)}, u32[]{:S(2)}) collective-permute-start(bf16[128,4096]{1,0:T(8,128)(2,1)S(1)} %get-tuple-element.100), channel_id=1, source_target_pairs={{0,1},{1,0},{2,3},{3,2},{4,5},{5,4},{6,7},{7,6},{8,9},{9,8},{10,11... | collective-permute-start | bytes 3145736 | tf_op jit(solution)/shard_map/ppermute | solution.py:683
  56.3 15.4 %collective-permute-start.8 = (bf16[1536,384]{1,0:T(8,128)(2,1)S(1)}, bf16[1536,384]{1,0:T(8,128)(2,1)S(1)}, u32[]{:S(2)}, u32[]{:S(2)}) collective-permute-start(bf16[1536,384]{1,0:T(8,128)(2,1)S(1)} %get-tuple-element.93), channel_id=1, source_target_pairs={{0,1},{1,0},{2,3},{3,2},{4,5},{5,4},{6,7},{7,6},{8,9},{9,8},{10,11... | collective-permute-start | bytes 3538952 | tf_op jit(solution)/shard_map/ppermute | solution.py:683
  56.6 14.7 %copy-start.30 = (bf16[128,4096]{1,0:T(8,128)(2,1)}, bf16[128,4096]{1,0:T(8,128)(2,1)S(1)}, u32[]{:S(2)}) copy-start(bf16[128,4096]{1,0:T(8,128)(2,1)S(1)} %collective-permute-done.9) | copy-start | bytes 3145732
  56.8 14.9 %collective-permute-start.10 = (bf16[64,4096]{1,0:T(8,128)(2,1)S(1)}, bf16[64,4096]{1,0:T(8,128)(2,1)}, u32[]{:S(2)}, u32[]{:S(2)}) collective-permute-start(bf16[64,4096]{1,0:T(8,128)(2,1)S(1)} %add_convert_fusion.1), channel_id=1, source_target_pairs={{0,2},{2,0},{1,3},{3,1},{4,6},{6,4},{5,7},{7,5},{8,10},{10,8},{9,1... | collective-permute-start | bytes 1572872 | tf_op jit(solution)/shard_map/ppermute | solution.py:683
  58.7 12.7 %collective-permute-start.11 = (bf16[24,896]{1,0:T(8,128)(2,1)S(1)}, bf16[24,896]{1,0:T(8,128)(2,1)S(1)}, u32[]{:S(2)}, u32[]{:S(2)}) collective-permute-start(bf16[24,896]{1,0:T(8,128)(2,1)S(1)} %get-tuple-element.106), channel_id=1, source_target_pairs={{0,4},{4,8},{8,12},{12,0},{1,5},{5,9},{9,13},{13,1},{2,6},{6,10},{... | collective-permute-start | bytes 129032 | tf_op jit(solution)/shard_map/ppermute | solution.py:688
  59.9 11.4 %collective-permute-start.12 = (bf16[24,896]{1,0:T(8,128)(2,1)S(1)}, bf16[24,896]{1,0:T(8,128)(2,1)S(1)}, u32[]{:S(2)}, u32[]{:S(2)}) collective-permute-start(bf16[24,896]{1,0:T(8,128)(2,1)S(1)} %get-tuple-element.107), channel_id=1, source_target_pairs={{0,8},{4,12},{8,0},{12,4},{1,9},{5,13},{9,1},{13,5},{2,10},{6,14},... | collective-permute-start | bytes 129032 | tf_op jit(solution)/shard_map/ppermute | solution.py:688
  62.3 9.0 %collective-permute-start.13 = (bf16[24,896]{1,0:T(8,128)(2,1)S(1)}, bf16[24,896]{1,0:T(8,128)(2,1)S(1)}, u32[]{:S(2)}, u32[]{:S(2)}) collective-permute-start(bf16[24,896]{1,0:T(8,128)(2,1)S(1)} %get-tuple-element.108), channel_id=1, source_target_pairs={{0,12},{4,0},{8,4},{12,8},{1,13},{5,1},{9,5},{13,9},{2,14},{6,2},{... | collective-permute-start | bytes 129032 | tf_op jit(solution)/shard_map/ppermute | solution.py:688
  73.3 28.8 %all-to-all-start.1 = ((bf16[64,80,128]{2,1,0:T(8,128)(2,1)}), bf16[64,80,128]{2,1,0:T(8,128)(2,1)S(1)}, u32[]{:S(2)}, u32[]{:S(2)}) async-start(bf16[64,80,128]{2,1,0:T(8,128)(2,1)} %shard_map.196), calls=%async_computation.1 | async-start | bytes 2621440 | tf_op jit(solution)/shard_map/all_to_all | solution.py:693
  87.3 5.9 %collective-permute-start.20 = (bf16[24,512]{1,0:T(8,128)(2,1)S(1)}, bf16[24,512]{1,0:T(8,128)(2,1)S(1)}, u32[]{:S(2)}, u32[]{:S(2)}) collective-permute-start(bf16[24,512]{1,0:T(8,128)(2,1)S(1)} %get-tuple-element.132), channel_id=1, source_target_pairs={{0,64},{1,65},{2,66},{3,67},{64,0},{65,1},{66,2},{67,3},{4,68},{5,... | collective-permute-start | bytes 73736 | tf_op jit(solution)/shard_map/ppermute | solution.py:683
  88.4 8.8 %collective-permute-start.19 = (bf16[24,512]{1,0:T(8,128)(2,1)S(1)}, bf16[24,512]{1,0:T(8,128)(2,1)S(1)}, u32[]{:S(2)}, u32[]{:S(2)}) collective-permute-start(bf16[24,512]{1,0:T(8,128)(2,1)S(1)} %get-tuple-element.133), channel_id=1, source_target_pairs={{0,2},{1,3},{2,0},{3,1},{64,66},{65,67},{66,64},{67,65},{4,6},{5,7... | collective-permute-start | bytes 73736 | tf_op jit(solution)/shard_map/ppermute | solution.py:683
  90.8 8.9 %collective-permute-start.18 = (bf16[24,512]{1,0:T(8,128)(2,1)S(1)}, bf16[24,512]{1,0:T(8,128)(2,1)S(1)}, u32[]{:S(2)}, u32[]{:S(2)}) collective-permute-start(bf16[24,512]{1,0:T(8,128)(2,1)S(1)} %get-tuple-element.134), channel_id=1, source_target_pairs={{0,66},{1,67},{2,64},{3,65},{64,2},{65,3},{66,0},{67,1},{4,70},{5,... | collective-permute-start | bytes 73736 | tf_op jit(solution)/shard_map/ppermute | solution.py:683
  91.2 8.5 %collective-permute-start.17 = (bf16[24,512]{1,0:T(8,128)(2,1)S(1)}, bf16[24,512]{1,0:T(8,128)(2,1)S(1)}, u32[]{:S(2)}, u32[]{:S(2)}) collective-permute-start(bf16[24,512]{1,0:T(8,128)(2,1)S(1)} %get-tuple-element.135), channel_id=1, source_target_pairs={{0,1},{1,0},{2,3},{3,2},{64,65},{65,64},{66,67},{67,66},{4,5},{5,4... | collective-permute-start | bytes 73736 | tf_op jit(solution)/shard_map/ppermute | solution.py:683
  93.1 6.6 %collective-permute-start.16 = (bf16[24,512]{1,0:T(8,128)(2,1)S(1)}, bf16[24,512]{1,0:T(8,128)(2,1)S(1)}, u32[]{:S(2)}, u32[]{:S(2)}) collective-permute-start(bf16[24,512]{1,0:T(8,128)(2,1)S(1)} %get-tuple-element.136), channel_id=1, source_target_pairs={{0,65},{1,64},{2,67},{3,66},{64,1},{65,0},{66,3},{67,2},{4,69},{5,... | collective-permute-start | bytes 73736 | tf_op jit(solution)/shard_map/ppermute | solution.py:683
  93.2 8.4 %collective-permute-start.15 = (bf16[24,512]{1,0:T(8,128)(2,1)S(1)}, bf16[24,512]{1,0:T(8,128)(2,1)S(1)}, u32[]{:S(2)}, u32[]{:S(2)}) collective-permute-start(bf16[24,512]{1,0:T(8,128)(2,1)S(1)} %get-tuple-element.137), channel_id=1, source_target_pairs={{0,3},{1,2},{2,1},{3,0},{64,67},{65,66},{66,65},{67,64},{4,7},{5,6... | collective-permute-start | bytes 73736 | tf_op jit(solution)/shard_map/ppermute | solution.py:683
  97.2 4.9 %collective-permute-start.14 = (bf16[24,512]{1,0:T(8,128)(2,1)S(1)}, bf16[24,512]{1,0:T(8,128)(2,1)S(1)}, u32[]{:S(2)}, u32[]{:S(2)}) collective-permute-start(bf16[24,512]{1,0:T(8,128)(2,1)S(1)} %get-tuple-element.138), channel_id=1, source_target_pairs={{0,67},{1,66},{2,65},{3,64},{64,3},{65,2},{66,1},{67,0},{4,71},{5,... | collective-permute-start | bytes 73736 | tf_op jit(solution)/shard_map/ppermute | solution.py:683
  104.0 47.1 %all-to-all-start.2 = ((bf16[64,176,128]{2,1,0:T(8,128)(2,1)}), bf16[64,176,128]{2,1,0:T(8,128)(2,1)S(1)}, u32[]{:S(2)}, u32[]{:S(2)}) async-start(bf16[64,176,128]{2,1,0:T(8,128)(2,1)} %copy-done.2), calls=%async_computation.2 | async-start | bytes 5767168 | tf_op jit(solution)/shard_map/all_to_all | solution.py:693
  151.1 6.7 %collective-permute-start.21 = (bf16[64,176,128]{2,1,0:T(8,128)(2,1)S(1)}, bf16[64,176,128]{2,1,0:T(8,128)(2,1)S(1)}, u32[]{:S(2)}, u32[]{:S(2)}) collective-permute-start(bf16[64,176,128]{2,1,0:T(8,128)(2,1)S(1)} %all-to-all-done.2.mine_ref), channel_id=1, source_target_pairs={{0,1},{1,0},{2,3},{3,2},{4,5},{5,4},{6,7},{7,6},{8,9},{9,8},{10,11... | collective-permute-start | bytes 8650760 | tf_op jit(solution)/shard_map/ppermute | solution.py:683
  (30 other events, 201.5 us)

commit v7 on v6

--- a/solution.py
+++ b/solution.py
@@ -325,7 +325,7 @@
         gp_ref[:, cols] = (cot * gelu_parts(pre)[1]).astype(BF)
     tok = nt(gp_ref[...], wc_ref[...])
     keep_ref[...] = tok[:128]
-    send_ref[...] = tok[128:]
+    send_ref[...] = tok[128:].astype(BF)
     poolt_ref[...] = pool_ref[...].astype(F32).T.astype(BF)
     for d, s_ref in enumerate((s0_ref, s1_ref, s2_ref, s3_ref)):
         rows = pl.ds(pl.multiple_of(((at_ref[3] + d) & 3) * 96, 96), 96)
@@ -339,7 +339,7 @@
         [
             shape((256, 896), BF),
             shape((128, 384), F32),
-            shape((128, 384), F32),
+            shape((128, 384), BF),
         ]
         + [shape((96, 896), BF)] * 4,
         [
@@ -357,7 +357,7 @@
     co_ref, near_ref, part_ref, far_ref, normt_ref, slope_ref, hsum_ref, gsum_ref, bsum_ref, wout_ref, scale_ref,
     keep_ref, send_ref, dpre_ref, small_ref, dh_ref,
 ):
-    dtok = (part_ref[0:64, :] + near_ref[0:64, :] + far_ref[...].astype(F32)) * (1.0 / 16.0)
+    dtok = (part_ref[0:64, :] + near_ref[0:64, :].astype(F32) + far_ref[...].astype(F32)) * (1.0 / 16.0)
     small_ref[0:1, :] = jnp.sum(dtok * bsum_ref[...], axis=0, keepdims=True)
     dbr = (dtok * scale_ref[...].reshape(1, 384)).astype(BF)
     dh_ref[...] = nt(dbr, wout_ref[...])
@@ -739,7 +739,7 @@
     grad_pre, part, give, *outer = connector_part(at, pays, cot, wc)
 
     near = swap(give, "co", 2, 1)
-    far = swap((part[64:] + near[64:]).astype(BF), "yh", 2, 1)
+    far = swap((part[64:] + near[64:].astype(F32)).astype(BF), "yh", 2, 1)
     outer = turn(outer, "z")
     row_part, row_give = token_rows(grad_pre, connector)
     near, far, row_part, row_give = lax.optimization_barrier((near, far, row_part, row_give))

time: 162 us -> 162 us (level)
  no operation moved by 1% of the time
where the time goes in v7:
time: 162 us; the launch traced here: 161 us
  starting transfers between devices  63.8 us (39%)
  Pallas kernels  44.8 us (28%)
  waiting for transfers between devices  39.6 us (24%)
  local copies, waits for them, and re-layouts  8.3 us (5%)
  other arithmetic  2.49 us (2%)
  between operations  2.05 us (1%)
    all_to_all x3, waiting for transfers between devices, exchange(): return lax.all_to_all(v, axes, split_axis=0, concat_axis=0, tiled=True)  33.5 us
    all_to_all x3, starting transfers between devices, exchange(): return lax.all_to_all(v, axes, split_axis=0, concat_axis=0, tiled=True)  29.2 us
    ppermute x16, starting transfers between devices, swap(): return lax.ppermute(v, axes, [(i, i ^ d) for i in range(size)])  24.8 us
    pallas_call x1, Pallas kernels, forward(): call(forward_kernel, [shape((64, 512), BF), shape((8, 384, 128), BF), sha...  12.1 us
    ppermute x6, starting transfers between devices, turn(): lax.ppermute(parts[d], axis, [(i, (i + d) % 4) for i in range(4)])  9.85 us
    unnamed x74, local copies, waits for them, and re-layouts  7.92 us
    pallas_call x1, Pallas kernels, front_back(): call(front_back_kernel, jax.ShapeDtypeStruct((56, 384), F32), [pltpu.VMEM...  7.78 us
    ppermute x16, waiting for transfers between devices, swap(): return lax.ppermute(v, axes, [(i, i ^ d) for i in range(size)])  6.08 us
  transfers between devices with their start and end apart: 25, of which 6 were waited for; matrix products, arithmetic and copies ran while one was open for 2% of the time, Pallas kernels for 22%

profile of v7, /device:TPU:1, one launch (start us, length us, event | category | flops | bytes accessed | tf_op | source)
XLA Modules:
  0.0 161.0 jit_solution(14548109658314383924)
XLA Ops:
  1.8 1.7 %shard_map.188 = bf16[512,896]{1,0:T(8,128)(2,1)} custom-call(bf16[512,896]{1,0:T(8,128)(2,1)S(1)} %copy-done.10), custom_call_target="tpu_custom_call" | custom-call | flops 2200000000 | bytes 1 | tf_op jit(solution)/shard_map/pallas_call | solution.py:713
  3.5 10.0 %all-to-all-start = ((bf16[32,16,896]{2,1,0:T(8,128)(2,1)}), bf16[32,16,896]{2,1,0:T(8,128)(2,1)}, u32[]{:S(2)}, u32[]{:S(2)}) async-start(bf16[32,16,896]{2,1,0:T(8,128)(2,1)} %bitcast.8), calls=%async_computation | async-start | bytes 1835008 | tf_op jit(solution)/shard_map/all_to_all | solution.py:693
  14.6 12.1 %shard_map.189 = (bf16[64,512]{1,0:T(8,128)(2,1)S(1)}, bf16[8,384,128]{2,1,0:T(8,128)(2,1)S(1)}, bf16[3,1024,128]{2,1,0:T(8,128)(2,1)S(1)}, f32[1024,128]{1,0:T(...) custom-call(bf16[2,16,32,384]{3,2,1,0:T(8,128)(2,1)S(1)} %copy-done., ...), custom_call_target="tpu_custom_call" | custom-call | flops 15400000512 | bytes 1 | tf_op jit(solution)/shard_map/pallas_call | solution.py:206
  26.9 3.5 %collective-permute-start.2 = (bf16[64,512]{1,0:T(8,128)(2,1)S(1)}, bf16[64,512]{1,0:T(8,128)(2,1)S(1)}, u32[]{:S(2)}, u32[]{:S(2)}) collective-permute-start(bf16[64,512]{1,0:T(8,128)(2,1)S(1)} %get-tuple-element.72.p0_ref), channel_id=1, source_target_pairs={{0,3},{1,2},{2,1},{3,0},{4,7},{5,6},{6,5},{7,4},{8,11},{9,10},{10,... | collective-permute-start | bytes 196616 | tf_op jit(solution)/shard_map/ppermute | solution.py:683
  30.8 3.4 %shard_map.190.wc_ref = bf16[384,896]{1,0:T(8,128)(2,1)S(1)} custom-call(bf16[384,4096]{1,0:T(8,128)(2,1)S(1)} %copy-done.1, bf16[4096,896]{1,0:T(8,128)(2,1)S(1)} %bitcast.29), custom_call_target="tpu_custom_call" | custom-call | flops 1 | bytes 1 | tf_op jit(solution)/shard_map/pallas_call | solution.py:243
  36.2 2.6 %shard_map.191 = (bf16[256,896]{1,0:T(8,128)(2,1)S(1)}, f32[128,384]{1,0:T(8,128)S(1)}, bf16[128,384]{1,0:T(8,128)(2,1)S(1)}, bf16[96,896]{1,0:T(8,128)(2,1)S(1)...) custom-call(s32[6]{0:T(128)S(1)} %stack.27.at_ref.co_ref, ...), custom_call_target="tpu_custom_call" | custom-call | flops 3300000000 | bytes 1 | tf_op jit(solution)/shard_map/pallas_call | solution.py:337
  38.8 1.6 %collective-permute-start.3 = (bf16[128,384]{1,0:T(8,128)(2,1)S(1)}, bf16[128,384]{1,0:T(8,128)(2,1)S(1)}, u32[]{:S(2)}, u32[]{:S(2)}) collective-permute-start(bf16[128,384]{1,0:T(8,128)(2,1)S(1)} %get-tuple-element.74), channel_id=1, source_target_pairs={{0,1},{1,0},{2,3},{3,2},{4,5},{5,4},{6,7},{7,6},{8,9},{9,8},{10,11... | collective-permute-start | bytes 294920 | tf_op jit(solution)/shard_map/ppermute | solution.py:683
  41.4 1.9 %collective-permute-start.4 = (bf16[64,384]{1,0:T(8,128)(2,1)S(1)}, bf16[64,384]{1,0:T(8,128)(2,1)S(1)}, u32[]{:S(2)}, u32[]{:S(2)}) collective-permute-start(bf16[64,384]{1,0:T(8,128)(2,1)S(1)} %add_convert_fusion.2), channel_id=1, source_target_pairs={{0,2},{2,0},{1,3},{3,1},{4,6},{6,4},{5,7},{7,5},{8,10},{10,8},{9,1... | collective-permute-start | bytes 147464 | tf_op jit(solution)/shard_map/ppermute | solution.py:683
  43.4 1.4 collective-permute-start.5
  44.8 2.4 %collective-permute-start.6 = (bf16[96,896]{1,0:T(8,128)(2,1)S(1)}, bf16[96,896]{1,0:T(8,128)(2,1)S(1)}, u32[]{:S(2)}, u32[]{:S(2)}) collective-permute-start(bf16[96,896]{1,0:T(8,128)(2,1)S(1)} %get-tuple-element.91), channel_id=1, source_target_pairs={{0,32},{16,48},{32,0},{48,16},{1,33},{17,49},{33,1},{49,17},{2,34}... | collective-permute-start | bytes 516104 | tf_op jit(solution)/shard_map/ppermute | solution.py:688
  48.4 2.4 %shard_map.192 = (bf16[128,4096]{1,0:T(8,128)(2,1)S(1)}, bf16[128,4096]{1,0:T(8,128)(2,1)S(1)}) custom-call(bf16[256,896]{1,0:T(8,128)(2,1)S(1)} %get-tuple-element.76.gp_ref, bf16[4096,896]{1,0:T(8,128)(2,1)S(1)} %bitcast.31), custom_call_target="tpu_custom_call" | custom-call | flops 1 | bytes 1 | tf_op jit(solution)/shard_map/pallas_call | solution.py:258
  50.8 1.6 collective-permute-start.9
  52.4 3.7 %shard_map.193 = (bf16[1536,384]{1,0:T(8,128)(2,1)S(1)}, bf16[1536,384]{1,0:T(8,128)(2,1)S(1)}, bf16[4,1024,384]{2,1,0:T(8,128)(2,1)S(1)}, f32[8,384]{1,0:T(8,128)S(1)}) custom-call(s32[6]{0:T(128)S(1)} %stack.27.at_ref.co_ref, bf16[128,384]{1,0:T(8,128)(2,1)S(1)} %collective-permute-done.3.near_ref, f32[128,384]{1,0:T(8,128)S(1)} %get-tuple-element.75.part_ref, ...), custom_call_target="tpu_custom_call" | custom-call | flops 13200000000 | bytes 1 | tf_op jit(solution)/shard_map/pallas_call | solution.py:403
  59.8 2.4 %collective-permute-start.12 = (bf16[24,896]{1,0:T(8,128)(2,1)S(1)}, bf16[24,896]{1,0:T(8,128)(2,1)S(1)}, u32[]{:S(2)}, u32[]{:S(2)}) collective-permute-start(bf16[24,896]{1,0:T(8,128)(2,1)S(1)} %get-tuple-element.107), channel_id=1, source_target_pairs={{0,8},{4,12},{8,0},{12,4},{1,9},{5,13},{9,1},{13,5},{2,10},{6,14},... | collective-permute-start | bytes 129032 | tf_op jit(solution)/shard_map/ppermute | solution.py:688
  63.4 7.8 %shard_map.194.b_ref = f32[56,384]{1,0:T(8,128)S(1)} custom-call(bf16[4,1024,384]{2,1,0:T(8,128)(2,1)S(1)} %get-tuple-element.95.dpre_ref, bf16[384,1536]{1,0:T(8,128)(2,1)S(1)} %copy-done.9, bf16[3,1024,128]{2,1,0:T(8,128)(2,1)S(1)} %copy-done.17, f32[1024,128]{1,0:T(8,128)S(1)} %copy-done.21, f32[384]{0:T(512)S(1)} %copy-done.15, ...), custom_call_target="tpu_custom_call" | custom-call | flops 2200000000 | bytes 1 | tf_op jit(solution)/shard_map/pallas_call | solution.py:497
  71.6 1.6 shard_map.196
  73.2 8.0 %all-to-all-start.1 = ((bf16[64,80,128]{2,1,0:T(8,128)(2,1)}), bf16[64,80,128]{2,1,0:T(8,128)(2,1)S(1)}, u32[]{:S(2)}, u32[]{:S(2)}) async-start(bf16[64,80,128]{2,1,0:T(8,128)(2,1)} %shard_map.196), calls=%async_computation.1 | async-start | bytes 2621440 | tf_op jit(solution)/shard_map/all_to_all | solution.py:693
  81.2 3.1 %copy-done = bf16[4096,896]{1,0:T(8,128)(2,1)S(1)} copy-done((bf16[4096,896]{1,0:T(8,128)(2,1)S(1)}, bf16[4096,896]{1,0:T(8,128)(2,1)}, u32[]{:S(2)}) %copy-start) | copy-done | bytes 7340056
  84.3 2.8 %shard_map.197 = bf16[8,24,512]{2,1,0:T(8,128)(2,1)S(1)} custom-call(s32[6]{0:T(128)S(1)} %stack.27.at_ref.co_ref, bf16[24,896]{1,0:T(8,128)(2,1)S(1)} %get-tuple-element.114.r0_ref, bf16[24,896]{1,0:T(8,128)(2,1)S(1)} %collective-permute-done.11.r1_ref, bf16[24,896]{1,0:T(8,128)(2,1)S(1)} %collective-permute-done.12.r2_ref, ...), custom_call_target="tpu_custom_call" | custom-call | flops 1 | bytes 1 | tf_op jit(solution)/shard_map/pallas_call | solution.py:294
  88.3 2.4 %collective-permute-start.19 = (bf16[24,512]{1,0:T(8,128)(2,1)S(1)}, bf16[24,512]{1,0:T(8,128)(2,1)S(1)}, u32[]{:S(2)}, u32[]{:S(2)}) collective-permute-start(bf16[24,512]{1,0:T(8,128)(2,1)S(1)} %get-tuple-element.133), channel_id=1, source_target_pairs={{0,2},{1,3},{2,0},{3,1},{64,66},{65,67},{66,64},{67,65},{4,6},{5,7... | collective-permute-start | bytes 73736 | tf_op jit(solution)/shard_map/ppermute | solution.py:683
  91.1 1.9 %collective-permute-start.17 = (bf16[24,512]{1,0:T(8,128)(2,1)S(1)}, bf16[24,512]{1,0:T(8,128)(2,1)S(1)}, u32[]{:S(2)}, u32[]{:S(2)}) collective-permute-start(bf16[24,512]{1,0:T(8,128)(2,1)S(1)} %get-tuple-element.135), channel_id=1, source_target_pairs={{0,1},{1,0},{2,3},{3,2},{64,65},{65,64},{66,67},{67,66},{4,5},{5,4... | collective-permute-start | bytes 73736 | tf_op jit(solution)/shard_map/ppermute | solution.py:683
  93.1 4.0 %collective-permute-start.15 = (bf16[24,512]{1,0:T(8,128)(2,1)S(1)}, bf16[24,512]{1,0:T(8,128)(2,1)S(1)}, u32[]{:S(2)}, u32[]{:S(2)}) collective-permute-start(bf16[24,512]{1,0:T(8,128)(2,1)S(1)} %get-tuple-element.137), channel_id=1, source_target_pairs={{0,3},{1,2},{2,1},{3,0},{64,67},{65,66},{66,65},{67,64},{4,7},{5,6... | collective-permute-start | bytes 73736 | tf_op jit(solution)/shard_map/ppermute | solution.py:683
  97.1 2.5 %collective-permute-start.14 = (bf16[24,512]{1,0:T(8,128)(2,1)S(1)}, bf16[24,512]{1,0:T(8,128)(2,1)S(1)}, u32[]{:S(2)}, u32[]{:S(2)}) collective-permute-start(bf16[24,512]{1,0:T(8,128)(2,1)S(1)} %get-tuple-element.138), channel_id=1, source_target_pairs={{0,67},{1,66},{2,65},{3,64},{64,3},{65,2},{66,1},{67,0},{4,71},{5,... | collective-permute-start | bytes 73736 | tf_op jit(solution)/shard_map/ppermute | solution.py:683
  99.6 1.8 %collective-permute-done.15.refs_2_ = bf16[24,512]{1,0:T(8,128)(2,1)S(1)} collective-permute-done((bf16[24,512]{1,0:T(8,128)(2,1)S(1)}, bf16[24,512]{1,0:T(8,128)(2,1)S(1)}, u32[]{:S(2)}, u32[]{:S(2)}) %collective-permute-start.15) | collective-permute-done | bytes 24608 | tf_op jit(solution)/shard_map/ppermute | solution.py:683
  102.3 1.6 copy-done.2
  103.9 11.2 %all-to-all-start.2 = ((bf16[64,176,128]{2,1,0:T(8,128)(2,1)}), bf16[64,176,128]{2,1,0:T(8,128)(2,1)S(1)}, u32[]{:S(2)}, u32[]{:S(2)}) async-start(bf16[64,176,128]{2,1,0:T(8,128)(2,1)} %copy-done.2), calls=%async_computation.2 | async-start | bytes 5767168 | tf_op jit(solution)/shard_map/all_to_all | solution.py:693
  115.1 2.3 %add_convert_fusion = bf16[64,4096]{1,0:T(8,128)(2,1)} fusion(bf16[64,4096]{1,0:T(8,128)(2,1)} %collective-permute-done.10, bf16[128,4096]{1,0:T(8,128)(2,1)} %copy-done.30, bf16[128,4096]{1,0:T(8,128)(2,1)} %copy-done.3), kind=kLoop, calls=%fused_computation | loop fusion | flops 1572864 | bytes 2097152 | tf_op jit(solution)/shard_map/convert_element_type | solution.py:770
  117.4 33.5 %all-to-all-done.2.mine_ref = bf16[64,176,128]{2,1,0:T(8,128)(2,1)S(1)} async-done(((bf16[64,176,128]{2,1,0:T(8,128)(2,1)}), bf16[64,176,128]{2,1,0:T(8,128)(2,1)S(1)}, u32[]{:S(2)}, u32[]{:S(2)}) %all-to-all-start.2) | async-done | bytes 2883616 | tf_op jit(solution)/shard_map/all_to_all | solution.py:693
  151.0 1.8 %collective-permute-start.21 = (bf16[64,176,128]{2,1,0:T(8,128)(2,1)S(1)}, bf16[64,176,128]{2,1,0:T(8,128)(2,1)S(1)}, u32[]{:S(2)}, u32[]{:S(2)}) collective-permute-start(bf16[64,176,128]{2,1,0:T(8,128)(2,1)S(1)} %all-to-all-done.2.mine_ref), channel_id=1, source_target_pairs={{0,1},{1,0},{2,3},{3,2},{4,5},{5,4},{6,7},{7,6},{8,9},{9,8},{10,11... | collective-permute-start | bytes 8650760 | tf_op jit(solution)/shard_map/ppermute | solution.py:683
  152.7 2.5 %shard_map.199 = (bf16[384,1536]{1,0:T(8,128)(2,1)}, bf16[1536,384]{1,0:T(8,128)(2,1)}, bf16[384,4096]{1,0:T(8,128)(2,1)}, f32[64,384]{1,0:T(8,128)S(1)}) custom-call(s32[6]{0:T(128)S(1)} %stack.27.at_ref.co_ref, bf16[64,176,128]{2,1,0:T(8,128)(2,1)S(1)} %all-to-all-done.2.mine_ref), custom_call_target="tpu_custom_call" | custom-call | flops 3300000000 | bytes 1 | tf_op jit(solution)/shard_map/pallas_call | solution.py:660
  155.3 2.4 %collective-permute-done.21.other_ref = bf16[64,176,128]{2,1,0:T(8,128)(2,1)S(1)} collective-permute-done((bf16[64,176,128]{2,1,0:T(8,128)(2,1)S(1)}, bf16[64,176,128]{2,1,0:T(8,128)(2,1)S(1)}, u32[]{:S(2)}, u32[]{:S(2)}) %collective-permute-start.21) | collective-permute-done | bytes 2883616 | tf_op jit(solution)/shard_map/ppermute | solution.py:683
  157.7 3.2 %shard_map.200 = (bf16[384,1536]{1,0:T(8,128)(2,1)}, bf16[1536,384]{1,0:T(8,128)(2,1)}, bf16[384,4096]{1,0:T(8,128)(2,1)}, f32[7,7,384]{2,1,0:T(8,128)}, f32[384]{0:T(512)}, /*index=5*/f32[1536]{0:T(1024)}, f32[384]{0:T(512)}) custom-call(s32[6]{0:T(128)S(1)} %stack.27.at_ref.co_ref, ...), custom_call_target="tpu_custom_call", output_to_operand_aliasing={{0}: (3, {}), {1}: (4, {}), {2}: (5, {})} | custom-call | flops 3300000000 | bytes 1 | tf_op jit(solution)/shard_map/pallas_call | solution.py:669
  (116 shorter events, 13.9 us)
Async XLA Ops:
  1.8 12.7 %copy-start.8 = (bf16[384,1536]{1,0:T(8,128)(2,1)S(1)}, bf16[384,1536]{1,0:T(8,128)(2,1)}, u32[]{:S(2)}) copy-start(bf16[384,1536]{1,0:T(8,128)(2,1)} %win_ref.1) | copy-start | bytes 3538948
  1.8 12.7 %copy-start.11 = (bf16[2,16,32,384]{3,2,1,0:T(8,128)(2,1)S(1)}, bf16[2,16,32,384]{3,2,1,0:T(8,128)(2,1)}, u32[]{:S(2)}) copy-start(bf16[2,16,32,384]{3,2,1,0:T(8,128)(2,1)} %x_hbm) | copy-start | bytes 2359300
  3.5 31.6 %all-to-all-start = ((bf16[32,16,896]{2,1,0:T(8,128)(2,1)}), bf16[32,16,896]{2,1,0:T(8,128)(2,1)}, u32[]{:S(2)}, u32[]{:S(2)}) async-start(bf16[32,16,896]{2,1,0:T(8,128)(2,1)} %bitcast.8), calls=%async_computation | async-start | bytes 1835008 | tf_op jit(solution)/shard_map/all_to_all | solution.py:693
  14.5 16.3 %slice-start = ((s8[7340032]{0:T(1024)(128)(4,1)}), s8[4194304]{0:T(1024)(128)(4,1)S(1)}, s32[]{:S(2)}) async-start(s8[7340032]{0:T(1024)(128)(4,1)} %bitcast.28), calls=%async_computation.3 | async-start | bytes 8388608
  14.6 16.1 %slice-start.1 = ((s8[7340032]{0:T(1024)(128)(4,1)}), s8[3145728]{0:T(1024)(128)(4,1)S(1)}, s32[]{:S(2)}) async-start(s8[7340032]{0:T(1024)(128)(4,1)} %bitcast.28), calls=%async_computation.4 | async-start | bytes 6291456
  14.6 16.1 %copy-start.1 = (bf16[384,4096]{1,0:T(8,128)(2,1)S(1)}, bf16[384,4096]{1,0:T(8,128)(2,1)}, u32[]{:S(2)}) copy-start(bf16[384,4096]{1,0:T(8,128)(2,1)} %proj_ref) | copy-start | bytes 9437188
  26.9 8.2 %collective-permute-start.2 = (bf16[64,512]{1,0:T(8,128)(2,1)S(1)}, bf16[64,512]{1,0:T(8,128)(2,1)S(1)}, u32[]{:S(2)}, u32[]{:S(2)}) collective-permute-start(bf16[64,512]{1,0:T(8,128)(2,1)S(1)} %get-tuple-element.72.p0_ref), channel_id=1, source_target_pairs={{0,3},{1,2},{2,1},{3,0},{4,7},{5,6},{6,5},{7,4},{8,11},{9,10},{10,... | collective-permute-start | bytes 196616 | tf_op jit(solution)/shard_map/ppermute | solution.py:683
  30.4 4.7 %collective-permute-start.1 = (bf16[64,512]{1,0:T(8,128)(2,1)S(1)}, bf16[64,512]{1,0:T(8,128)(2,1)S(1)}, u32[]{:S(2)}, u32[]{:S(2)}) collective-permute-start(bf16[64,512]{1,0:T(8,128)(2,1)S(1)} %get-tuple-element.72.p0_ref), channel_id=1, source_target_pairs={{0,1},{1,0},{2,3},{3,2},{4,5},{5,4},{6,7},{7,6},{8,9},{9,8},{10,11... | collective-permute-start | bytes 196616 | tf_op jit(solution)/shard_map/ppermute | solution.py:683
  30.4 4.7 %collective-permute-start = (bf16[64,512]{1,0:T(8,128)(2,1)S(1)}, bf16[64,512]{1,0:T(8,128)(2,1)S(1)}, u32[]{:S(2)}, u32[]{:S(2)}) collective-permute-start(bf16[64,512]{1,0:T(8,128)(2,1)S(1)} %get-tuple-element.72.p0_ref), channel_id=1, source_target_pairs={{0,2},{1,3},{2,0},{3,1},{4,6},{5,7},{6,4},{7,5},{8,10},{9,11},{10,... | collective-permute-start | bytes 196616 | tf_op jit(solution)/shard_map/ppermute | solution.py:683
  30.8 17.6 %slice-start.2 = ((s8[7340032]{0:T(1024)(128)(4,1)}), s8[3145728]{0:T(1024)(128)(4,1)S(1)}, s32[]{:S(2)}) async-start(s8[7340032]{0:T(1024)(128)(4,1)} %bitcast.30), calls=%async_computation.5 | async-start | bytes 6291456
  38.8 2.6 %collective-permute-start.3 = (bf16[128,384]{1,0:T(8,128)(2,1)S(1)}, bf16[128,384]{1,0:T(8,128)(2,1)S(1)}, u32[]{:S(2)}, u32[]{:S(2)}) collective-permute-start(bf16[128,384]{1,0:T(8,128)(2,1)S(1)} %get-tuple-element.74), channel_id=1, source_target_pairs={{0,1},{1,0},{2,3},{3,2},{4,5},{5,4},{6,7},{7,6},{8,9},{9,8},{10,11... | collective-permute-start | bytes 294920 | tf_op jit(solution)/shard_map/ppermute | solution.py:683
  41.4 9.4 %collective-permute-start.4 = (bf16[64,384]{1,0:T(8,128)(2,1)S(1)}, bf16[64,384]{1,0:T(8,128)(2,1)S(1)}, u32[]{:S(2)}, u32[]{:S(2)}) collective-permute-start(bf16[64,384]{1,0:T(8,128)(2,1)S(1)} %add_convert_fusion.2), channel_id=1, source_target_pairs={{0,2},{2,0},{1,3},{3,1},{4,6},{6,4},{5,7},{7,5},{8,10},{10,8},{9,1... | collective-permute-start | bytes 147464 | tf_op jit(solution)/shard_map/ppermute | solution.py:683
  43.4 12.8 %collective-permute-start.5 = (bf16[96,896]{1,0:T(8,128)(2,1)S(1)}, bf16[96,896]{1,0:T(8,128)(2,1)S(1)}, u32[]{:S(2)}, u32[]{:S(2)}) collective-permute-start(bf16[96,896]{1,0:T(8,128)(2,1)S(1)} %get-tuple-element.90), channel_id=1, source_target_pairs={{0,16},{16,32},{32,48},{48,0},{1,17},{17,33},{33,49},{49,1},{2,18}... | collective-permute-start | bytes 516104 | tf_op jit(solution)/shard_map/ppermute | solution.py:688
  44.8 11.3 %collective-permute-start.6 = (bf16[96,896]{1,0:T(8,128)(2,1)S(1)}, bf16[96,896]{1,0:T(8,128)(2,1)S(1)}, u32[]{:S(2)}, u32[]{:S(2)}) collective-permute-start(bf16[96,896]{1,0:T(8,128)(2,1)S(1)} %get-tuple-element.91), channel_id=1, source_target_pairs={{0,32},{16,48},{32,0},{48,16},{1,33},{17,49},{33,1},{49,17},{2,34}... | collective-permute-start | bytes 516104 | tf_op jit(solution)/shard_map/ppermute | solution.py:688
  47.2 8.9 %collective-permute-start.7 = (bf16[96,896]{1,0:T(8,128)(2,1)S(1)}, bf16[96,896]{1,0:T(8,128)(2,1)S(1)}, u32[]{:S(2)}, u32[]{:S(2)}) collective-permute-start(bf16[96,896]{1,0:T(8,128)(2,1)S(1)} %get-tuple-element.92), channel_id=1, source_target_pairs={{0,48},{16,0},{32,16},{48,32},{1,49},{17,1},{33,17},{49,33},{2,50}... | collective-permute-start | bytes 516104 | tf_op jit(solution)/shard_map/ppermute | solution.py:688
  50.8 5.6 %collective-permute-start.9 = (bf16[128,4096]{1,0:T(8,128)(2,1)S(1)}, bf16[128,4096]{1,0:T(8,128)(2,1)S(1)}, u32[]{:S(2)}, u32[]{:S(2)}) collective-permute-start(bf16[128,4096]{1,0:T(8,128)(2,1)S(1)} %get-tuple-element.100), channel_id=1, source_target_pairs={{0,1},{1,0},{2,3},{3,2},{4,5},{5,4},{6,7},{7,6},{8,9},{9,8},{10,11... | collective-permute-start | bytes 3145736 | tf_op jit(solution)/shard_map/ppermute | solution.py:683
  56.2 15.4 %collective-permute-start.8 = (bf16[1536,384]{1,0:T(8,128)(2,1)S(1)}, bf16[1536,384]{1,0:T(8,128)(2,1)S(1)}, u32[]{:S(2)}, u32[]{:S(2)}) collective-permute-start(bf16[1536,384]{1,0:T(8,128)(2,1)S(1)} %get-tuple-element.93), channel_id=1, source_target_pairs={{0,1},{1,0},{2,3},{3,2},{4,5},{5,4},{6,7},{7,6},{8,9},{9,8},{10,11... | collective-permute-start | bytes 3538952 | tf_op jit(solution)/shard_map/ppermute | solution.py:683
  56.5 14.7 %copy-start.30 = (bf16[128,4096]{1,0:T(8,128)(2,1)}, bf16[128,4096]{1,0:T(8,128)(2,1)S(1)}, u32[]{:S(2)}) copy-start(bf16[128,4096]{1,0:T(8,128)(2,1)S(1)} %collective-permute-done.9) | copy-start | bytes 3145732
  56.7 14.9 %collective-permute-start.10 = (bf16[64,4096]{1,0:T(8,128)(2,1)S(1)}, bf16[64,4096]{1,0:T(8,128)(2,1)}, u32[]{:S(2)}, u32[]{:S(2)}) collective-permute-start(bf16[64,4096]{1,0:T(8,128)(2,1)S(1)} %add_convert_fusion.1), channel_id=1, source_target_pairs={{0,2},{2,0},{1,3},{3,1},{4,6},{6,4},{5,7},{7,5},{8,10},{10,8},{9,1... | collective-permute-start | bytes 1572872 | tf_op jit(solution)/shard_map/ppermute | solution.py:683
  58.5 12.7 %collective-permute-start.11 = (bf16[24,896]{1,0:T(8,128)(2,1)S(1)}, bf16[24,896]{1,0:T(8,128)(2,1)S(1)}, u32[]{:S(2)}, u32[]{:S(2)}) collective-permute-start(bf16[24,896]{1,0:T(8,128)(2,1)S(1)} %get-tuple-element.106), channel_id=1, source_target_pairs={{0,4},{4,8},{8,12},{12,0},{1,5},{5,9},{9,13},{13,1},{2,6},{6,10},{... | collective-permute-start | bytes 129032 | tf_op jit(solution)/shard_map/ppermute | solution.py:688
  59.8 11.4 %collective-permute-start.12 = (bf16[24,896]{1,0:T(8,128)(2,1)S(1)}, bf16[24,896]{1,0:T(8,128)(2,1)S(1)}, u32[]{:S(2)}, u32[]{:S(2)}) collective-permute-start(bf16[24,896]{1,0:T(8,128)(2,1)S(1)} %get-tuple-element.107), channel_id=1, source_target_pairs={{0,8},{4,12},{8,0},{12,4},{1,9},{5,13},{9,1},{13,5},{2,10},{6,14},... | collective-permute-start | bytes 129032 | tf_op jit(solution)/shard_map/ppermute | solution.py:688
  62.2 9.0 %collective-permute-start.13 = (bf16[24,896]{1,0:T(8,128)(2,1)S(1)}, bf16[24,896]{1,0:T(8,128)(2,1)S(1)}, u32[]{:S(2)}, u32[]{:S(2)}) collective-permute-start(bf16[24,896]{1,0:T(8,128)(2,1)S(1)} %get-tuple-element.108), channel_id=1, source_target_pairs={{0,12},{4,0},{8,4},{12,8},{1,13},{5,1},{9,5},{13,9},{2,14},{6,2},{... | collective-permute-start | bytes 129032 | tf_op jit(solution)/shard_map/ppermute | solution.py:688
  73.2 28.8 %all-to-all-start.1 = ((bf16[64,80,128]{2,1,0:T(8,128)(2,1)}), bf16[64,80,128]{2,1,0:T(8,128)(2,1)S(1)}, u32[]{:S(2)}, u32[]{:S(2)}) async-start(bf16[64,80,128]{2,1,0:T(8,128)(2,1)} %shard_map.196), calls=%async_computation.1 | async-start | bytes 2621440 | tf_op jit(solution)/shard_map/all_to_all | solution.py:693
  87.1 5.9 %collective-permute-start.20 = (bf16[24,512]{1,0:T(8,128)(2,1)S(1)}, bf16[24,512]{1,0:T(8,128)(2,1)S(1)}, u32[]{:S(2)}, u32[]{:S(2)}) collective-permute-start(bf16[24,512]{1,0:T(8,128)(2,1)S(1)} %get-tuple-element.132), channel_id=1, source_target_pairs={{0,64},{1,65},{2,66},{3,67},{64,0},{65,1},{66,2},{67,3},{4,68},{5,... | collective-permute-start | bytes 73736 | tf_op jit(solution)/shard_map/ppermute | solution.py:683
  88.3 8.7 %collective-permute-start.19 = (bf16[24,512]{1,0:T(8,128)(2,1)S(1)}, bf16[24,512]{1,0:T(8,128)(2,1)S(1)}, u32[]{:S(2)}, u32[]{:S(2)}) collective-permute-start(bf16[24,512]{1,0:T(8,128)(2,1)S(1)} %get-tuple-element.133), channel_id=1, source_target_pairs={{0,2},{1,3},{2,0},{3,1},{64,66},{65,67},{66,64},{67,65},{4,6},{5,7... | collective-permute-start | bytes 73736 | tf_op jit(solution)/shard_map/ppermute | solution.py:683
  90.7 8.9 %collective-permute-start.18 = (bf16[24,512]{1,0:T(8,128)(2,1)S(1)}, bf16[24,512]{1,0:T(8,128)(2,1)S(1)}, u32[]{:S(2)}, u32[]{:S(2)}) collective-permute-start(bf16[24,512]{1,0:T(8,128)(2,1)S(1)} %get-tuple-element.134), channel_id=1, source_target_pairs={{0,66},{1,67},{2,64},{3,65},{64,2},{65,3},{66,0},{67,1},{4,70},{5,... | collective-permute-start | bytes 73736 | tf_op jit(solution)/shard_map/ppermute | solution.py:683
  91.1 8.5 %collective-permute-start.17 = (bf16[24,512]{1,0:T(8,128)(2,1)S(1)}, bf16[24,512]{1,0:T(8,128)(2,1)S(1)}, u32[]{:S(2)}, u32[]{:S(2)}) collective-permute-start(bf16[24,512]{1,0:T(8,128)(2,1)S(1)} %get-tuple-element.135), channel_id=1, source_target_pairs={{0,1},{1,0},{2,3},{3,2},{64,65},{65,64},{66,67},{67,66},{4,5},{5,4... | collective-permute-start | bytes 73736 | tf_op jit(solution)/shard_map/ppermute | solution.py:683
  93.0 6.6 %collective-permute-start.16 = (bf16[24,512]{1,0:T(8,128)(2,1)S(1)}, bf16[24,512]{1,0:T(8,128)(2,1)S(1)}, u32[]{:S(2)}, u32[]{:S(2)}) collective-permute-start(bf16[24,512]{1,0:T(8,128)(2,1)S(1)} %get-tuple-element.136), channel_id=1, source_target_pairs={{0,65},{1,64},{2,67},{3,66},{64,1},{65,0},{66,3},{67,2},{4,69},{5,... | collective-permute-start | bytes 73736 | tf_op jit(solution)/shard_map/ppermute | solution.py:683
  93.1 8.4 %collective-permute-start.15 = (bf16[24,512]{1,0:T(8,128)(2,1)S(1)}, bf16[24,512]{1,0:T(8,128)(2,1)S(1)}, u32[]{:S(2)}, u32[]{:S(2)}) collective-permute-start(bf16[24,512]{1,0:T(8,128)(2,1)S(1)} %get-tuple-element.137), channel_id=1, source_target_pairs={{0,3},{1,2},{2,1},{3,0},{64,67},{65,66},{66,65},{67,64},{4,7},{5,6... | collective-permute-start | bytes 73736 | tf_op jit(solution)/shard_map/ppermute | solution.py:683
  97.1 4.9 %collective-permute-start.14 = (bf16[24,512]{1,0:T(8,128)(2,1)S(1)}, bf16[24,512]{1,0:T(8,128)(2,1)S(1)}, u32[]{:S(2)}, u32[]{:S(2)}) collective-permute-start(bf16[24,512]{1,0:T(8,128)(2,1)S(1)} %get-tuple-element.138), channel_id=1, source_target_pairs={{0,67},{1,66},{2,65},{3,64},{64,3},{65,2},{66,1},{67,0},{4,71},{5,... | collective-permute-start | bytes 73736 | tf_op jit(solution)/shard_map/ppermute | solution.py:683
  103.9 47.1 %all-to-all-start.2 = ((bf16[64,176,128]{2,1,0:T(8,128)(2,1)}), bf16[64,176,128]{2,1,0:T(8,128)(2,1)S(1)}, u32[]{:S(2)}, u32[]{:S(2)}) async-start(bf16[64,176,128]{2,1,0:T(8,128)(2,1)} %copy-done.2), calls=%async_computation.2 | async-start | bytes 5767168 | tf_op jit(solution)/shard_map/all_to_all | solution.py:693
  151.0 6.7 %collective-permute-start.21 = (bf16[64,176,128]{2,1,0:T(8,128)(2,1)S(1)}, bf16[64,176,128]{2,1,0:T(8,128)(2,1)S(1)}, u32[]{:S(2)}, u32[]{:S(2)}) collective-permute-start(bf16[64,176,128]{2,1,0:T(8,128)(2,1)S(1)} %all-to-all-done.2.mine_ref), channel_id=1, source_target_pairs={{0,1},{1,0},{2,3},{3,2},{4,5},{5,4},{6,7},{7,6},{8,9},{9,8},{10,11... | collective-permute-start | bytes 8650760 | tf_op jit(solution)/shard_map/ppermute | solution.py:683
  (30 other events, 201.3 us)
